TPU v7x, 512 devices: a whole 4x8x8 slice. The times are simulated.
512 devices in a mesh: row: 16 (over y, core), col: 32 (over x, z).
Axes of the slice: x: 4, y: 8, z: 8, core: 2. Of those that a mesh axis runs over, the one named last changes fastest.
Arguments:
- start_vector: float32 [100663296], P(('row', 'col')), may hold values from -8 to 8
- tile_blocks: bfloat16 [16, 32, 64, 128, 128], P('row', 'col'), may hold values from -0.5 to 0.5
- row_owner: int32 [16, 32, 64, 1], P('row', 'col'), may hold values from 0 to 31; in each aligned block of 64 rows (0 to 63, 64 to 127, ..., all dimensions but the last counted through in order) at most 4 rows name the same one
- row_block: int32 [16, 32, 64], P('row', 'col'), may hold values from 0 to 1535
- col_owner: int32 [16, 32, 64, 1], P('row', 'col'), may hold values from 0 to 15; in each aligned block of 64 rows (0 to 63, 64 to 127, ..., all dimensions but the last counted through in order) at most 8 rows name the same one
- col_block: int32 [16, 32, 64], P('row', 'col'), may hold values from 0 to 1535
- tile_counts: int32 [16, 32], P('row', 'col'), may hold values from 8 to 64, as said below
Outputs:
- lanczos_basis: float32 [2, 100663296], P(None, ('row', 'col'))
- start_alpha: float32 [1], replicated
- tridiagonal: float32 [3], replicated
Inputs may be any that keep to these rules, and one draw needn't show every extreme that they name: `row_owner`: within the 64 slots of one grid position no value is named by more than 4 slots; some grid positions reach 4. `col_owner`: within the 64 slots of one grid position no value is named by more than 8 slots; some grid positions reach 8. `tile_counts`: at least one grid position has exactly 64 live tiles.
All inputs are finite; a program needn't handle non-finite values.
Results may differ from a plain program's by a relative error of at most 0.0023.
Values may be sent and summed in bfloat16 or wider, within the bound.
No kernel may reach another device: no remote copies, remote signals or barrier semaphores. Data moves between devices by JAX's collectives and lax.ppermute only.
A program may use at most 64 MiB of HBM per device.

v0:
```python
import jax
import jax.numpy as jnp
from jax import lax
from jax.sharding import PartitionSpec as P

TILE = 128
ITERS = 2


def owner_slots(owner, capacity):
    order = jnp.arange(owner.shape[0])
    same = (owner[:, None] == owner[None, :]) & (order[None, :] < order[:, None])
    rank = jnp.sum(same.astype(jnp.int32), axis=1)
    return owner * capacity + rank


def request_table(slot_place, block, alive, width):
    marked = jnp.where(alive, block, -1)
    return jnp.full((width,), -1, jnp.int32).at[slot_place].set(marked)


def add_received(received, served, pieces):
    target = jnp.where(served >= 0, served, pieces)
    summed = jnp.zeros((pieces + 1, received.shape[1]), jnp.float32).at[target].add(received)
    return summed[:pieces]


def per_device(start_vector, tile_blocks, row_owner, row_block, col_owner, col_block, tile_counts):
    blocks = tile_blocks[0, 0]
    owner_r = row_owner[0, 0, :, 0]
    block_r = row_block[0, 0]
    owner_c = col_owner[0, 0, :, 0]
    block_c = col_block[0, 0]
    filled = tile_counts[0, 0]
    slot_total = blocks.shape[0]
    pieces = start_vector.shape[0] // TILE
    row_count = lax.axis_size("row")
    col_count = lax.axis_size("col")
    row_capacity = max(2, 2 * slot_total // col_count)
    col_capacity = max(2, 2 * slot_total // row_count)
    total = float(pieces * TILE * row_count * col_count)
    alive = jnp.arange(slot_total) < filled
    live = alive.astype(jnp.float32)[:, None]
    slot_r = owner_slots(owner_r, row_capacity)
    slot_c = owner_slots(owner_c, col_capacity)
    width_r = col_count * row_capacity
    width_c = row_count * col_capacity
    served_r = lax.all_to_all(
        request_table(slot_r, block_r, alive, width_r),
        "col",
        split_axis=0,
        concat_axis=0,
        tiled=True,
    )
    served_c = lax.all_to_all(
        request_table(slot_c, block_c, alive, width_c),
        "row",
        split_axis=0,
        concat_axis=0,
        tiled=True,
    )
    safe_r = jnp.clip(served_r, 0, pieces - 1)
    safe_c = jnp.clip(served_c, 0, pieces - 1)
    energy = lax.psum(jnp.sum(start_vector * start_vector), ("row", "col"))
    current = start_vector / jnp.sqrt(energy / total + 1e-06)
    basis = [current]
    alphas = []
    betas = []
    for step in range(ITERS):
        narrow = basis[-1].astype(jnp.bfloat16).reshape(pieces, TILE)
        fetched_r = lax.all_to_all(narrow[safe_r], "col", split_axis=0, concat_axis=0, tiled=True)
        row_x = fetched_r[slot_r]
        fetched_c = lax.all_to_all(narrow[safe_c], "row", split_axis=0, concat_axis=0, tiled=True)
        col_x = fetched_c[slot_c]
        direct = jnp.einsum("tab,tb->ta", blocks, col_x, preferred_element_type=jnp.float32) * live
        mirror = jnp.einsum("tab,ta->tb", blocks, row_x, preferred_element_type=jnp.float32) * live
        outgoing_r = jnp.zeros((width_r, TILE), jnp.float32).at[slot_r].set(direct)
        outgoing_c = jnp.zeros((width_c, TILE), jnp.float32).at[slot_c].set(mirror)
        back_r = lax.all_to_all(outgoing_r, "col", split_axis=0, concat_axis=0, tiled=True)
        back_c = lax.all_to_all(outgoing_c, "row", split_axis=0, concat_axis=0, tiled=True)
        result = add_received(back_r, served_r, pieces) + add_received(back_c, served_c, pieces)
        image = result.reshape(-1)
        correlations = (
            lax.psum(jnp.stack([jnp.sum(older * image) for older in basis]), ("row", "col")) / total
        )
        update = image
        for index in range(len(basis)):
            update = update - correlations[index] * basis[index]
        square = lax.psum(jnp.sum(update * update), ("row", "col")) / total
        norm_value = jnp.sqrt(square + 1e-06)
        basis.append(update / norm_value)
        alphas.append(correlations[-1])
        betas.append(norm_value)
    entries = [betas[0]]
    index = 1
    entries.append(alphas[index])
    entries.append(betas[index])
    return (jnp.stack(basis[1:]), jnp.stack([alphas[0]]), jnp.stack(entries))


def solution(mesh):
    return jax.shard_map(
        per_device,
        mesh=mesh,
        in_specs=(
            P(("row", "col")),
            P("row", "col", None, None, None),
            P("row", "col", None, None),
            P("row", "col", None),
            P("row", "col", None, None),
            P("row", "col", None),
            P("row", "col"),
        ),
        out_specs=(P(None, ("row", "col")), P(), P()),
        check_vma=False,
    )
```

profile of v0, /device:TPU:1, one launch (start us, length us, event | category | flops | bytes accessed | tf_op | source)
XLA Modules:
  0.0 656.2 jit_solution(12482295571592582210)
XLA Ops:
  1.4 0.9 convert_reduce_fusion
  2.4 0.7 fusion.44
  3.0 0.7 bitcast_select_fusion
  3.7 0.8 scatter_custom_fusion.1
  4.5 0.7 all_to_all.83
  5.2 10.2 %all-to-all-start.1 = ((s32[16,8,1]{1,2,0:T(1,128)}), s32[16,8,1]{1,2,0:T(1,128)S(1)}, u32[]{:S(2)}, u32[]{:S(2)}) async-start(s32[16,8,1]{1,2,0:T(1,128)} %bitcast.14), calls=%async_computation.1 | async-start | bytes 16384 | tf_op jit(solution)/shard_map/all_to_all | solution.py:55
  15.3 1.9 multiply_reduce_fusion.5
  17.3 103.1 %psum.35 = f32[]{:T(128)} all-reduce(f32[]{:T(128)} %multiply_reduce_fusion.5), channel_id=1, replica_groups=mesh['row'=16,'col'=32] {'row','col'}, use_global_device_ids=true, to_apply=%region_3.4 | all-reduce | flops 1 | bytes 8 | tf_op jit(solution)/shard_map/psum | solution.py:64
  121.1 0.9 convert_reduce_fusion.1
  122.0 0.7 fusion.42
  122.7 1.2 convert_bitcast_fusion.1
  123.9 0.8 scatter_custom_fusion
  124.7 0.7 all_to_all.80
  125.4 3.8 all-to-all-start
  129.7 0.7 reduce.6
  130.5 1.3 gather_fusion
  131.8 6.0 all-to-all-done
  137.8 8.0 %all-to-all-start.2 = ((bf16[16,8,128]{2,1,0:T(8,128)(2,1)}), bf16[16,8,128]{2,1,0:T(8,128)(2,1)S(1)}, u32[]{:S(2)}, u32[]{:S(2)}) async-start(bf16[16,8,128]{2,1,0:T(8,128)(2,1)} %bitcast.16), calls=%async_computation.2 | async-start | bytes 65536 | tf_op jit(solution)/shard_map/all_to_all | solution.py:73
  145.8 0.7 reduce.7
  146.6 1.3 gather_fusion.2
  148.0 5.2 all-to-all-done.2
  153.2 3.9 all-to-all-start.4
  157.1 0.6 gather_fusion.1
  157.7 8.1 %all-to-all-done.4 = bf16[32,4,128]{2,1,0:T(4,128)(2,1)S(1)} async-done(((bf16[32,4,128]{2,1,0:T(4,128)(2,1)}), bf16[32,4,128]{2,1,0:T(4,128)(2,1)S(1)}, u32[]{:S(2)}, u32[]{:S(2)}) %all-to-all-start.4) | async-done | bytes 32800 | tf_op jit(solution)/shard_map/all_to_all | solution.py:71
  166.5 0.6 fusion.4
  167.1 1.4 scatter_custom_fusion.4
  168.5 4.9 all-to-all-start.5
  173.4 1.2 fusion.6
  174.6 1.4 scatter_custom_fusion.2
  176.0 5.3 all-to-all-done.5
  181.3 3.9 all-to-all-start.3
  185.1 2.3 scatter_custom_fusion.5
  187.4 6.6 %all-to-all-done.3 = f32[32,4,128]{2,1,0:T(4,128)S(1)} async-done(((f32[32,4,128]{2,1,0:T(4,128)}), f32[32,4,128]{2,1,0:T(4,128)S(1)}, u32[]{:S(2)}, u32[]{:S(2)}) %all-to-all-start.3) | async-done | bytes 65568 | tf_op jit(solution)/shard_map/all_to_all | solution.py:79
  194.0 2.3 scatter_custom_fusion.3
  196.3 2.2 multiply_reduce_fusion.4
  198.5 93.6 %psum.36 = f32[1]{0:T(128)} all-reduce(f32[1]{0:T(128)} %bitcast.34), channel_id=1, replica_groups=mesh['row'=16,'col'=32] {'row','col'}, use_global_device_ids=true, to_apply=%region_11.12 | all-reduce | flops 1 | bytes 8 | tf_op jit(solution)/shard_map/psum | solution.py:84
  292.8 2.2 multiply_reduce_fusion.3
  295.0 95.2 %psum.37 = f32[]{:T(128)} all-reduce(f32[]{:T(128)} %multiply_reduce_fusion.3), channel_id=1, replica_groups=mesh['row'=16,'col'=32] {'row','col'}, use_global_device_ids=true, to_apply=%region_13.14 | all-reduce | flops 1 | bytes 8 | tf_op jit(solution)/shard_map/psum | solution.py:89
  390.9 2.4 convert_bitcast_fusion
  393.3 1.3 gather_fusion.4
  394.6 5.3 all-to-all-start.6
  399.9 1.3 gather_fusion.6
  401.2 6.1 all-to-all-done.6
  407.3 4.8 all-to-all-start.8
  412.7 8.1 %all-to-all-done.8 = bf16[32,4,128]{2,1,0:T(4,128)(2,1)S(1)} async-done(((bf16[32,4,128]{2,1,0:T(4,128)(2,1)}), bf16[32,4,128]{2,1,0:T(4,128)(2,1)S(1)}, u32[]{:S(2)}, u32[]{:S(2)}) %all-to-all-start.8) | async-done | bytes 32800 | tf_op jit(solution)/shard_map/all_to_all | solution.py:71
  421.5 0.6 fusion
  422.1 1.4 scatter_custom_fusion.8
  423.5 5.1 all-to-all-start.9
  428.6 1.2 fusion.2
  429.8 1.4 scatter_custom_fusion.6
  431.2 5.3 all-to-all-done.9
  436.4 3.9 all-to-all-start.7
  440.3 2.3 scatter_custom_fusion.9
  442.6 6.6 %all-to-all-done.7 = f32[32,4,128]{2,1,0:T(4,128)S(1)} async-done(((f32[32,4,128]{2,1,0:T(4,128)}), f32[32,4,128]{2,1,0:T(4,128)S(1)}, u32[]{:S(2)}, u32[]{:S(2)}) %all-to-all-start.7) | async-done | bytes 65568 | tf_op jit(solution)/shard_map/all_to_all | solution.py:79
  449.1 2.3 scatter_custom_fusion.7
  451.4 2.5 multiply_reduce_fusion.2
  453.9 1.4 pad_maximum_fusion.1
  455.3 93.7 %psum.38 = f32[2]{0:T(128)S(1)} all-reduce(f32[2]{0:T(128)S(1)} %pad_maximum_fusion.1), channel_id=1, replica_groups=mesh['row'=16,'col'=32] {'row','col'}, use_global_device_ids=true, to_apply=%region_20.21 | all-reduce | flops 2 | bytes 16 | tf_op jit(solution)/shard_map/psum | solution.py:84
  549.0 0.7 fusion.53
  549.6 4.6 multiply_reduce_fusion
  554.3 95.3 %psum.39 = f32[]{:T(128)} all-reduce(f32[]{:T(128)} %get-tuple-element.5), channel_id=1, replica_groups=mesh['row'=16,'col'=32] {'row','col'}, use_global_device_ids=true, to_apply=%region_22.23 | all-reduce | flops 1 | bytes 8 | tf_op jit(solution)/shard_map/psum | solution.py:89
  650.3 1.2 broadcast_divide_fusion
  651.5 1.3 pad_maximum_fusion.2
  652.7 2.3 pad_maximum_fusion
  (21 shorter events, 2.7 us)
Async XLA Ops:
  0.6 165.9 %copy-start = (bf16[1,1,64,128,128]{4,3,2,1,0:T(8,128)(2,1)S(1)}, bf16[1,1,64,128,128]{4,3,2,1,0:T(8,128)(2,1)}, u32[]{:S(2)}) copy-start(bf16[1,1,64,128,128]{4,3,2,1,0:T(8,128)(2,1)} %param.8) | copy-start | bytes 6291460
  5.2 120.2 %all-to-all-start.1 = ((s32[16,8,1]{1,2,0:T(1,128)}), s32[16,8,1]{1,2,0:T(1,128)S(1)}, u32[]{:S(2)}, u32[]{:S(2)}) async-start(s32[16,8,1]{1,2,0:T(1,128)} %bitcast.14), calls=%async_computation.1 | async-start | bytes 16384 | tf_op jit(solution)/shard_map/all_to_all | solution.py:55
  125.4 12.4 %all-to-all-start = ((s32[32,4,1]{1,2,0:T(1,128)}), s32[32,4,1]{1,2,0:T(1,128)S(1)}, u32[]{:S(2)}, u32[]{:S(2)}) async-start(s32[32,4,1]{1,2,0:T(1,128)} %bitcast.6), calls=%async_computation | async-start | bytes 32768 | tf_op jit(solution)/shard_map/all_to_all | solution.py:48
  137.8 15.4 %all-to-all-start.2 = ((bf16[16,8,128]{2,1,0:T(8,128)(2,1)}), bf16[16,8,128]{2,1,0:T(8,128)(2,1)S(1)}, u32[]{:S(2)}, u32[]{:S(2)}) async-start(bf16[16,8,128]{2,1,0:T(8,128)(2,1)} %bitcast.16), calls=%async_computation.2 | async-start | bytes 65536 | tf_op jit(solution)/shard_map/all_to_all | solution.py:73
  153.2 12.6 %all-to-all-start.4 = ((bf16[32,4,128]{2,1,0:T(4,128)(2,1)}), bf16[32,4,128]{2,1,0:T(4,128)(2,1)S(1)}, u32[]{:S(2)}, u32[]{:S(2)}) async-start(bf16[32,4,128]{2,1,0:T(4,128)(2,1)} %bitcast.26), calls=%async_computation.4 | async-start | bytes 65536 | tf_op jit(solution)/shard_map/all_to_all | solution.py:71
  168.5 27.7 %copy-start.1 = (f32[196608]{0:T(1024)S(1)}, f32[196608]{0:T(1024)}, u32[]{:S(2)}) copy-start(f32[196608]{0:T(1024)} %param.7) | copy-start | bytes 2359300
  168.5 12.7 %all-to-all-start.5 = ((f32[16,8,128]{2,1,0:T(8,128)}), f32[16,8,128]{2,1,0:T(8,128)S(1)}, u32[]{:S(2)}, u32[]{:S(2)}) async-start(f32[16,8,128]{2,1,0:T(8,128)} %bitcast.31), calls=%async_computation.5 | async-start | bytes 131072 | tf_op jit(solution)/shard_map/all_to_all | solution.py:80
  181.3 12.7 %all-to-all-start.3 = ((f32[32,4,128]{2,1,0:T(4,128)}), f32[32,4,128]{2,1,0:T(4,128)S(1)}, u32[]{:S(2)}, u32[]{:S(2)}) async-start(f32[32,4,128]{2,1,0:T(4,128)} %bitcast.22), calls=%async_computation.3 | async-start | bytes 131072 | tf_op jit(solution)/shard_map/all_to_all | solution.py:79
  394.6 12.6 %all-to-all-start.6 = ((bf16[16,8,128]{2,1,0:T(8,128)(2,1)}), bf16[16,8,128]{2,1,0:T(8,128)(2,1)S(1)}, u32[]{:S(2)}, u32[]{:S(2)}) async-start(bf16[16,8,128]{2,1,0:T(8,128)(2,1)} %bitcast.38), calls=%async_computation.6 | async-start | bytes 65536 | tf_op jit(solution)/shard_map/all_to_all | solution.py:73
  407.3 13.5 %all-to-all-start.8 = ((bf16[32,4,128]{2,1,0:T(4,128)(2,1)}), bf16[32,4,128]{2,1,0:T(4,128)(2,1)S(1)}, u32[]{:S(2)}, u32[]{:S(2)}) async-start(bf16[32,4,128]{2,1,0:T(4,128)(2,1)} %bitcast.45), calls=%async_computation.8 | async-start | bytes 65536 | tf_op jit(solution)/shard_map/all_to_all | solution.py:71
  423.5 12.9 %all-to-all-start.9 = ((f32[16,8,128]{2,1,0:T(8,128)}), f32[16,8,128]{2,1,0:T(8,128)S(1)}, u32[]{:S(2)}, u32[]{:S(2)}) async-start(f32[16,8,128]{2,1,0:T(8,128)} %bitcast.50), calls=%async_computation.9 | async-start | bytes 131072 | tf_op jit(solution)/shard_map/all_to_all | solution.py:80
  436.4 12.7 %all-to-all-start.7 = ((f32[32,4,128]{2,1,0:T(4,128)}), f32[32,4,128]{2,1,0:T(4,128)S(1)}, u32[]{:S(2)}, u32[]{:S(2)}) async-start(f32[32,4,128]{2,1,0:T(4,128)} %bitcast.43), calls=%async_computation.7 | async-start | bytes 131072 | tf_op jit(solution)/shard_map/all_to_all | solution.py:79
  554.3 98.5 %copy-start.2 = (f32[196608]{0:T(1024)S(1)}, f32[196608]{0:T(1024)}, u32[]{:S(2)}) copy-start(f32[196608]{0:T(1024)} %get-tuple-element.8) | copy-start | bytes 2359300
where the time goes:
time: 658 us; the launch traced here: 656 us
  blocking collectives  481 us (73%)
  waiting for transfers between devices  57.3 us (9%)
  starting transfers between devices  53.5 us (8%)
  other arithmetic  43.2 us (7%)
  local copies, waits for them, and re-layouts  12.1 us (2%)
    psum x2, blocking collectives, per_device(): square = lax.psum(jnp.sum(update * update), ('row', 'col')) / total  191 us
    psum x2, blocking collectives, per_device(): lax.psum(jnp.stack([jnp.sum(older * image) for older in basis]), ('row',...  187 us
    psum x1, blocking collectives, per_device(): energy = lax.psum(jnp.sum(start_vector * start_vector), ('row', 'col'))  103 us
    all_to_all x2, waiting for transfers between devices, per_device(): lax.all_to_all(narrow[safe_r], 'col', split_axis=0, concat_axis=0, tiled=...  16.3 us
    all_to_all x2, starting transfers between devices, per_device(): lax.all_to_all(narrow[safe_c], 'row', split_axis=0, concat_axis=0, tiled=...  13.3 us
    all_to_all x2, waiting for transfers between devices, per_device(): lax.all_to_all(outgoing_r, 'col', split_axis=0, concat_axis=0, tiled=True)  13.2 us
  transfers between devices with their start and end apart: 10, of which 9 were waited for; matrix products, arithmetic and copies ran while one was open for 3% of the time, Pallas kernels for 0%

commit v1 on v0

v1 whole, which is shorter than its diff:
```python
import jax
import jax.numpy as jnp
from jax import lax
from jax.experimental import pallas as pl
from jax.experimental.pallas import tpu as pltpu
from jax.sharding import PartitionSpec as P

TILE = 128
LANE = 8
HALF = 4
SCALE = 1024.0
F32 = jnp.float32
BF16 = jnp.bfloat16
VMEM = pl.BlockSpec(memory_space=pltpu.VMEM)
SMEM = pl.BlockSpec(memory_space=pltpu.SMEM)


def iota(shape, axis):
    return lax.broadcasted_iota(jnp.int32, shape, axis)


def halves(x):
    high = x.astype(BF16)
    low = (x - high.astype(F32)).astype(BF16)
    return high, low


def dot(a, b):
    return jnp.dot(a, b, preferred_element_type=F32)


def exact_dot(select, x):
    high, low = halves(x)
    return dot(select, high) + dot(select, low)


def place_of(owner):
    count = owner.shape[1]
    shape = (count, count)
    down, across = iota(shape, 0), iota(shape, 1)
    column = jnp.sum(jnp.where(down == across, owner, 0.0), axis=1, keepdims=True)
    same = column == owner
    rank_row = jnp.sum(jnp.where(same & (down < across), 1.0, 0.0), axis=0, keepdims=True)
    rank_column = jnp.sum(jnp.where(same & (across < down), 1.0, 0.0), axis=1, keepdims=True)
    return (owner * LANE + rank_row).astype(jnp.int32), (column * LANE + rank_column).astype(jnp.int32)


def request_kernel(own_r, blk_r, own_c, blk_c, filled, ask_row, ask_col, pick_row, put_row, pick_col, put_col):
    count = own_r.shape[1]
    alive = iota((1, count), 1) < filled[...]
    for owner, block, ask, pick, put, shift in (
        (own_c, blk_c, ask_row, pick_row, put_row, 0),
        (own_r, blk_r, ask_col, pick_col, put_col, HALF),
    ):
        width = ask.shape[0]
        across, down = place_of(owner[...].astype(F32))
        value = jnp.where(alive, block[...] + 1, 0).astype(F32)
        spot = iota((width, count), 0)
        there = spot == across
        back = spot == across + shift
        wanted = jnp.sum(jnp.where(there | back, value, 0.0), axis=1, keepdims=True) - 1.0
        ask[...] = jnp.broadcast_to(wanted, (width, TILE)).astype(jnp.int32)
        pick[...] = jnp.where(iota((count, width), 1) == down, 1.0, 0.0).astype(BF16)
        put[...] = jnp.where(back, 1.0, 0.0).astype(BF16)


def gather(asked, vector):
    pieces = vector.shape[0]
    rows = asked.shape[0]
    lanes = iota((rows, TILE), 1)
    select = jnp.concatenate(
        [jnp.where(asked == lanes + k * TILE, 1.0, 0.0).astype(BF16) for k in range(pieces // TILE)], axis=1
    )
    return exact_dot(select, vector)


def gather_kernel(asked, vector, out, energy):
    v = vector[...] * SCALE
    out[...] = gather(asked[...], v)
    energy[...] = jnp.sum((v * v).reshape(-1, 8, TILE), axis=0)


def product_lane(asked_row, asked_col):
    rows = [asked_row[...].astype(F32).T[0:1, :]]
    width = asked_col.shape[0]
    for k in range(width // TILE):
        part = asked_col[k * TILE : (k + 1) * TILE, :].astype(F32).T[0:1, :]
        lane = iota((1, TILE), 1)
        rows.append(jnp.where(lane % LANE >= HALF, part, -2.0))
    return [row.astype(jnp.int32) for row in rows]


def meet_kernel(asked_row, asked_col, vector, out, meet):
    out[...] = gather(asked_col[...], vector[...] * SCALE)
    lanes = product_lane(asked_row, asked_col)
    base = 0
    for asked in (asked_row, asked_col):
        mine = asked[...]
        for k, lane in enumerate(lanes):
            hit = (mine == lane) & (mine >= 0)
            meet[base : base + mine.shape[0], k * TILE : (k + 1) * TILE] = jnp.where(hit, 1.0, 0.0).astype(BF16)
        base += mine.shape[0]


def multiply(x, tiles, across):
    count = x.shape[0]
    dims = (((1,), (1 if across else 0,)), ((), ()))
    row = iota((8, TILE), 0)
    groups = []
    for g in range(count // 8):
        part = x[g * 8 : (g + 1) * 8, :]
        high = part.astype(BF16).astype(F32)
        both = jnp.concatenate([high, part - high], axis=0).astype(BF16)
        total = jnp.zeros((8, TILE), F32)
        for j in range(8):
            y = lax.dot_general(both, tiles[g * 8 + j], dims, preferred_element_type=F32)
            total = jnp.where(row == j, y[0:8] + y[8:16], total)
        groups.append(total)
    return jnp.concatenate(groups, axis=0)


def direct_kernel(got, pick, tiles, put, extra, out):
    y = multiply(exact_dot(pick[...], got[...]), tiles, True)
    forward = iota(extra.shape, 0) % LANE < HALF
    out[...] = exact_dot(put[...], y) + jnp.where(forward, extra[...], 0.0)


def mirror_kernel(got, pick, tiles, put, out):
    y = multiply(exact_dot(pick[...], got[...]), tiles, False)
    out[...] = exact_dot(put[...], y)


def sum_kernel(meet, back_row, back_col, out_row, out_col):
    total = exact_dot(meet[...], jnp.concatenate([back_row[...], back_col[...]], axis=0))
    width = out_row.shape[0]
    out_row[...] = total[:width]
    out_col[...] = total[width:]


def inner_kernel(
    meet, energy, v_row, v_col, i_row, i_col, first_row, first_col, second_row, second_col, out
):
    total = exact_dot(meet[...], jnp.concatenate([second_row[...], second_col[...]], axis=0))
    width = v_row.shape[0]
    returned = iota(v_col.shape, 0) % LANE >= HALF
    first_c = jnp.where(returned, first_col[...], 0.0)
    second_c = jnp.where(returned, second_col[...], 0.0)
    first_r, second_r = first_row[...], second_row[...]

    def inner(a_r, b_r, a_c, b_c):
        rows = jnp.sum(a_r * b_r, axis=0, keepdims=True) + jnp.sum(a_c * b_c, axis=0, keepdims=True)
        return jnp.sum(rows, axis=1, keepdims=True)

    values = [
        jnp.sum(jnp.sum(energy[...], axis=0, keepdims=True), axis=1, keepdims=True),
        inner(v_row[...], first_r, v_col[...], first_c),
        inner(i_row[...], first_r, i_col[...], first_c),
        inner(v_row[...], second_r, v_col[...], second_c),
        inner(i_row[...], second_r, i_col[...], second_c),
        inner(total[:width], second_r, total[width:], second_c),
    ]
    lane = iota((1, TILE), 1)
    packed = jnp.zeros((1, TILE), F32)
    for k, value in enumerate(values):
        packed = jnp.where(lane == k, value, packed)
    out[...] = jnp.broadcast_to(packed, out.shape)


def partial_kernel(got, out):
    total = jnp.sum(got[...], axis=0, keepdims=True) * (1.0 / LANE)
    out[...] = jnp.broadcast_to(total, out.shape)


def spread_kernel(asked_row, asked_col, back_row, back_col, out):
    lanes = jnp.concatenate(product_lane(asked_row, asked_col), axis=1)
    high, low = halves(jnp.concatenate([back_row[...], back_col[...]], axis=0))
    step = 256
    for start in range(0, out.shape[0], step):
        place = iota((step, lanes.shape[1]), 0) + start
        select = jnp.where(place == lanes, 1.0, 0.0).astype(BF16)
        out[start : start + step, :] = dot(select, high) + dot(select, low)


def final_kernel(total, got, vector, image, second, out, alpha, rest):
    sums = jnp.sum(got[...], axis=0, keepdims=True) * (1.0 / LANE)
    lane = iota((1, TILE), 1)

    def value(k):
        return jnp.sum(jnp.where(lane == k, sums, 0.0), axis=1, keepdims=True)

    vv, vi, ii, vw, iw, ww = [value(k) for k in range(6)]
    g = 1.0 / (SCALE * jnp.sqrt(vv / (total * SCALE * SCALE) + 1e-06))
    c0 = g * (g * vi / total)
    square = g * (g * (ii - 2.0 * c0 * vi + c0 * c0 * vv) / total)
    b0 = jnp.sqrt(jnp.maximum(square, 0.0) + 1e-06)
    h = g / b0
    c10 = h * (g * (vw - c0 * vi) / total)
    c11 = h * (h * (iw - c0 * ii - c0 * vw + c0 * c0 * vi) / total)
    a = c0 + c11
    b = c11 * c0 - c10 * b0
    square = h * (h * (ww + a * a * ii + b * b * vv - 2.0 * a * iw + 2.0 * b * vw - 2.0 * a * b * vi) / total)
    b1 = jnp.sqrt(jnp.maximum(square, 0.0) + 1e-06)
    f = h / b1
    pieces = vector.shape[0]
    v, i = vector[...], image[...]
    out[pl.ds(0, pieces, 2), :] = h * i - (h * c0 * SCALE) * v
    out[pl.ds(1, pieces, 2), :] = f * second[...] - (f * a) * i + (f * b * SCALE) * v
    alpha[0] = c0[0, 0]
    rest[0] = b0[0, 0]
    rest[1] = c11[0, 0]
    rest[2] = b1[0, 0]


def shape(*dims, dtype=F32):
    return jax.ShapeDtypeStruct(dims, dtype)


def call(kernel, outs, *args, flops=0):
    many = isinstance(outs, tuple)
    return pl.pallas_call(
        kernel,
        out_shape=outs,
        in_specs=[VMEM] * len(args),
        out_specs=tuple([VMEM] * len(outs)) if many else VMEM,
        compiler_params=pltpu.CompilerParams(vmem_limit_bytes=32 * 1024 * 1024),
    )(*args)


def exchange(x, axis, count):
    sent = x.reshape(count, LANE, TILE)
    got = lax.all_to_all(sent, axis, split_axis=0, concat_axis=0, tiled=True)
    return got.reshape(x.shape)


def per_device(start_vector, tile_blocks, row_owner, row_block, col_owner, col_block, tile_counts):
    tiles = tile_blocks[0, 0]
    count = tiles.shape[0]
    vector = start_vector.reshape(-1, TILE)
    pieces = vector.shape[0]
    n_row, n_col = lax.axis_size("row"), lax.axis_size("col")
    wide_r, wide_c = n_row * LANE, n_col * LANE
    every = wide_r + wide_c
    total = float(pieces * TILE * n_row * n_col)

    def over_row(x):
        return exchange(x, "row", n_row)

    def over_col(x):
        return exchange(x, "col", n_col)

    ask_row, ask_col, pick_row, put_row, pick_col, put_col = call(
        request_kernel,
        (
            shape(wide_r, TILE, dtype=jnp.int32),
            shape(wide_c, TILE, dtype=jnp.int32),
            shape(count, wide_r, dtype=BF16),
            shape(wide_r, count, dtype=BF16),
            shape(count, wide_c, dtype=BF16),
            shape(wide_c, count, dtype=BF16),
        ),
        row_owner.reshape(1, count),
        row_block.reshape(1, count),
        col_owner.reshape(1, count),
        col_block.reshape(1, count),
        tile_counts.reshape(1, 1),
    )
    asked_row = over_row(ask_row)
    asked_col = over_col(ask_col)
    v_row, energy = call(gather_kernel, (shape(wide_r, TILE), shape(8, TILE)), asked_row, vector)
    x_col = over_row(v_row)
    v_col, meet = call(
        meet_kernel, (shape(wide_c, TILE), shape(every, every, dtype=BF16)), asked_row, asked_col, vector
    )
    first_col = over_col(call(direct_kernel, shape(wide_c, TILE), x_col, pick_row, tiles, put_col, v_col))
    first_row = over_row(call(mirror_kernel, shape(wide_r, TILE), first_col, pick_col, tiles, put_row))
    i_row, i_col = call(sum_kernel, (shape(wide_r, TILE), shape(wide_c, TILE)), meet, first_row, first_col)
    x_col = over_row(i_row)
    image = call(spread_kernel, shape(pieces, TILE), asked_row, asked_col, first_row, first_col)
    second_col = over_col(call(direct_kernel, shape(wide_c, TILE), x_col, pick_row, tiles, put_col, i_col))
    second_row = over_row(call(mirror_kernel, shape(wide_r, TILE), second_col, pick_col, tiles, put_row))
    inner = call(
        inner_kernel,
        shape(wide_r, TILE),
        meet,
        energy,
        v_row,
        v_col,
        i_row,
        i_col,
        first_row,
        first_col,
        second_row,
        second_col,
    )
    inner = over_row(inner)
    second = call(spread_kernel, shape(pieces, TILE), asked_row, asked_col, second_row, second_col)
    inner = over_col(call(partial_kernel, shape(wide_c, TILE), inner))

    def finish(*refs):
        final_kernel(total, *refs)

    out, alpha, rest = pl.pallas_call(
        finish,
        out_shape=(shape(2 * pieces, TILE), shape(1), shape(3)),
        in_specs=[VMEM] * 4,
        out_specs=(VMEM, SMEM, SMEM),
        compiler_params=pltpu.CompilerParams(vmem_limit_bytes=32 * 1024 * 1024),
    )(inner, vector, image, second)
    basis = out.reshape(pieces, 2, TILE).transpose(1, 0, 2).reshape(2, pieces * TILE)
    return (basis, alpha, rest)


def solution(mesh):
    return jax.shard_map(
        per_device,
        mesh=mesh,
        in_specs=(
            P(("row", "col")),
            P("row", "col", None, None, None),
            P("row", "col", None, None),
            P("row", "col", None),
            P("row", "col", None, None),
            P("row", "col", None),
            P("row", "col"),
        ),
        out_specs=(P(None, ("row", "col")), P(), P()),
        check_vma=False,
    )
```

time: 658 us -> 150 us (0.23)
  blocking collectives: 481 us -> 87.5 us
  other arithmetic: 43.2 us -> 0 us
  waiting for transfers between devices: 57.3 us -> 20.3 us
  starting transfers between devices: 53.5 us -> 21.2 us
  Pallas kernels: 0 us -> 13.5 us
  local copies, waits for them, and re-layouts: 12.1 us -> 4.88 us
    psum x5 -> x0, blocking collectives: 481 us -> none  [the longest x2 191 us: per_device(): square = lax.psum(jnp.sum(update * update), ('row', 'col')) / total]
    all_to_all x0 -> x7, blocking collectives: none -> 87.5 us  [exchange(): got = lax.all_to_all(sent, axis, split_axis=0, concat_axis=0, tiled=True)]
    all_to_all x10 -> x3, waiting for transfers between devices: 57.3 us -> 20.3 us  [exchange(): got = lax.all_to_all(sent, axis, split_axis=0, concat_axis=0, tiled=True)]
    all_to_all x10 -> x3, starting transfers between devices: 53.5 us -> 21.2 us  [exchange(): got = lax.all_to_all(sent, axis, split_axis=0, concat_axis=0, tiled=True)]
    reduce_sum x7 -> x0, other arithmetic: 15.3 us -> none  [the longest x2 6.83 us: per_device(): square = lax.psum(jnp.sum(update * update), ('row', 'col')) / total]
    pallas_call x0 -> x13, Pallas kernels: none -> 13.5 us  [the longest x12 11.6 us: call(): pl.pallas_call(kernel, out_shape=outs, in_specs=[VMEM] * len(args), out_s...]
    scatter-add x4 -> x0, other arithmetic: 9.14 us -> none  [add_received(): jnp.zeros((pieces + 1, received.shape[1]), jnp.float32).at[target]]
    gather x8 -> x0, local copies, waits for them, and re-layouts: 7.77 us -> none  [the longest x2 2.63 us: per_device(): narrow[safe_r]]
  transfers between devices with their start and end apart: 10 -> 3, of which waited for: 9 -> 3; matrix products, arithmetic and copies ran while one was open for 3% -> 0% of each run, Pallas kernels for 0% -> 2%
where the time goes in v1:
time: 150 us; the launch traced here: 149 us
  blocking collectives  87.5 us (58%)
  starting transfers between devices  21.2 us (14%)
  waiting for transfers between devices  20.3 us (14%)
  Pallas kernels  13.5 us (9%)
  local copies, waits for them, and re-layouts  4.88 us (3%)
  between operations  1.55 us (1%)
    all_to_all x7, blocking collectives, exchange(): got = lax.all_to_all(sent, axis, split_axis=0, concat_axis=0, tiled=True)  87.5 us
    all_to_all x3, starting transfers between devices, exchange(): got = lax.all_to_all(sent, axis, split_axis=0, concat_axis=0, tiled=True)  21.2 us
    all_to_all x3, waiting for transfers between devices, exchange(): got = lax.all_to_all(sent, axis, split_axis=0, concat_axis=0, tiled=True)  20.3 us
    pallas_call x12, Pallas kernels, call(): pl.pallas_call(kernel, out_shape=outs, in_specs=[VMEM] * len(args), out_s...  11.6 us
    unnamed x16, local copies, waits for them, and re-layouts  4.88 us
  transfers between devices with their start and end apart: 3, of which 3 were waited for; matrix products, arithmetic and copies ran while one was open for 0% of the time, Pallas kernels for 2%

profile of v1, /device:TPU:1, one launch (start us, length us, event | category | flops | bytes accessed | tf_op | source)
XLA Modules:
  0.0 148.9 jit_solution(15435458254785620813)
XLA Ops:
  0.6 0.0 copy-start
  1.4 0.0 copy-start.4
  1.4 0.6 copy-done.4
  2.1 0.0 copy-start.5
  2.1 0.7 copy-done.5
  2.7 0.0 copy-start.6
  2.8 0.7 copy-done.6
  3.4 0.0 copy-start.7
  3.4 0.7 copy-done.7
  4.1 0.9 shard_map.94
  5.0 17.1 %all_to_all.50 = s32[16,8,128]{2,1,0:T(8,128)S(1)} all-to-all(s32[16,8,128]{2,1,0:T(8,128)S(1)} %bitcast.67), channel_id=1, replica_groups=mesh['row'=16,'col'=32] {'row'}, dimensions={0} | all-to-all | bytes 131072 | tf_op jit(solution)/shard_map/all_to_all | solution.py:231
  22.1 12.0 %all-to-all-start.1 = ((s32[32,8,128]{2,1,0:T(8,128)}), s32[32,8,128]{2,1,0:T(8,128)S(1)}, u32[]{:S(2)}, u32[]{:S(2)}) async-start(s32[32,8,128]{2,1,0:T(8,128)} %bitcast.6), calls=%async_computation.1 | async-start | bytes 262144 | tf_op jit(solution)/shard_map/all_to_all | solution.py:231
  34.1 0.0 copy-start.1
  34.1 1.1 copy-done.1
  35.2 1.1 shard_map.96
  36.4 6.9 %all-to-all-done.1 = s32[32,8,128]{2,1,0:T(8,128)S(1)} async-done(((s32[32,8,128]{2,1,0:T(8,128)}), s32[32,8,128]{2,1,0:T(8,128)S(1)}, u32[]{:S(2)}, u32[]{:S(2)}) %all-to-all-start.1) | async-done | bytes 131104 | tf_op jit(solution)/shard_map/all_to_all | solution.py:231
  43.2 5.4 %all-to-all-start.2 = ((f32[16,8,128]{2,1,0:T(8,128)}), f32[16,8,128]{2,1,0:T(8,128)S(1)}, u32[]{:S(2)}, u32[]{:S(2)}) async-start(f32[16,8,128]{2,1,0:T(8,128)} %bitcast.9), calls=%async_computation.2 | async-start | bytes 131072 | tf_op jit(solution)/shard_map/all_to_all | solution.py:231
  48.6 0.0 copy-start.2
  48.6 1.1 copy-done.2
  49.7 0.7 shard_map.95
  50.4 6.0 %all-to-all-done.2 = f32[16,8,128]{2,1,0:T(8,128)S(1)} async-done(((f32[16,8,128]{2,1,0:T(8,128)}), f32[16,8,128]{2,1,0:T(8,128)S(1)}, u32[]{:S(2)}, u32[]{:S(2)}) %all-to-all-start.2) | async-done | bytes 65568 | tf_op jit(solution)/shard_map/all_to_all | solution.py:231
  56.4 0.0 copy-done
  56.5 1.5 %shard_map.97 = f32[256,128]{1,0:T(8,128)S(1)} custom-call(f32[128,128]{1,0:T(8,128)S(1)} %bitcast.61, bf16[64,128]{1,0:T(8,128)(2,1)S(1)} %get-tuple-element.24.pick, bf16[64,128,128]{2,1,0:T(8,128)(2,1)S(1)} %bitcast.31, bf16[256,64]{1,0:T(8,128)(2,1)S(1)} %get-tuple-element.25.put, f32[256,128]{1,0:T(8,128)S(1)} %get-tuple-element.23.extra.v_col), custom_call_target="tpu_custom_call" | custom-call | tf_op jit(solution)/shard_map/pallas_call | solution.py:220
  58.0 12.4 %all_to_all.51 = f32[32,8,128]{2,1,0:T(8,128)S(1)} all-to-all(f32[32,8,128]{2,1,0:T(8,128)S(1)} %bitcast.59), channel_id=1, replica_groups=mesh['row'=16,'col'=32] {'col'}, dimensions={0} | all-to-all | bytes 262144 | tf_op jit(solution)/shard_map/all_to_all | solution.py:231
  70.4 0.9 shard_map.98
  71.3 12.3 %all_to_all.52 = f32[16,8,128]{2,1,0:T(8,128)S(1)} all-to-all(f32[16,8,128]{2,1,0:T(8,128)S(1)} %bitcast.66), channel_id=1, replica_groups=mesh['row'=16,'col'=32] {'row'}, dimensions={0} | all-to-all | bytes 131072 | tf_op jit(solution)/shard_map/all_to_all | solution.py:231
  83.7 0.3 shard_map.99
  84.0 10.4 %all_to_all.53 = f32[16,8,128]{2,1,0:T(8,128)S(1)} all-to-all(f32[16,8,128]{2,1,0:T(8,128)S(1)} %bitcast.60), channel_id=1, replica_groups=mesh['row'=16,'col'=32] {'row'}, dimensions={0} | all-to-all | bytes 131072 | tf_op jit(solution)/shard_map/all_to_all | solution.py:231
  94.4 1.5 %shard_map.100 = f32[256,128]{1,0:T(8,128)S(1)} custom-call(f32[128,128]{1,0:T(8,128)S(1)} %bitcast.63, bf16[64,128]{1,0:T(8,128)(2,1)S(1)} %get-tuple-element.24.pick, bf16[64,128,128]{2,1,0:T(8,128)(2,1)S(1)} %bitcast.33, bf16[256,64]{1,0:T(8,128)(2,1)S(1)} %get-tuple-element.25.put, f32[256,128]{1,0:T(8,128)S(1)} %get-tuple-element.29.extra.i_col), custom_call_target="tpu_custom_call" | custom-call | tf_op jit(solution)/shard_map/pallas_call | solution.py:220
  95.9 12.4 %all_to_all.54 = f32[32,8,128]{2,1,0:T(8,128)S(1)} all-to-all(f32[32,8,128]{2,1,0:T(8,128)S(1)} %bitcast.58), channel_id=1, replica_groups=mesh['row'=16,'col'=32] {'col'}, dimensions={0} | all-to-all | bytes 262144 | tf_op jit(solution)/shard_map/all_to_all | solution.py:231
  108.3 0.9 shard_map.101
  109.3 0.0 copy-start.3
  109.3 12.5 %all_to_all.55 = f32[16,8,128]{2,1,0:T(8,128)S(1)} all-to-all(f32[16,8,128]{2,1,0:T(8,128)S(1)} %bitcast.64), channel_id=1, replica_groups=mesh['row'=16,'col'=32] {'row'}, dimensions={0} | all-to-all | bytes 131072 | tf_op jit(solution)/shard_map/all_to_all | solution.py:231
  121.7 1.2 shard_map.102
  123.0 10.4 %all_to_all.56 = f32[16,8,128]{2,1,0:T(8,128)S(1)} all-to-all(f32[16,8,128]{2,1,0:T(8,128)S(1)} %bitcast.62), channel_id=1, replica_groups=mesh['row'=16,'col'=32] {'row'}, dimensions={0} | all-to-all | bytes 131072 | tf_op jit(solution)/shard_map/all_to_all | solution.py:231
  133.4 0.7 shard_map.103
  134.0 3.9 %all-to-all-start.9 = ((f32[32,8,128]{2,1,0:T(8,128)}), f32[32,8,128]{2,1,0:T(8,128)S(1)}, u32[]{:S(2)}, u32[]{:S(2)}) async-start(f32[32,8,128]{2,1,0:T(8,128)} %bitcast.24), calls=%async_computation.9 | async-start | bytes 262144 | tf_op jit(solution)/shard_map/all_to_all | solution.py:231
  137.9 0.9 shard_map.104.refs_2_
  138.8 0.9 shard_map.105.refs_3_
  139.7 7.4 %all-to-all-done.9 = f32[32,8,128]{2,1,0:T(8,128)S(1)} async-done(((f32[32,8,128]{2,1,0:T(8,128)}), f32[32,8,128]{2,1,0:T(8,128)S(1)}, u32[]{:S(2)}, u32[]{:S(2)}) %all-to-all-start.9) | async-done | bytes 131104 | tf_op jit(solution)/shard_map/all_to_all | solution.py:231
  147.1 0.0 copy-done.3
  147.1 1.8 %shard_map.106 = (f32[3072,128]{1,0:T(8,128)}, f32[1]{0:T(128)}, f32[3]{0:T(128)}) custom-call(f32[256,128]{1,0:T(8,128)S(1)} %bitcast.57, f32[1536,128]{1,0:T(8,128)S(1)} %bitcast.37, f32[1536,128]{1,0:T(8,128)S(1)} %shard_map.104.refs_2_, f32[1536,128]{1,0:T(8,128)S(1)} %shard_map.105.refs_3_), custom_call_target="tpu_custom_call" | custom-call | tf_op jit(solution)/shard_map/pallas_call | solution.py:302
Async XLA Ops:
  0.6 55.8 %copy-start = (bf16[1,1,64,128,128]{4,3,2,1,0:T(8,128)(2,1)S(1)}, bf16[1,1,64,128,128]{4,3,2,1,0:T(8,128)(2,1)}, u32[]{:S(2)}) copy-start(bf16[1,1,64,128,128]{4,3,2,1,0:T(8,128)(2,1)} %param.8) | copy-start | bytes 6291460
  1.4 0.7 copy-start.4
  2.1 0.7 copy-start.5
  2.7 0.7 copy-start.6
  3.4 0.7 copy-start.7
  22.1 21.1 %all-to-all-start.1 = ((s32[32,8,128]{2,1,0:T(8,128)}), s32[32,8,128]{2,1,0:T(8,128)S(1)}, u32[]{:S(2)}, u32[]{:S(2)}) async-start(s32[32,8,128]{2,1,0:T(8,128)} %bitcast.6), calls=%async_computation.1 | async-start | bytes 262144 | tf_op jit(solution)/shard_map/all_to_all | solution.py:231
  34.1 1.1 copy-start.1
  43.2 13.2 %all-to-all-start.2 = ((f32[16,8,128]{2,1,0:T(8,128)}), f32[16,8,128]{2,1,0:T(8,128)S(1)}, u32[]{:S(2)}, u32[]{:S(2)}) async-start(f32[16,8,128]{2,1,0:T(8,128)} %bitcast.9), calls=%async_computation.2 | async-start | bytes 131072 | tf_op jit(solution)/shard_map/all_to_all | solution.py:231
  48.6 1.1 copy-start.2
  109.3 37.8 %copy-start.3 = (f32[196608]{0:T(1024)S(1)}, f32[196608]{0:T(1024)}, u32[]{:S(2)}) copy-start(f32[196608]{0:T(1024)} %param.7) | copy-start | bytes 2359300
  134.0 13.0 %all-to-all-start.9 = ((f32[32,8,128]{2,1,0:T(8,128)}), f32[32,8,128]{2,1,0:T(8,128)S(1)}, u32[]{:S(2)}, u32[]{:S(2)}) async-start(f32[32,8,128]{2,1,0:T(8,128)} %bitcast.24), calls=%async_computation.9 | async-start | bytes 262144 | tf_op jit(solution)/shard_map/all_to_all | solution.py:231

commit v2 on v1

--- a/solution.py
+++ b/solution.py
@@ -13,6 +13,7 @@
 BF16 = jnp.bfloat16
 VMEM = pl.BlockSpec(memory_space=pltpu.VMEM)
 SMEM = pl.BlockSpec(memory_space=pltpu.SMEM)
+HBM = pl.BlockSpec(memory_space=pltpu.HBM)
 
 
 def iota(shape, axis):
@@ -45,7 +46,15 @@
     return (owner * LANE + rank_row).astype(jnp.int32), (column * LANE + rank_column).astype(jnp.int32)
 
 
-def request_kernel(own_r, blk_r, own_c, blk_c, filled, ask_row, ask_col, pick_row, put_row, pick_col, put_col):
+def request_kernel(*refs):
+    far, outs, near, sems = refs[:5], refs[5:11], refs[11:16], refs[16]
+    copies = [pltpu.make_async_copy(a, b, sems.at[k]) for k, (a, b) in enumerate(zip(far, near))]
+    for copy in copies:
+        copy.start()
+    for copy in copies:
+        copy.wait()
+    own_r, blk_r, own_c, blk_c, filled = near
+    ask_row, ask_col, pick_row, put_row, pick_col, put_col = outs
     count = own_r.shape[1]
     alive = iota((1, count), 1) < filled[...]
     for owner, block, ask, pick, put, shift in (
@@ -74,10 +83,12 @@
     return exact_dot(select, vector)
 
 
-def gather_kernel(asked, vector, out, energy):
+def gather_kernel(asked, vector, tiles, out, energy, turned):
     v = vector[...] * SCALE
     out[...] = gather(asked[...], v)
     energy[...] = jnp.sum((v * v).reshape(-1, 8, TILE), axis=0)
+    for t in range(tiles.shape[0]):
+        turned[t] = tiles[t].T
 
 
 def product_lane(asked_row, asked_col):
@@ -102,9 +113,8 @@
         base += mine.shape[0]
 
 
-def multiply(x, tiles, across):
+def multiply(x, tiles):
     count = x.shape[0]
-    dims = (((1,), (1 if across else 0,)), ((), ()))
     row = iota((8, TILE), 0)
     groups = []
     for g in range(count // 8):
@@ -113,20 +123,20 @@
         both = jnp.concatenate([high, part - high], axis=0).astype(BF16)
         total = jnp.zeros((8, TILE), F32)
         for j in range(8):
-            y = lax.dot_general(both, tiles[g * 8 + j], dims, preferred_element_type=F32)
+            y = dot(both, tiles[g * 8 + j])
             total = jnp.where(row == j, y[0:8] + y[8:16], total)
         groups.append(total)
     return jnp.concatenate(groups, axis=0)
 
 
-def direct_kernel(got, pick, tiles, put, extra, out):
-    y = multiply(exact_dot(pick[...], got[...]), tiles, True)
+def direct_kernel(got, pick, turned, put, extra, out):
+    y = multiply(exact_dot(pick[...], got[...]), turned)
     forward = iota(extra.shape, 0) % LANE < HALF
     out[...] = exact_dot(put[...], y) + jnp.where(forward, extra[...], 0.0)
 
 
 def mirror_kernel(got, pick, tiles, put, out):
-    y = multiply(exact_dot(pick[...], got[...]), tiles, False)
+    y = multiply(exact_dot(pick[...], got[...]), tiles)
     out[...] = exact_dot(put[...], y)
 
 
@@ -148,27 +158,26 @@
     first_r, second_r = first_row[...], second_row[...]
 
     def inner(a_r, b_r, a_c, b_c):
-        rows = jnp.sum(a_r * b_r, axis=0, keepdims=True) + jnp.sum(a_c * b_c, axis=0, keepdims=True)
-        return jnp.sum(rows, axis=1, keepdims=True)
+        return jnp.sum(a_r * b_r, axis=0, keepdims=True) + jnp.sum(a_c * b_c, axis=0, keepdims=True)
 
     values = [
-        jnp.sum(jnp.sum(energy[...], axis=0, keepdims=True), axis=1, keepdims=True),
+        jnp.sum(energy[...], axis=0, keepdims=True),
         inner(v_row[...], first_r, v_col[...], first_c),
         inner(i_row[...], first_r, i_col[...], first_c),
         inner(v_row[...], second_r, v_col[...], second_c),
         inner(i_row[...], second_r, i_col[...], second_c),
         inner(total[:width], second_r, total[width:], second_c),
     ]
-    lane = iota((1, TILE), 1)
-    packed = jnp.zeros((1, TILE), F32)
-    for k, value in enumerate(values):
-        packed = jnp.where(lane == k, value, packed)
+    packed = jnp.concatenate(values + [jnp.zeros((2, TILE), F32)], axis=0)
+    for k in range(out.shape[0]):
+        out[k] = packed
+
+
+def partial_kernel(got, out):
+    total = jnp.sum(got[...], axis=0)
+    sums = jnp.sum(total, axis=1, keepdims=True)
+    packed = jnp.sum(jnp.where(iota(total.shape, 0) == iota(total.shape, 1), sums, 0.0), axis=0, keepdims=True)
     out[...] = jnp.broadcast_to(packed, out.shape)
-
-
-def partial_kernel(got, out):
-    total = jnp.sum(got[...], axis=0, keepdims=True) * (1.0 / LANE)
-    out[...] = jnp.broadcast_to(total, out.shape)
 
 
 def spread_kernel(asked_row, asked_col, back_row, back_col, out):
@@ -181,8 +190,8 @@
         out[start : start + step, :] = dot(select, high) + dot(select, low)
 
 
-def final_kernel(total, got, vector, image, second, out, alpha, rest):
-    sums = jnp.sum(got[...], axis=0, keepdims=True) * (1.0 / LANE)
+def final_kernel(total, got, vector, image, second, out, alpha, rest, near, sems):
+    sums = jnp.sum(got[...], axis=0, keepdims=True)
     lane = iota((1, TILE), 1)
 
     def value(k):
@@ -201,33 +210,44 @@
     square = h * (h * (ww + a * a * ii + b * b * vv - 2.0 * a * iw + 2.0 * b * vw - 2.0 * a * b * vi) / total)
     b1 = jnp.sqrt(jnp.maximum(square, 0.0) + 1e-06)
     f = h / b1
-    pieces = vector.shape[0]
-    v, i = vector[...], image[...]
-    out[pl.ds(0, pieces, 2), :] = h * i - (h * c0 * SCALE) * v
-    out[pl.ds(1, pieces, 2), :] = f * second[...] - (f * a) * i + (f * b * SCALE) * v
+    parts = sems.shape[0]
+    step = vector.shape[0] // parts
+    copies = []
+    for k in range(parts):
+        rows = pl.ds(k * step, step)
+        v, i = vector[rows, :], image[rows, :]
+        near[pl.ds(2 * k * step, step, 2), :] = h * i - (h * c0 * SCALE) * v
+        near[pl.ds(2 * k * step + 1, step, 2), :] = f * second[rows, :] - (f * a) * i + (f * b * SCALE) * v
+        done = pl.ds(2 * k * step, 2 * step)
+        copies.append(pltpu.make_async_copy(near.at[done], out.at[done], sems.at[k]))
+        copies[-1].start()
     alpha[0] = c0[0, 0]
     rest[0] = b0[0, 0]
     rest[1] = c11[0, 0]
     rest[2] = b1[0, 0]
+    for copy in copies:
+        copy.wait()
 
 
 def shape(*dims, dtype=F32):
     return jax.ShapeDtypeStruct(dims, dtype)
 
 
-def call(kernel, outs, *args, flops=0):
-    many = isinstance(outs, tuple)
+def call(kernel, outs, *args, ins=VMEM, out_specs=VMEM, scratch=(), limit=32):
+    if isinstance(outs, tuple) and not isinstance(out_specs, tuple):
+        out_specs = tuple([out_specs] * len(outs))
     return pl.pallas_call(
         kernel,
         out_shape=outs,
-        in_specs=[VMEM] * len(args),
-        out_specs=tuple([VMEM] * len(outs)) if many else VMEM,
-        compiler_params=pltpu.CompilerParams(vmem_limit_bytes=32 * 1024 * 1024),
+        in_specs=[ins] * len(args),
+        out_specs=out_specs,
+        scratch_shapes=scratch,
+        compiler_params=pltpu.CompilerParams(vmem_limit_bytes=limit * 1024 * 1024),
     )(*args)
 
 
 def exchange(x, axis, count):
-    sent = x.reshape(count, LANE, TILE)
+    sent = x.reshape(count, -1, TILE)
     got = lax.all_to_all(sent, axis, split_axis=0, concat_axis=0, tiled=True)
     return got.reshape(x.shape)
 
@@ -263,24 +283,34 @@
         col_owner.reshape(1, count),
         col_block.reshape(1, count),
         tile_counts.reshape(1, 1),
+        ins=HBM,
+        limit=63,
+        scratch=[pltpu.VMEM((1, count), jnp.int32)] * 4
+        + [pltpu.VMEM((1, 1), jnp.int32), pltpu.SemaphoreType.DMA((5,))],
     )
     asked_row = over_row(ask_row)
     asked_col = over_col(ask_col)
-    v_row, energy = call(gather_kernel, (shape(wide_r, TILE), shape(8, TILE)), asked_row, vector)
+    v_row, energy, turned = call(
+        gather_kernel,
+        (shape(wide_r, TILE), shape(8, TILE), shape(*tiles.shape, dtype=BF16)),
+        asked_row,
+        vector,
+        tiles,
+    )
     x_col = over_row(v_row)
     v_col, meet = call(
         meet_kernel, (shape(wide_c, TILE), shape(every, every, dtype=BF16)), asked_row, asked_col, vector
     )
-    first_col = over_col(call(direct_kernel, shape(wide_c, TILE), x_col, pick_row, tiles, put_col, v_col))
+    first_col = over_col(call(direct_kernel, shape(wide_c, TILE), x_col, pick_row, turned, put_col, v_col))
     first_row = over_row(call(mirror_kernel, shape(wide_r, TILE), first_col, pick_col, tiles, put_row))
     i_row, i_col = call(sum_kernel, (shape(wide_r, TILE), shape(wide_c, TILE)), meet, first_row, first_col)
     x_col = over_row(i_row)
     image = call(spread_kernel, shape(pieces, TILE), asked_row, asked_col, first_row, first_col)
-    second_col = over_col(call(direct_kernel, shape(wide_c, TILE), x_col, pick_row, tiles, put_col, i_col))
+    second_col = over_col(call(direct_kernel, shape(wide_c, TILE), x_col, pick_row, turned, put_col, i_col))
     second_row = over_row(call(mirror_kernel, shape(wide_r, TILE), second_col, pick_col, tiles, put_row))
     inner = call(
         inner_kernel,
-        shape(wide_r, TILE),
+        shape(n_row, 8, TILE),
         meet,
         energy,
         v_row,
@@ -294,18 +324,21 @@
     )
     inner = over_row(inner)
     second = call(spread_kernel, shape(pieces, TILE), asked_row, asked_col, second_row, second_col)
-    inner = over_col(call(partial_kernel, shape(wide_c, TILE), inner))
+    inner = over_col(call(partial_kernel, shape(n_col, TILE), inner))
 
     def finish(*refs):
         final_kernel(total, *refs)
 
-    out, alpha, rest = pl.pallas_call(
+    out, alpha, rest = call(
         finish,
-        out_shape=(shape(2 * pieces, TILE), shape(1), shape(3)),
-        in_specs=[VMEM] * 4,
-        out_specs=(VMEM, SMEM, SMEM),
-        compiler_params=pltpu.CompilerParams(vmem_limit_bytes=32 * 1024 * 1024),
-    )(inner, vector, image, second)
+        (shape(2 * pieces, TILE), shape(1), shape(3)),
+        inner,
+        vector,
+        image,
+        second,
+        out_specs=(HBM, SMEM, SMEM),
+        scratch=[pltpu.VMEM((2 * pieces, TILE), F32), pltpu.SemaphoreType.DMA((4,))],
+    )
     basis = out.reshape(pieces, 2, TILE).transpose(1, 0, 2).reshape(2, pieces * TILE)
     return (basis, alpha, rest)
 

time: 150 us -> 150 us (level)
  waiting for transfers between devices: 20.3 us -> 16.4 us
  blocking collectives: 87.5 us -> 89.8 us
  local copies, waits for them, and re-layouts: 4.88 us -> 6.98 us
    all_to_all x3, waiting for transfers between devices: 20.3 us -> 16.4 us  [exchange(): got = lax.all_to_all(sent, axis, split_axis=0, concat_axis=0, tiled=True)]
    all_to_all x7, blocking collectives: 87.5 us -> 89.8 us  [exchange(): got = lax.all_to_all(sent, axis, split_axis=0, concat_axis=0, tiled=True)]
    unnamed x16 -> x34, local copies, waits for them, and re-layouts: 4.88 us -> 6.98 us
where the time goes in v2:
time: 150 us; the launch traced here: 149 us
  blocking collectives  89.8 us (60%)
  starting transfers between devices  20.7 us (14%)
  waiting for transfers between devices  16.4 us (11%)
  Pallas kernels  13.4 us (9%)
  local copies, waits for them, and re-layouts  6.98 us (5%)
    all_to_all x7, blocking collectives, exchange(): got = lax.all_to_all(sent, axis, split_axis=0, concat_axis=0, tiled=True)  89.8 us
    all_to_all x3, starting transfers between devices, exchange(): got = lax.all_to_all(sent, axis, split_axis=0, concat_axis=0, tiled=True)  20.7 us
    all_to_all x3, waiting for transfers between devices, exchange(): got = lax.all_to_all(sent, axis, split_axis=0, concat_axis=0, tiled=True)  16.4 us
    pallas_call x13, Pallas kernels, call(): pl.pallas_call(kernel, out_shape=outs, in_specs=[ins] * len(args), out_sp...  13.4 us
    unnamed x34, local copies, waits for them, and re-layouts  6.98 us
  transfers between devices with their start and end apart: 3, of which 3 were waited for; matrix products, arithmetic and copies ran while one was open for 0% of the time, Pallas kernels for 2%

profile of v2, /device:TPU:1, one launch (start us, length us, event | category | flops | bytes accessed | tf_op | source)
XLA Modules:
  0.0 148.7 jit_solution(9220770152279673105)
XLA Ops:
  1.3 1.7 %shard_map.94 = (s32[128,128]{1,0:T(8,128)}, s32[256,128]{1,0:T(8,128)}, bf16[64,128]{1,0:T(8,128)(2,1)}, bf16[128,64]{1,0:T(8,128)(2,1)}, bf16[64,256]{1,0:T(8,128)(2,1)}, /*index=5*/bf16[256,64]{1,0:T(8,128)(2,1)}) custom-call(s32[1,64]{1,0:T(1,128)} %bitcast.66, s32[1,64]{1,0:T(1,128)} %bitcast.67, s32[1,64]{1,0:T(1,128)} %bitcast.68, s32[1,64]{1,0:T(1,128)} %bitcast.69, ...), custom_call_target="tpu_custom_call" | custom-call | tf_op jit(solution)/shard_map/pallas_call | solution.py:239
  3.0 18.0 %all_to_all.50 = s32[16,8,128]{2,1,0:T(8,128)S(1)} all-to-all(s32[16,8,128]{2,1,0:T(8,128)} %bitcast.65), channel_id=1, replica_groups=mesh['row'=16,'col'=32] {'row'}, dimensions={0} | all-to-all | bytes 131072 | tf_op jit(solution)/shard_map/all_to_all | solution.py:251
  21.0 0.0 copy-start.9
  21.0 0.0 copy-start.14
  21.0 11.5 %all-to-all-start.1 = ((s32[32,8,128]{2,1,0:T(8,128)}), s32[32,8,128]{2,1,0:T(8,128)S(1)}, u32[]{:S(2)}, u32[]{:S(2)}) async-start(s32[32,8,128]{2,1,0:T(8,128)} %bitcast.64), calls=%async_computation.1 | async-start | bytes 262144 | tf_op jit(solution)/shard_map/all_to_all | solution.py:251
  32.4 0.0 copy-start
  32.4 1.6 %copy-done = bf16[1,1,64,128,128]{4,3,2,1,0:T(8,128)(2,1)S(1)} copy-done((bf16[1,1,64,128,128]{4,3,2,1,0:T(8,128)(2,1)S(1)}, bf16[1,1,64,128,128]{4,3,2,1,0:T(8,128)(2,1)}, u32[]{:S(2)}) %copy-start) | copy-done | bytes 2097176
  34.0 0.0 copy-start.5
  34.0 1.1 copy-done.5
  35.2 0.0 copy-start.6
  35.2 0.0 copy-start.10
  35.2 0.0 copy-start.12
  35.2 1.3 shard_map.96
  36.4 0.0 copy-start.2
  36.4 1.3 copy-done.2
  37.8 0.0 copy-start.15
  37.8 0.6 copy-done.15
  38.4 0.0 copy-start.1
  38.4 3.2 %all-to-all-done.1 = s32[32,8,128]{2,1,0:T(8,128)S(1)} async-done(((s32[32,8,128]{2,1,0:T(8,128)}), s32[32,8,128]{2,1,0:T(8,128)S(1)}, u32[]{:S(2)}, u32[]{:S(2)}) %all-to-all-start.1) | async-done | bytes 131104 | tf_op jit(solution)/shard_map/all_to_all | solution.py:251
  41.6 5.4 %all-to-all-start.2 = ((f32[16,8,128]{2,1,0:T(8,128)}), f32[16,8,128]{2,1,0:T(8,128)S(1)}, u32[]{:S(2)}, u32[]{:S(2)}) async-start(f32[16,8,128]{2,1,0:T(8,128)} %bitcast.10), calls=%async_computation.2 | async-start | bytes 131072 | tf_op jit(solution)/shard_map/all_to_all | solution.py:251
  47.0 0.0 copy-done.6
  47.0 0.7 shard_map.95
  47.7 0.0 copy-start.7
  47.7 0.7 copy-done.7
  48.4 6.4 %all-to-all-done.2 = f32[16,8,128]{2,1,0:T(8,128)S(1)} async-done(((f32[16,8,128]{2,1,0:T(8,128)}), f32[16,8,128]{2,1,0:T(8,128)S(1)}, u32[]{:S(2)}, u32[]{:S(2)}) %all-to-all-start.2) | async-done | bytes 65568 | tf_op jit(solution)/shard_map/all_to_all | solution.py:251
  54.8 0.0 copy-done.9
  54.8 0.0 copy-done.14
  54.8 0.0 copy-start.3
  54.8 1.6 %copy-done.3 = bf16[64,128,128]{2,1,0:T(8,128)(2,1)S(1)} copy-done((bf16[64,128,128]{2,1,0:T(8,128)(2,1)S(1)}, bf16[64,128,128]{2,1,0:T(8,128)(2,1)}, u32[]{:S(2)}) %copy-start.3) | copy-done | bytes 2097176
  56.4 0.0 copy-start.8
  56.4 1.0 shard_map.97
  57.4 0.0 copy-start.4
  57.4 13.8 %all_to_all.51 = f32[32,8,128]{2,1,0:T(8,128)S(1)} all-to-all(f32[32,8,128]{2,1,0:T(8,128)S(1)} %bitcast.57), channel_id=1, replica_groups=mesh['row'=16,'col'=32] {'col'}, dimensions={0} | all-to-all | bytes 262144 | tf_op jit(solution)/shard_map/all_to_all | solution.py:251
  71.2 0.0 copy-done.10
  71.2 0.0 copy-done.12
  71.2 0.0 copy-done.1
  71.2 1.0 shard_map.98
  72.2 0.0 copy-start.11
  72.2 0.0 copy-start.13
  72.2 12.5 %all_to_all.52 = f32[16,8,128]{2,1,0:T(8,128)S(1)} all-to-all(f32[16,8,128]{2,1,0:T(8,128)S(1)} %bitcast.62), channel_id=1, replica_groups=mesh['row'=16,'col'=32] {'row'}, dimensions={0} | all-to-all | bytes 131072 | tf_op jit(solution)/shard_map/all_to_all | solution.py:251
  84.7 0.0 copy-done.8
  84.7 0.3 shard_map.99
  85.0 10.4 %all_to_all.53 = f32[16,8,128]{2,1,0:T(8,128)S(1)} all-to-all(f32[16,8,128]{2,1,0:T(8,128)S(1)} %bitcast.58), channel_id=1, replica_groups=mesh['row'=16,'col'=32] {'row'}, dimensions={0} | all-to-all | bytes 131072 | tf_op jit(solution)/shard_map/all_to_all | solution.py:251
  95.4 0.0 copy-done.4
  95.4 0.0 copy-start.16
  95.4 1.0 shard_map.100
  96.4 12.4 %all_to_all.54 = f32[32,8,128]{2,1,0:T(8,128)S(1)} all-to-all(f32[32,8,128]{2,1,0:T(8,128)S(1)} %bitcast.56), channel_id=1, replica_groups=mesh['row'=16,'col'=32] {'col'}, dimensions={0} | all-to-all | bytes 262144 | tf_op jit(solution)/shard_map/all_to_all | solution.py:251
  108.8 0.0 copy-done.11
  108.8 0.0 copy-done.13
  108.8 0.9 shard_map.101
  109.8 12.3 %all_to_all.55 = f32[16,8,128]{2,1,0:T(8,128)S(1)} all-to-all(f32[16,8,128]{2,1,0:T(8,128)S(1)} %bitcast.61), channel_id=1, replica_groups=mesh['row'=16,'col'=32] {'row'}, dimensions={0} | all-to-all | bytes 131072 | tf_op jit(solution)/shard_map/all_to_all | solution.py:251
  122.1 0.0 copy-done.16
  122.1 1.2 shard_map.102
  123.3 10.4 %all_to_all.56.got = f32[16,8,128]{2,1,0:T(8,128)S(1)} all-to-all(f32[16,8,128]{2,1,0:T(8,128)S(1)} %shard_map.102), channel_id=1, replica_groups=mesh['row'=16,'col'=32] {'row'}, dimensions={0} | all-to-all | bytes 131072 | tf_op jit(solution)/shard_map/all_to_all | solution.py:251
  133.7 0.7 shard_map.103
  134.4 3.8 %all-to-all-start.9 = ((f32[32,1,128]{2,1,0:T(1,128)}), f32[32,1,128]{2,1,0:T(1,128)S(1)}, u32[]{:S(2)}, u32[]{:S(2)}) async-start(f32[32,1,128]{2,1,0:T(1,128)} %bitcast.23), calls=%async_computation.9 | async-start | bytes 32768 | tf_op jit(solution)/shard_map/all_to_all | solution.py:251
  138.2 0.9 shard_map.104.refs_2_
  139.1 0.9 shard_map.105.refs_3_
  140.0 6.8 %all-to-all-done.9 = f32[32,1,128]{2,1,0:T(1,128)S(1)} async-done(((f32[32,1,128]{2,1,0:T(1,128)}), f32[32,1,128]{2,1,0:T(1,128)S(1)}, u32[]{:S(2)}, u32[]{:S(2)}) %all-to-all-start.9) | async-done | bytes 16416 | tf_op jit(solution)/shard_map/all_to_all | solution.py:251
  146.8 2.0 %shard_map.106 = (f32[3072,128]{1,0:T(8,128)}, f32[1]{0:T(128)}, f32[3]{0:T(128)}) custom-call(f32[32,128]{1,0:T(8,128)S(1)} %bitcast.63, f32[1536,128]{1,0:T(8,128)S(1)} %bitcast.36, f32[1536,128]{1,0:T(8,128)S(1)} %shard_map.104.refs_2_, f32[1536,128]{1,0:T(8,128)S(1)} %shard_map.105.refs_3_), custom_call_target="tpu_custom_call" | custom-call | tf_op jit(solution)/shard_map/pallas_call | solution.py:239
Async XLA Ops:
  21.0 33.8 %copy-start.9 = (bf16[256,64]{1,0:T(8,128)(2,1)S(1)}, bf16[256,64]{1,0:T(8,128)(2,1)}, u32[]{:S(2)}) copy-start(bf16[256,64]{1,0:T(8,128)(2,1)} %get-tuple-element.27.put) | copy-start | bytes 98308
  21.0 33.8 %copy-start.14 = (bf16[64,128]{1,0:T(8,128)(2,1)S(1)}, bf16[64,128]{1,0:T(8,128)(2,1)}, u32[]{:S(2)}) copy-start(bf16[64,128]{1,0:T(8,128)(2,1)} %get-tuple-element.25.pick) | copy-start | bytes 49156
  21.0 20.6 %all-to-all-start.1 = ((s32[32,8,128]{2,1,0:T(8,128)}), s32[32,8,128]{2,1,0:T(8,128)S(1)}, u32[]{:S(2)}, u32[]{:S(2)}) async-start(s32[32,8,128]{2,1,0:T(8,128)} %bitcast.64), calls=%async_computation.1 | async-start | bytes 262144 | tf_op jit(solution)/shard_map/all_to_all | solution.py:251
  32.4 1.6 %copy-start = (bf16[1,1,64,128,128]{4,3,2,1,0:T(8,128)(2,1)S(1)}, bf16[1,1,64,128,128]{4,3,2,1,0:T(8,128)(2,1)}, u32[]{:S(2)}) copy-start(bf16[1,1,64,128,128]{4,3,2,1,0:T(8,128)(2,1)} %param.8) | copy-start | bytes 6291460
  34.0 1.1 copy-start.5
  35.2 11.8 %copy-start.6 = (f32[196608]{0:T(1024)S(1)}, f32[196608]{0:T(1024)}, u32[]{:S(2)}) copy-start(f32[196608]{0:T(1024)} %param.7) | copy-start | bytes 2359300
  35.2 36.1 %copy-start.10 = (bf16[128,64]{1,0:T(8,128)(2,1)S(1)}, bf16[128,64]{1,0:T(8,128)(2,1)}, u32[]{:S(2)}) copy-start(bf16[128,64]{1,0:T(8,128)(2,1)} %get-tuple-element.29.put) | copy-start | bytes 49156
  35.2 36.1 %copy-start.12 = (bf16[64,256]{1,0:T(8,128)(2,1)S(1)}, bf16[64,256]{1,0:T(8,128)(2,1)}, u32[]{:S(2)}) copy-start(bf16[64,256]{1,0:T(8,128)(2,1)} %get-tuple-element.28.pick) | copy-start | bytes 98308
  36.4 1.3 copy-start.2
  37.8 0.6 copy-start.15
  38.4 32.9 %copy-start.1 = (bf16[1,1,64,128,128]{4,3,2,1,0:T(8,128)(2,1)S(1)}, bf16[1,1,64,128,128]{4,3,2,1,0:T(8,128)(2,1)}, u32[]{:S(2)}) copy-start(bf16[1,1,64,128,128]{4,3,2,1,0:T(8,128)(2,1)} %param.8) | copy-start | bytes 6291460
  41.6 13.2 %all-to-all-start.2 = ((f32[16,8,128]{2,1,0:T(8,128)}), f32[16,8,128]{2,1,0:T(8,128)S(1)}, u32[]{:S(2)}, u32[]{:S(2)}) async-start(f32[16,8,128]{2,1,0:T(8,128)} %bitcast.10), calls=%async_computation.2 | async-start | bytes 131072 | tf_op jit(solution)/shard_map/all_to_all | solution.py:251
  47.7 0.7 copy-start.7
  54.8 1.6 %copy-start.3 = (bf16[64,128,128]{2,1,0:T(8,128)(2,1)S(1)}, bf16[64,128,128]{2,1,0:T(8,128)(2,1)}, u32[]{:S(2)}) copy-start(bf16[64,128,128]{2,1,0:T(8,128)(2,1)} %copy-done.2) | copy-start | bytes 6291460
  56.4 28.3 %copy-start.8 = (bf16[384,384]{1,0:T(8,128)(2,1)S(1)}, bf16[384,384]{1,0:T(8,128)(2,1)}, u32[]{:S(2)}) copy-start(bf16[384,384]{1,0:T(8,128)(2,1)} %copy-done.7) | copy-start | bytes 884740
  57.4 38.0 %copy-start.4 = (bf16[64,128,128]{2,1,0:T(8,128)(2,1)S(1)}, bf16[64,128,128]{2,1,0:T(8,128)(2,1)}, u32[]{:S(2)}) copy-start(bf16[64,128,128]{2,1,0:T(8,128)(2,1)} %copy-done.2) | copy-start | bytes 6291460
  72.2 36.6 %copy-start.11 = (bf16[128,64]{1,0:T(8,128)(2,1)S(1)}, bf16[128,64]{1,0:T(8,128)(2,1)}, u32[]{:S(2)}) copy-start(bf16[128,64]{1,0:T(8,128)(2,1)} %get-tuple-element.29.put) | copy-start | bytes 49156
  72.2 36.6 %copy-start.13 = (bf16[64,256]{1,0:T(8,128)(2,1)S(1)}, bf16[64,256]{1,0:T(8,128)(2,1)}, u32[]{:S(2)}) copy-start(bf16[64,256]{1,0:T(8,128)(2,1)} %get-tuple-element.28.pick) | copy-start | bytes 98308
  95.4 26.7 %copy-start.16 = (f32[8,128]{1,0:T(8,128)S(1)}, f32[8,128]{1,0:T(8,128)}, u32[]{:S(2)}) copy-start(f32[8,128]{1,0:T(8,128)} %copy-done.15) | copy-start | bytes 12292
  134.4 12.4 %all-to-all-start.9 = ((f32[32,1,128]{2,1,0:T(1,128)}), f32[32,1,128]{2,1,0:T(1,128)S(1)}, u32[]{:S(2)}, u32[]{:S(2)}) async-start(f32[32,1,128]{2,1,0:T(1,128)} %bitcast.23), calls=%async_computation.9 | async-start | bytes 32768 | tf_op jit(solution)/shard_map/all_to_all | solution.py:251

commit v3 on v2

--- a/solution.py
+++ b/solution.py
@@ -1,3 +1,5 @@
+import functools
+
 import jax
 import jax.numpy as jnp
 from jax import lax
@@ -46,24 +48,17 @@
     return (owner * LANE + rank_row).astype(jnp.int32), (column * LANE + rank_column).astype(jnp.int32)
 
 
-def request_kernel(*refs):
-    far, outs, near, sems = refs[:5], refs[5:11], refs[11:16], refs[16]
-    copies = [pltpu.make_async_copy(a, b, sems.at[k]) for k, (a, b) in enumerate(zip(far, near))]
-    for copy in copies:
-        copy.start()
-    for copy in copies:
-        copy.wait()
-    own_r, blk_r, own_c, blk_c, filled = near
-    ask_row, ask_col, pick_row, put_row, pick_col, put_col = outs
+def request_kernel(pieces, slots, ask_row, ask_col, pick_row, put_row, pick_col, put_col, pick_pair, mine):
+    own_r, blk_r, own_c, blk_c, filled = [slots[k : k + 1, :] for k in range(5)]
     count = own_r.shape[1]
-    alive = iota((1, count), 1) < filled[...]
+    alive = iota((1, count), 1) < filled
     for owner, block, ask, pick, put, shift in (
         (own_c, blk_c, ask_row, pick_row, put_row, 0),
         (own_r, blk_r, ask_col, pick_col, put_col, HALF),
     ):
         width = ask.shape[0]
-        across, down = place_of(owner[...].astype(F32))
-        value = jnp.where(alive, block[...] + 1, 0).astype(F32)
+        across, down = place_of(owner.astype(F32))
+        value = jnp.where(alive, block + 1, 0).astype(F32)
         spot = iota((width, count), 0)
         there = spot == across
         back = spot == across + shift
@@ -71,6 +66,23 @@
         ask[...] = jnp.broadcast_to(wanted, (width, TILE)).astype(jnp.int32)
         pick[...] = jnp.where(iota((count, width), 1) == down, 1.0, 0.0).astype(BF16)
         put[...] = jnp.where(back, 1.0, 0.0).astype(BF16)
+    ident = jnp.where(alive, own_c * pieces + blk_c, -1)
+    width = ask_row.shape[0]
+    lane = iota((width, TILE), 1)
+    number = iota((width, TILE), 0) // LANE
+    ids = jnp.concatenate([ident, ident], axis=1)
+    ask_row[...] = jnp.where(lane >= count, ids, jnp.where(lane == count - 1, number, ask_row[...]))
+    across = iota((count, count), 0) == iota((count, count), 1)
+    down = jnp.sum(jnp.where(across, ident.astype(F32), 0.0), axis=1, keepdims=True).astype(jnp.int32)
+    mine[...] = jnp.broadcast_to(jnp.where(down < 0, -2, down), mine.shape)
+    place = place_of(own_c.astype(F32))[1]
+    high = place + place // LANE * LANE
+    lane = iota(pick_pair.shape, 1)
+    pick_pair[...] = jnp.where((lane == high) | (lane == high + LANE), 1.0, 0.0).astype(BF16)
+
+
+def first_lane(asked):
+    return jnp.broadcast_to(asked[:, 0:1], asked.shape)
 
 
 def gather(asked, vector):
@@ -85,14 +97,14 @@
 
 def gather_kernel(asked, vector, tiles, out, energy, turned):
     v = vector[...] * SCALE
-    out[...] = gather(asked[...], v)
+    out[...] = gather(first_lane(asked[...]), v)
     energy[...] = jnp.sum((v * v).reshape(-1, 8, TILE), axis=0)
     for t in range(tiles.shape[0]):
         turned[t] = tiles[t].T
 
 
 def product_lane(asked_row, asked_col):
-    rows = [asked_row[...].astype(F32).T[0:1, :]]
+    rows = [first_lane(asked_row[...]).astype(F32).T[0:1, :]]
     width = asked_col.shape[0]
     for k in range(width // TILE):
         part = asked_col[k * TILE : (k + 1) * TILE, :].astype(F32).T[0:1, :]
@@ -101,16 +113,27 @@
     return [row.astype(jnp.int32) for row in rows]
 
 
-def meet_kernel(asked_row, asked_col, vector, out, meet):
+def meet_kernel(asked_row, asked_col, mine, vector, out, meet, link, link_col):
     out[...] = gather(asked_col[...], vector[...] * SCALE)
     lanes = product_lane(asked_row, asked_col)
     base = 0
-    for asked in (asked_row, asked_col):
-        mine = asked[...]
+    served_row, served_col = first_lane(asked_row[...]), asked_col[...]
+    for served in (served_row, served_col):
         for k, lane in enumerate(lanes):
-            hit = (mine == lane) & (mine >= 0)
-            meet[base : base + mine.shape[0], k * TILE : (k + 1) * TILE] = jnp.where(hit, 1.0, 0.0).astype(BF16)
-        base += mine.shape[0]
+            hit = (served == lane) & (served >= 0)
+            meet[base : base + served.shape[0], k * TILE : (k + 1) * TILE] = jnp.where(hit, 1.0, 0.0).astype(BF16)
+        base += served.shape[0]
+    count = mine.shape[0]
+    index = asked_row[0:1, count - 1 : count]
+    ident = jnp.where(served_col < 0, -3, served_col + index * vector.shape[0])
+    lane = iota((1, TILE), 1)
+    for k in range(asked_row.shape[0] // (2 * LANE)):
+        even = asked_row[2 * k * LANE : 2 * k * LANE + 1, :]
+        odd = asked_row[(2 * k + 1) * LANE : (2 * k + 1) * LANE + 1, :]
+        ids = jnp.where(lane < count, pltpu.roll(even, count, 1), odd)
+        cols = slice(k * TILE, (k + 1) * TILE)
+        link[:, cols] = jnp.where(mine[...] == ids, 1.0, 0.0).astype(BF16)
+        link_col[:, cols] = jnp.where(ident == ids, 1.0, 0.0).astype(BF16)
 
 
 def multiply(x, tiles):
@@ -135,27 +158,53 @@
     out[...] = exact_dot(put[...], y) + jnp.where(forward, extra[...], 0.0)
 
 
-def mirror_kernel(got, pick, tiles, put, out):
+def mirror_kernel(got, pick, tiles, put, meet, out, first):
     y = multiply(exact_dot(pick[...], got[...]), tiles)
-    out[...] = exact_dot(put[...], y)
-
-
-def sum_kernel(meet, back_row, back_col, out_row, out_col):
-    total = exact_dot(meet[...], jnp.concatenate([back_row[...], back_col[...]], axis=0))
-    width = out_row.shape[0]
-    out_row[...] = total[:width]
-    out_col[...] = total[width:]
-
-
-def inner_kernel(
-    meet, energy, v_row, v_col, i_row, i_col, first_row, first_col, second_row, second_col, out
-):
-    total = exact_dot(meet[...], jnp.concatenate([second_row[...], second_col[...]], axis=0))
+    first[...] = exact_dot(put[...], y)
+    width = first.shape[0]
+    total = exact_dot(meet[:width, width:], got[...])
+    high = total.astype(BF16).astype(F32)
+    low = total - high
+    count = y.shape[0]
+    narrow = y.astype(BF16)
+    for k in range(out.shape[0]):
+        rows = slice(k * LANE, (k + 1) * LANE)
+        out[k, :count, :] = narrow
+        out[k, count:, :] = jnp.concatenate([high[rows], low[rows]], axis=0).astype(BF16)
+
+
+def second_direct_kernel(got, link, link_col, pick, meet, first_col, turned, put, out):
+    count = link.shape[0]
+    peers = range(got.shape[0])
+    mirrors = jnp.concatenate([got[k, :count, :] for k in peers], axis=0)
+    sums = jnp.concatenate([got[k, count:, :] for k in peers], axis=0)
+    y = multiply(dot(link[...], mirrors) + dot(pick[...], sums), turned)
+    width = got.shape[0] * LANE
+    image = dot(link_col[...], mirrors) + exact_dot(meet[width:, width:], first_col[...])
+    forward = iota(image.shape, 0) % LANE < HALF
+    out[...] = exact_dot(put[...], y) + jnp.where(forward, image, 0.0)
+
+
+def second_mirror_kernel(got, pick, tiles, put, first, out):
+    y = exact_dot(put[...], multiply(exact_dot(pick[...], got[...]), tiles))
+    out[:, :LANE, :] = y.reshape(-1, LANE, TILE)
+    out[:, LANE:, :] = first[...].reshape(-1, LANE, TILE)
+
+
+def split_rows(got):
+    return got[:, LANE:, :].reshape(-1, TILE), got[:, :LANE, :].reshape(-1, TILE)
+
+
+def inner_kernel(meet, energy, v_row, v_col, got, first_col, second_col, out):
+    first_r, second_r = split_rows(got[...])
+    first = jnp.concatenate([first_r, first_col[...]], axis=0)
+    second = jnp.concatenate([second_r, second_col[...]], axis=0)
+    both = exact_dot(meet[...], jnp.concatenate([first, second], axis=1))
+    image, total = both[:, :TILE], both[:, TILE:]
     width = v_row.shape[0]
     returned = iota(v_col.shape, 0) % LANE >= HALF
     first_c = jnp.where(returned, first_col[...], 0.0)
     second_c = jnp.where(returned, second_col[...], 0.0)
-    first_r, second_r = first_row[...], second_row[...]
 
     def inner(a_r, b_r, a_c, b_c):
         return jnp.sum(a_r * b_r, axis=0, keepdims=True) + jnp.sum(a_c * b_c, axis=0, keepdims=True)
@@ -163,9 +212,9 @@
     values = [
         jnp.sum(energy[...], axis=0, keepdims=True),
         inner(v_row[...], first_r, v_col[...], first_c),
-        inner(i_row[...], first_r, i_col[...], first_c),
+        inner(image[:width], first_r, image[width:], first_c),
         inner(v_row[...], second_r, v_col[...], second_c),
-        inner(i_row[...], second_r, i_col[...], second_c),
+        inner(image[:width], second_r, image[width:], second_c),
         inner(total[:width], second_r, total[width:], second_c),
     ]
     packed = jnp.concatenate(values + [jnp.zeros((2, TILE), F32)], axis=0)
@@ -180,9 +229,9 @@
     out[...] = jnp.broadcast_to(packed, out.shape)
 
 
-def spread_kernel(asked_row, asked_col, back_row, back_col, out):
+def spread_kernel(which, asked_row, asked_col, got, back_col, out):
     lanes = jnp.concatenate(product_lane(asked_row, asked_col), axis=1)
-    high, low = halves(jnp.concatenate([back_row[...], back_col[...]], axis=0))
+    high, low = halves(jnp.concatenate([split_rows(got[...])[which], back_col[...]], axis=0))
     step = 256
     for start in range(0, out.shape[0], step):
         place = iota((step, lanes.shape[1]), 0) + start
@@ -233,7 +282,7 @@
     return jax.ShapeDtypeStruct(dims, dtype)
 
 
-def call(kernel, outs, *args, ins=VMEM, out_specs=VMEM, scratch=(), limit=32):
+def call(kernel, outs, *args, ins=VMEM, out_specs=VMEM, scratch=(), limit=16):
     if isinstance(outs, tuple) and not isinstance(out_specs, tuple):
         out_specs = tuple([out_specs] * len(outs))
     return pl.pallas_call(
@@ -268,8 +317,13 @@
     def over_col(x):
         return exchange(x, "col", n_col)
 
-    ask_row, ask_col, pick_row, put_row, pick_col, put_col = call(
-        request_kernel,
+    slots = jnp.concatenate(
+        [x.reshape(1, count) for x in (row_owner, row_block, col_owner, col_block)]
+        + [jnp.broadcast_to(tile_counts.reshape(1, 1), (1, count))],
+        axis=0,
+    )
+    ask_row, ask_col, pick_row, put_row, pick_col, put_col, pick_pair, mine = call(
+        functools.partial(request_kernel, pieces),
         (
             shape(wide_r, TILE, dtype=jnp.int32),
             shape(wide_c, TILE, dtype=jnp.int32),
@@ -277,16 +331,10 @@
             shape(wide_r, count, dtype=BF16),
             shape(count, wide_c, dtype=BF16),
             shape(wide_c, count, dtype=BF16),
+            shape(count, 2 * wide_r, dtype=BF16),
+            shape(count, TILE, dtype=jnp.int32),
         ),
-        row_owner.reshape(1, count),
-        row_block.reshape(1, count),
-        col_owner.reshape(1, count),
-        col_block.reshape(1, count),
-        tile_counts.reshape(1, 1),
-        ins=HBM,
-        limit=63,
-        scratch=[pltpu.VMEM((1, count), jnp.int32)] * 4
-        + [pltpu.VMEM((1, 1), jnp.int32), pltpu.SemaphoreType.DMA((5,))],
+        slots,
     )
     asked_row = over_row(ask_row)
     asked_col = over_col(ask_col)
@@ -298,16 +346,46 @@
         tiles,
     )
     x_col = over_row(v_row)
-    v_col, meet = call(
-        meet_kernel, (shape(wide_c, TILE), shape(every, every, dtype=BF16)), asked_row, asked_col, vector
+    v_col, meet, link, link_col = call(
+        meet_kernel,
+        (
+            shape(wide_c, TILE),
+            shape(every, every, dtype=BF16),
+            shape(count, n_row * count, dtype=BF16),
+            shape(wide_c, n_row * count, dtype=BF16),
+        ),
+        asked_row,
+        asked_col,
+        mine,
+        vector,
     )
     first_col = over_col(call(direct_kernel, shape(wide_c, TILE), x_col, pick_row, turned, put_col, v_col))
-    first_row = over_row(call(mirror_kernel, shape(wide_r, TILE), first_col, pick_col, tiles, put_row))
-    i_row, i_col = call(sum_kernel, (shape(wide_r, TILE), shape(wide_c, TILE)), meet, first_row, first_col)
-    x_col = over_row(i_row)
-    image = call(spread_kernel, shape(pieces, TILE), asked_row, asked_col, first_row, first_col)
-    second_col = over_col(call(direct_kernel, shape(wide_c, TILE), x_col, pick_row, turned, put_col, i_col))
-    second_row = over_row(call(mirror_kernel, shape(wide_r, TILE), second_col, pick_col, tiles, put_row))
+    packed, first = call(
+        mirror_kernel,
+        (shape(n_row, count + 2 * LANE, TILE, dtype=BF16), shape(wide_r, TILE)),
+        first_col,
+        pick_col,
+        tiles,
+        put_row,
+        meet,
+    )
+    second_col = call(
+        second_direct_kernel,
+        shape(wide_c, TILE),
+        over_row(packed),
+        link,
+        link_col,
+        pick_pair,
+        meet,
+        first_col,
+        turned,
+        put_col,
+    )
+    second_col = over_col(second_col)
+    back = call(
+        second_mirror_kernel, shape(n_row, 2 * LANE, TILE), second_col, pick_col, tiles, put_row, first
+    )
+    back = over_row(back)
     inner = call(
         inner_kernel,
         shape(n_row, 8, TILE),
@@ -315,15 +393,15 @@
         energy,
         v_row,
         v_col,
-        i_row,
-        i_col,
-        first_row,
+        back,
         first_col,
-        second_row,
         second_col,
     )
     inner = over_row(inner)
-    second = call(spread_kernel, shape(pieces, TILE), asked_row, asked_col, second_row, second_col)
+    image, second = [
+        call(functools.partial(spread_kernel, k), shape(pieces, TILE), asked_row, asked_col, back, column)
+        for k, column in enumerate((first_col, second_col))
+    ]
     inner = over_col(call(partial_kernel, shape(n_col, TILE), inner))
 
     def finish(*refs):

time: 150 us -> 149 us (level)
  local copies, waits for them, and re-layouts: 6.98 us -> 12.2 us
  blocking collectives: 89.8 us -> 85 us
  waiting for transfers between devices: 16.4 us -> 14 us
    all_to_all x7 -> x6, blocking collectives: 89.8 us -> 85 us  [exchange(): got = lax.all_to_all(sent, axis, split_axis=0, concat_axis=0, tiled=True)]
    unnamed x34 -> x52, local copies, waits for them, and re-layouts: 6.98 us -> 11.4 us
    all_to_all x3, waiting for transfers between devices: 16.4 us -> 14 us  [exchange(): got = lax.all_to_all(sent, axis, split_axis=0, concat_axis=0, tiled=True)]
    pallas_call x13 -> x12, Pallas kernels: 13.4 us -> 13.5 us  [call(): pl.pallas_call(kernel, out_shape=outs, in_specs=[ins] * len(args), out_sp...]
  transfers between devices with their start and end apart: 3 -> 3, of which waited for: 3 -> 3; matrix products, arithmetic and copies ran while one was open for 0% -> 0% of each run, Pallas kernels for 2% -> 3%
where the time goes in v3:
time: 149 us; the launch traced here: 148 us
  blocking collectives  85 us (57%)
  starting transfers between devices  21.8 us (15%)
  waiting for transfers between devices  14 us (9%)
  Pallas kernels  13.5 us (9%)
  local copies, waits for them, and re-layouts  12.2 us (8%)
  between operations  1.51 us (1%)
    all_to_all x6, blocking collectives, exchange(): got = lax.all_to_all(sent, axis, split_axis=0, concat_axis=0, tiled=True)  85 us
    all_to_all x3, starting transfers between devices, exchange(): got = lax.all_to_all(sent, axis, split_axis=0, concat_axis=0, tiled=True)  21.8 us
    all_to_all x3, waiting for transfers between devices, exchange(): got = lax.all_to_all(sent, axis, split_axis=0, concat_axis=0, tiled=True)  14 us
    pallas_call x12, Pallas kernels, call(): pl.pallas_call(kernel, out_shape=outs, in_specs=[ins] * len(args), out_sp...  13.5 us
    unnamed x52, local copies, waits for them, and re-layouts  11.4 us
  transfers between devices with their start and end apart: 3, of which 3 were waited for; matrix products, arithmetic and copies ran while one was open for 0% of the time, Pallas kernels for 3%

profile of v3, /device:TPU:1, one launch (start us, length us, event | category | flops | bytes accessed | tf_op | source)
XLA Modules:
  0.0 148.0 jit_solution(741325327711741565)
XLA Ops:
  1.3 0.7 concatenate.3.slots
  2.0 0.9 shard_map.94
  2.9 0.6 copy-done.13
  3.5 0.0 copy-start.16
  3.5 0.6 copy-done.16
  4.1 0.0 copy-start.20
  4.1 17.1 %all_to_all.45 = s32[16,8,128]{2,1,0:T(8,128)S(1)} all-to-all(s32[16,8,128]{2,1,0:T(8,128)S(1)} %bitcast.50), channel_id=1, replica_groups=mesh['row'=16,'col'=32] {'row'}, dimensions={0} | all-to-all | bytes 131072 | tf_op jit(solution)/shard_map/all_to_all | solution.py:300
  21.3 0.0 copy-done.20
  21.3 0.0 copy-done.22
  21.3 12.0 %all-to-all-start.1 = ((s32[32,8,128]{2,1,0:T(8,128)}), s32[32,8,128]{2,1,0:T(8,128)S(1)}, u32[]{:S(2)}, u32[]{:S(2)}) async-start(s32[32,8,128]{2,1,0:T(8,128)} %bitcast.7), calls=%async_computation.1 | async-start | bytes 262144 | tf_op jit(solution)/shard_map/all_to_all | solution.py:300
  33.3 0.0 copy-start
  33.3 1.6 %copy-done = bf16[1,1,64,128,128]{4,3,2,1,0:T(8,128)(2,1)S(1)} copy-done((bf16[1,1,64,128,128]{4,3,2,1,0:T(8,128)(2,1)S(1)}, bf16[1,1,64,128,128]{4,3,2,1,0:T(8,128)(2,1)}, u32[]{:S(2)}) %copy-start) | copy-done | bytes 2097176
  34.9 1.1 copy-done.5
  36.0 1.2 shard_map.96
  37.2 1.3 copy-done.2
  38.5 0.6 copy-done.24
  39.1 3.3 %all-to-all-done.1 = s32[32,8,128]{2,1,0:T(8,128)S(1)} async-done(((s32[32,8,128]{2,1,0:T(8,128)}), s32[32,8,128]{2,1,0:T(8,128)S(1)}, u32[]{:S(2)}, u32[]{:S(2)}) %all-to-all-start.1) | async-done | bytes 131104 | tf_op jit(solution)/shard_map/all_to_all | solution.py:300
  42.4 6.0 %all-to-all-start.2 = ((f32[16,8,128]{2,1,0:T(8,128)}), f32[16,8,128]{2,1,0:T(8,128)}, u32[]{:S(2)}, u32[]{:S(2)}) async-start(f32[16,8,128]{2,1,0:T(8,128)} %bitcast.11), calls=%async_computation.2 | async-start | bytes 131072 | tf_op jit(solution)/shard_map/all_to_all | solution.py:300
  48.4 0.0 copy-done.6
  48.4 0.0 copy-start.23
  48.4 0.7 copy-done.23
  49.1 0.8 shard_map.95
  50.0 0.0 copy-start.9
  50.0 0.8 copy-done.9
  50.8 0.6 copy-done.18
  51.4 4.9 %all-to-all-done.2 = f32[16,8,128]{2,1,0:T(8,128)} async-done(((f32[16,8,128]{2,1,0:T(8,128)}), f32[16,8,128]{2,1,0:T(8,128)}, u32[]{:S(2)}, u32[]{:S(2)}) %all-to-all-start.2) | async-done | bytes 65568 | tf_op jit(solution)/shard_map/all_to_all | solution.py:300
  56.3 1.6 %copy-done.3 = bf16[64,128,128]{2,1,0:T(8,128)(2,1)S(1)} copy-done((bf16[64,128,128]{2,1,0:T(8,128)(2,1)S(1)}, bf16[64,128,128]{2,1,0:T(8,128)(2,1)}, u32[]{:S(2)}) %copy-start.3) | copy-done | bytes 2097176
  57.9 0.8 copy-done.14
  58.7 1.8 %shard_map.97 = f32[256,128]{1,0:T(8,128)S(1)} custom-call(f32[128,128]{1,0:T(8,128)} %bitcast.12.got, bf16[64,128]{1,0:T(8,128)(2,1)S(1)} %get-tuple-element.30.pick, bf16[64,128,128]{2,1,0:T(8,128)(2,1)S(1)} %copy-done.3, bf16[256,64]{1,0:T(8,128)(2,1)S(1)} %copy-done.14, f32[256,128]{1,0:T(8,128)S(1)} %get-tuple-element.29.extra.v_col), custom_call_target="tpu_custom_call" | custom-call | tf_op jit(solution)/shard_map/pallas_call | solution.py:288
  60.6 0.0 copy-done.11
  60.6 0.0 copy-start.4
  60.6 0.0 copy-start.10
  60.6 0.0 copy-start.15
  60.6 0.0 copy-start.19
  60.6 0.0 copy-start.21
  60.6 13.9 %all_to_all.46 = f32[32,8,128]{2,1,0:T(8,128)S(1)} all-to-all(f32[32,8,128]{2,1,0:T(8,128)S(1)} %bitcast.48), channel_id=1, replica_groups=mesh['row'=16,'col'=32] {'col'}, dimensions={0} | all-to-all | bytes 262144 | tf_op jit(solution)/shard_map/all_to_all | solution.py:300
  74.5 0.0 copy-done.1
  74.5 0.0 copy-done.17
  74.5 1.0 shard_map.98
  75.5 17.6 %all_to_all.47.got = bf16[16,80,128]{2,1,0:T(8,128)(2,1)S(1)} all-to-all(bf16[16,80,128]{2,1,0:T(8,128)(2,1)S(1)} %get-tuple-element.35), channel_id=1, replica_groups=mesh['row'=16,'col'=32] {'row'}, dimensions={0} | all-to-all | bytes 655360 | tf_op jit(solution)/shard_map/all_to_all | solution.py:300
  93.1 0.0 copy-done.4
  93.1 0.0 copy-done.10
  93.1 0.0 copy-done.15
  93.1 0.0 copy-done.19
  93.1 0.0 copy-done.21
  93.1 1.1 shard_map.99
  94.2 0.0 copy-start.12
  94.2 0.0 copy-start.25
  94.3 13.0 %all_to_all.48 = f32[32,8,128]{2,1,0:T(8,128)S(1)} all-to-all(f32[32,8,128]{2,1,0:T(8,128)S(1)} %bitcast.47), channel_id=1, replica_groups=mesh['row'=16,'col'=32] {'col'}, dimensions={0} | all-to-all | bytes 262144 | tf_op jit(solution)/shard_map/all_to_all | solution.py:300
  107.3 0.9 shard_map.100
  108.2 13.2 %all_to_all.49.got = f32[16,16,128]{2,1,0:T(8,128)S(1)} all-to-all(f32[16,16,128]{2,1,0:T(8,128)S(1)} %shard_map.100), channel_id=1, replica_groups=mesh['row'=16,'col'=32] {'row'}, dimensions={0} | all-to-all | bytes 262144 | tf_op jit(solution)/shard_map/all_to_all | solution.py:300
  121.4 0.0 copy-done.12
  121.4 0.0 copy-done.25
  121.4 1.2 shard_map.101
  122.7 0.0 copy-done.7
  122.7 10.2 %all_to_all.50.got = f32[16,8,128]{2,1,0:T(8,128)S(1)} all-to-all(f32[16,8,128]{2,1,0:T(8,128)S(1)} %shard_map.101), channel_id=1, replica_groups=mesh['row'=16,'col'=32] {'row'}, dimensions={0} | all-to-all | bytes 131072 | tf_op jit(solution)/shard_map/all_to_all | solution.py:300
  132.9 0.7 shard_map.102
  133.6 3.8 %all-to-all-start.8 = ((f32[32,1,128]{2,1,0:T(1,128)}), f32[32,1,128]{2,1,0:T(1,128)S(1)}, u32[]{:S(2)}, u32[]{:S(2)}) async-start(f32[32,1,128]{2,1,0:T(1,128)} %bitcast.18), calls=%async_computation.8 | async-start | bytes 32768 | tf_op jit(solution)/shard_map/all_to_all | solution.py:300
  137.5 0.0 copy-start.8
  137.5 0.9 copy-done.8
  138.4 0.9 shard_map.104.refs_3_
  139.3 0.9 shard_map.103.refs_2_
  140.2 5.9 %all-to-all-done.8 = f32[32,1,128]{2,1,0:T(1,128)S(1)} async-done(((f32[32,1,128]{2,1,0:T(1,128)}), f32[32,1,128]{2,1,0:T(1,128)S(1)}, u32[]{:S(2)}, u32[]{:S(2)}) %all-to-all-start.8) | async-done | bytes 16416 | tf_op jit(solution)/shard_map/all_to_all | solution.py:300
  146.1 2.0 %shard_map.105 = (f32[3072,128]{1,0:T(8,128)}, f32[1]{0:T(128)}, f32[3]{0:T(128)}) custom-call(f32[32,128]{1,0:T(8,128)S(1)} %bitcast.49, f32[1536,128]{1,0:T(8,128)S(1)} %bitcast.32, f32[1536,128]{1,0:T(8,128)S(1)} %shard_map.103.refs_2_, f32[1536,128]{1,0:T(8,128)S(1)} %shard_map.104.refs_3_), custom_call_target="tpu_custom_call" | custom-call | tf_op jit(solution)/shard_map/pallas_call | solution.py:288
  (14 shorter events, 0.0 us)
Async XLA Ops:
  2.9 0.6 copy-start.13
  3.5 0.6 copy-start.16
  4.1 17.1 %copy-start.20 = (bf16[64,256]{1,0:T(8,128)(2,1)}, bf16[64,256]{1,0:T(8,128)(2,1)S(1)}, u32[]{:S(2)}) copy-start(bf16[64,256]{1,0:T(8,128)(2,1)S(1)} %get-tuple-element.38.pick) | copy-start | bytes 98308
  4.1 17.1 %copy-start.22 = (s32[64,128]{1,0:T(8,128)}, s32[64,128]{1,0:T(8,128)S(1)}, u32[]{:S(2)}) copy-start(s32[64,128]{1,0:T(8,128)S(1)} %get-tuple-element.25.mine) | copy-start | bytes 98308
  21.3 21.1 %all-to-all-start.1 = ((s32[32,8,128]{2,1,0:T(8,128)}), s32[32,8,128]{2,1,0:T(8,128)S(1)}, u32[]{:S(2)}, u32[]{:S(2)}) async-start(s32[32,8,128]{2,1,0:T(8,128)} %bitcast.7), calls=%async_computation.1 | async-start | bytes 262144 | tf_op jit(solution)/shard_map/all_to_all | solution.py:300
  33.3 1.6 %copy-start = (bf16[1,1,64,128,128]{4,3,2,1,0:T(8,128)(2,1)S(1)}, bf16[1,1,64,128,128]{4,3,2,1,0:T(8,128)(2,1)}, u32[]{:S(2)}) copy-start(bf16[1,1,64,128,128]{4,3,2,1,0:T(8,128)(2,1)} %param.8) | copy-start | bytes 6291460
  34.8 1.1 copy-start.5
  36.0 12.4 %copy-start.6 = (f32[196608]{0:T(1024)S(1)}, f32[196608]{0:T(1024)}, u32[]{:S(2)}) copy-start(f32[196608]{0:T(1024)} %param.7) | copy-start | bytes 2359300
  37.2 1.3 copy-start.2
  38.5 0.6 copy-start.24
  39.1 35.4 %copy-start.1 = (bf16[1,1,64,128,128]{4,3,2,1,0:T(8,128)(2,1)S(1)}, bf16[1,1,64,128,128]{4,3,2,1,0:T(8,128)(2,1)}, u32[]{:S(2)}) copy-start(bf16[1,1,64,128,128]{4,3,2,1,0:T(8,128)(2,1)} %param.8) | copy-start | bytes 6291460
  42.4 13.9 %all-to-all-start.2 = ((f32[16,8,128]{2,1,0:T(8,128)}), f32[16,8,128]{2,1,0:T(8,128)}, u32[]{:S(2)}, u32[]{:S(2)}) async-start(f32[16,8,128]{2,1,0:T(8,128)} %bitcast.11), calls=%async_computation.2 | async-start | bytes 131072 | tf_op jit(solution)/shard_map/all_to_all | solution.py:300
  48.4 0.8 copy-start.23
  50.0 0.8 copy-start.9
  50.8 0.6 copy-start.18
  51.4 9.2 %copy-start.11 = (f32[256,128]{1,0:T(8,128)}, f32[256,128]{1,0:T(8,128)S(1)}, u32[]{:S(2)}) copy-start(f32[256,128]{1,0:T(8,128)S(1)} %get-tuple-element.29.extra.v_col) | copy-start | bytes 393220
  56.3 1.6 %copy-start.3 = (bf16[64,128,128]{2,1,0:T(8,128)(2,1)S(1)}, bf16[64,128,128]{2,1,0:T(8,128)(2,1)}, u32[]{:S(2)}) copy-start(bf16[64,128,128]{2,1,0:T(8,128)(2,1)} %copy-done.2) | copy-start | bytes 6291460
  57.9 0.8 copy-start.14
  58.7 15.8 %copy-start.17 = (bf16[64,256]{1,0:T(8,128)(2,1)S(1)}, bf16[64,256]{1,0:T(8,128)(2,1)}, u32[]{:S(2)}) copy-start(bf16[64,256]{1,0:T(8,128)(2,1)} %copy-done.16) | copy-start | bytes 98308
  60.6 32.5 %copy-start.4 = (bf16[64,128,128]{2,1,0:T(8,128)(2,1)S(1)}, bf16[64,128,128]{2,1,0:T(8,128)(2,1)}, u32[]{:S(2)}) copy-start(bf16[64,128,128]{2,1,0:T(8,128)(2,1)} %copy-done.2) | copy-start | bytes 6291460
  60.6 32.5 %copy-start.10 = (bf16[256,1024]{1,0:T(8,128)(2,1)S(1)}, bf16[256,1024]{1,0:T(8,128)(2,1)}, u32[]{:S(2)}) copy-start(bf16[256,1024]{1,0:T(8,128)(2,1)} %copy-done.9) | copy-start | bytes 1572868
  60.6 32.5 %copy-start.15 = (bf16[256,64]{1,0:T(8,128)(2,1)S(1)}, bf16[256,64]{1,0:T(8,128)(2,1)}, u32[]{:S(2)}) copy-start(bf16[256,64]{1,0:T(8,128)(2,1)} %copy-done.13) | copy-start | bytes 98308
  60.6 32.5 %copy-start.19 = (bf16[64,1024]{1,0:T(8,128)(2,1)S(1)}, bf16[64,1024]{1,0:T(8,128)(2,1)}, u32[]{:S(2)}) copy-start(bf16[64,1024]{1,0:T(8,128)(2,1)} %copy-done.18) | copy-start | bytes 393220
  60.6 32.5 %copy-start.21 = (bf16[64,256]{1,0:T(8,128)(2,1)S(1)}, bf16[64,256]{1,0:T(8,128)(2,1)}, u32[]{:S(2)}) copy-start(bf16[64,256]{1,0:T(8,128)(2,1)} %copy-done.20) | copy-start | bytes 98308
  94.2 27.2 %copy-start.12 = (f32[256,128]{1,0:T(8,128)S(1)}, f32[256,128]{1,0:T(8,128)}, u32[]{:S(2)}) copy-start(f32[256,128]{1,0:T(8,128)} %copy-done.11) | copy-start | bytes 393220
  94.2 27.2 %copy-start.25 = (f32[8,128]{1,0:T(8,128)S(1)}, f32[8,128]{1,0:T(8,128)}, u32[]{:S(2)}) copy-start(f32[8,128]{1,0:T(8,128)} %copy-done.24) | copy-start | bytes 12292
  107.3 15.4 %copy-start.7 = (f32[32,8,128]{2,1,0:T(8,128)}, f32[32,8,128]{2,1,0:T(8,128)S(1)}, u32[]{:S(2)}) copy-start(f32[32,8,128]{2,1,0:T(8,128)S(1)} %all_to_all.48) | copy-start | bytes 393220
  133.6 12.5 %all-to-all-start.8 = ((f32[32,1,128]{2,1,0:T(1,128)}), f32[32,1,128]{2,1,0:T(1,128)S(1)}, u32[]{:S(2)}, u32[]{:S(2)}) async-start(f32[32,1,128]{2,1,0:T(1,128)} %bitcast.18), calls=%async_computation.8 | async-start | bytes 32768 | tf_op jit(solution)/shard_map/all_to_all | solution.py:300
  137.5 0.9 copy-start.8

commit v4 on v3

--- a/solution.py
+++ b/solution.py
@@ -70,7 +70,10 @@
     width = ask_row.shape[0]
     lane = iota((width, TILE), 1)
     number = iota((width, TILE), 0) // LANE
+    spot = place_of(own_c.astype(F32))[0]
     ids = jnp.concatenate([ident, ident], axis=1)
+    spots = jnp.concatenate([spot, spot], axis=1)
+    ids = jnp.where(iota((width, TILE), 0) % 2 == 0, ids, spots)
     ask_row[...] = jnp.where(lane >= count, ids, jnp.where(lane == count - 1, number, ask_row[...]))
     across = iota((count, count), 0) == iota((count, count), 1)
     down = jnp.sum(jnp.where(across, ident.astype(F32), 0.0), axis=1, keepdims=True).astype(jnp.int32)
@@ -78,7 +81,7 @@
     place = place_of(own_c.astype(F32))[1]
     high = place + place // LANE * LANE
     lane = iota(pick_pair.shape, 1)
-    pick_pair[...] = jnp.where((lane == high) | (lane == high + LANE), 1.0, 0.0).astype(BF16)
+    pick_pair[...] = jnp.where(lane == high, 1.0, 0.0).astype(BF16)
 
 
 def first_lane(asked):
@@ -95,12 +98,10 @@
     return exact_dot(select, vector)
 
 
-def gather_kernel(asked, vector, tiles, out, energy, turned):
+def gather_kernel(asked, vector, out, energy):
     v = vector[...] * SCALE
     out[...] = gather(first_lane(asked[...]), v)
     energy[...] = jnp.sum((v * v).reshape(-1, 8, TILE), axis=0)
-    for t in range(tiles.shape[0]):
-        turned[t] = tiles[t].T
 
 
 def product_lane(asked_row, asked_col):
@@ -113,8 +114,7 @@
     return [row.astype(jnp.int32) for row in rows]
 
 
-def meet_kernel(asked_row, asked_col, mine, vector, out, meet, link, link_col):
-    out[...] = gather(asked_col[...], vector[...] * SCALE)
+def meet_tables(asked_row, asked_col, mine, pieces, meet, link, link_col, owned):
     lanes = product_lane(asked_row, asked_col)
     base = 0
     served_row, served_col = first_lane(asked_row[...]), asked_col[...]
@@ -125,19 +125,25 @@
         base += served.shape[0]
     count = mine.shape[0]
     index = asked_row[0:1, count - 1 : count]
-    ident = jnp.where(served_col < 0, -3, served_col + index * vector.shape[0])
+    ident = jnp.where(served_col < 0, -3, served_col + index * pieces)
     lane = iota((1, TILE), 1)
+    slot = iota(owned.shape[:1] + (TILE,), 0)
+    half = iota(owned.shape[:1] + (TILE,), 1) // count
     for k in range(asked_row.shape[0] // (2 * LANE)):
-        even = asked_row[2 * k * LANE : 2 * k * LANE + 1, :]
-        odd = asked_row[(2 * k + 1) * LANE : (2 * k + 1) * LANE + 1, :]
-        ids = jnp.where(lane < count, pltpu.roll(even, count, 1), odd)
+        start = 2 * k * LANE
+        even = [asked_row[start + j : start + j + 1, :] for j in range(2)]
+        odd = [asked_row[start + LANE + j : start + LANE + j + 1, :] for j in range(2)]
+        ids, spots = [jnp.where(lane < count, pltpu.roll(a, count, 1), b) for a, b in zip(even, odd)]
         cols = slice(k * TILE, (k + 1) * TILE)
         link[:, cols] = jnp.where(mine[...] == ids, 1.0, 0.0).astype(BF16)
         link_col[:, cols] = jnp.where(ident == ids, 1.0, 0.0).astype(BF16)
-
-
-def multiply(x, tiles):
+        sent = (spots == index * LANE + slot % LANE) & (slot // LANE == 2 * k + half)
+        owned[:, cols] = jnp.where(sent, 1.0, 0.0).astype(BF16)
+
+
+def multiply(x, tiles, across):
     count = x.shape[0]
+    dims = (((1,), (1 if across else 0,)), ((), ()))
     row = iota((8, TILE), 0)
     groups = []
     for g in range(count // 8):
@@ -146,57 +152,57 @@
         both = jnp.concatenate([high, part - high], axis=0).astype(BF16)
         total = jnp.zeros((8, TILE), F32)
         for j in range(8):
-            y = dot(both, tiles[g * 8 + j])
+            y = lax.dot_general(both, tiles[g * 8 + j], dims, preferred_element_type=F32)
             total = jnp.where(row == j, y[0:8] + y[8:16], total)
         groups.append(total)
     return jnp.concatenate(groups, axis=0)
 
 
-def direct_kernel(got, pick, turned, put, extra, out):
-    y = multiply(exact_dot(pick[...], got[...]), turned)
-    forward = iota(extra.shape, 0) % LANE < HALF
-    out[...] = exact_dot(put[...], y) + jnp.where(forward, extra[...], 0.0)
-
-
-def mirror_kernel(got, pick, tiles, put, meet, out, first):
-    y = multiply(exact_dot(pick[...], got[...]), tiles)
-    first[...] = exact_dot(put[...], y)
-    width = first.shape[0]
+def direct_kernel(
+    got, pick, tiles, put, asked_row, asked_col, mine, vector, out, v_col, meet, link, link_col, owned
+):
+    y = multiply(exact_dot(pick[...], got[...]), tiles, True)
+    v = gather(asked_col[...], vector[...] * SCALE)
+    v_col[...] = v
+    forward = iota(v.shape, 0) % LANE < HALF
+    out[...] = exact_dot(put[...], y) + jnp.where(forward, v, 0.0)
+    meet_tables(asked_row, asked_col, mine, vector.shape[0], meet, link, link_col, owned)
+
+
+def mirror_kernel(got, pick, tiles, put, meet, out):
+    y = multiply(exact_dot(pick[...], got[...]), tiles, False)
+    high, low = halves(y)
+    width = put.shape[0]
     total = exact_dot(meet[:width, width:], got[...])
-    high = total.astype(BF16).astype(F32)
-    low = total - high
+    low = dot(put[...], low)
     count = y.shape[0]
-    narrow = y.astype(BF16)
     for k in range(out.shape[0]):
         rows = slice(k * LANE, (k + 1) * LANE)
-        out[k, :count, :] = narrow
-        out[k, count:, :] = jnp.concatenate([high[rows], low[rows]], axis=0).astype(BF16)
-
-
-def second_direct_kernel(got, link, link_col, pick, meet, first_col, turned, put, out):
+        out[k, :count, :] = high
+        out[k, count:, :] = jnp.concatenate([total[rows], low[rows]], axis=0).astype(BF16)
+
+
+def second_direct_kernel(got, link, link_col, owned, pick, meet, first_col, tiles, put, out, first_row):
     count = link.shape[0]
     peers = range(got.shape[0])
     mirrors = jnp.concatenate([got[k, :count, :] for k in peers], axis=0)
     sums = jnp.concatenate([got[k, count:, :] for k in peers], axis=0)
-    y = multiply(dot(link[...], mirrors) + dot(pick[...], sums), turned)
+    y = multiply(dot(link[...], mirrors) + dot(pick[...], sums), tiles, True)
     width = got.shape[0] * LANE
     image = dot(link_col[...], mirrors) + exact_dot(meet[width:, width:], first_col[...])
     forward = iota(image.shape, 0) % LANE < HALF
     out[...] = exact_dot(put[...], y) + jnp.where(forward, image, 0.0)
-
-
-def second_mirror_kernel(got, pick, tiles, put, first, out):
-    y = exact_dot(put[...], multiply(exact_dot(pick[...], got[...]), tiles))
-    out[:, :LANE, :] = y.reshape(-1, LANE, TILE)
-    out[:, LANE:, :] = first[...].reshape(-1, LANE, TILE)
-
-
-def split_rows(got):
-    return got[:, LANE:, :].reshape(-1, TILE), got[:, :LANE, :].reshape(-1, TILE)
-
-
-def inner_kernel(meet, energy, v_row, v_col, got, first_col, second_col, out):
-    first_r, second_r = split_rows(got[...])
+    slot = iota((width, 2 * width), 0)
+    low = iota((width, 2 * width), 1) == slot + slot // LANE * LANE + LANE
+    first_row[...] = dot(owned[...], mirrors) + dot(jnp.where(low, 1.0, 0.0).astype(BF16), sums)
+
+
+def second_mirror_kernel(got, pick, tiles, put, out):
+    out[...] = exact_dot(put[...], multiply(exact_dot(pick[...], got[...]), tiles, False))
+
+
+def inner_kernel(meet, energy, v_row, v_col, first_row, second_row, first_col, second_col, out):
+    first_r, second_r = first_row[...], second_row[...]
     first = jnp.concatenate([first_r, first_col[...]], axis=0)
     second = jnp.concatenate([second_r, second_col[...]], axis=0)
     both = exact_dot(meet[...], jnp.concatenate([first, second], axis=1))
@@ -229,14 +235,18 @@
     out[...] = jnp.broadcast_to(packed, out.shape)
 
 
-def spread_kernel(which, asked_row, asked_col, got, back_col, out):
+def spread_kernel(asked_row, asked_col, first_row, second_row, first_col, second_col, image, second):
     lanes = jnp.concatenate(product_lane(asked_row, asked_col), axis=1)
-    high, low = halves(jnp.concatenate([split_rows(got[...])[which], back_col[...]], axis=0))
+    rows = jnp.concatenate([first_row[...], second_row[...]], axis=1)
+    columns = jnp.concatenate([first_col[...], second_col[...]], axis=1)
+    high, low = halves(jnp.concatenate([rows, columns], axis=0))
     step = 256
-    for start in range(0, out.shape[0], step):
+    for start in range(0, image.shape[0], step):
         place = iota((step, lanes.shape[1]), 0) + start
         select = jnp.where(place == lanes, 1.0, 0.0).astype(BF16)
-        out[start : start + step, :] = dot(select, high) + dot(select, low)
+        both = dot(select, high) + dot(select, low)
+        image[start : start + step, :] = both[:, :TILE]
+        second[start : start + step, :] = both[:, TILE:]
 
 
 def final_kernel(total, got, vector, image, second, out, alpha, rest, near, sems):
@@ -338,70 +348,60 @@
     )
     asked_row = over_row(ask_row)
     asked_col = over_col(ask_col)
-    v_row, energy, turned = call(
-        gather_kernel,
-        (shape(wide_r, TILE), shape(8, TILE), shape(*tiles.shape, dtype=BF16)),
-        asked_row,
-        vector,
-        tiles,
-    )
+    v_row, energy = call(gather_kernel, (shape(wide_r, TILE), shape(8, TILE)), asked_row, vector)
     x_col = over_row(v_row)
-    v_col, meet, link, link_col = call(
-        meet_kernel,
+    first_col, v_col, meet, link, link_col, owned = call(
+        direct_kernel,
         (
+            shape(wide_c, TILE),
             shape(wide_c, TILE),
             shape(every, every, dtype=BF16),
             shape(count, n_row * count, dtype=BF16),
             shape(wide_c, n_row * count, dtype=BF16),
+            shape(wide_r, n_row * count, dtype=BF16),
         ),
+        x_col,
+        pick_row,
+        tiles,
+        put_col,
         asked_row,
         asked_col,
         mine,
         vector,
     )
-    first_col = over_col(call(direct_kernel, shape(wide_c, TILE), x_col, pick_row, turned, put_col, v_col))
-    packed, first = call(
+    first_col = over_col(first_col)
+    packed = call(
         mirror_kernel,
-        (shape(n_row, count + 2 * LANE, TILE, dtype=BF16), shape(wide_r, TILE)),
+        shape(n_row, count + 2 * LANE, TILE, dtype=BF16),
         first_col,
         pick_col,
         tiles,
         put_row,
         meet,
     )
-    second_col = call(
+    second_col, first_row = call(
         second_direct_kernel,
-        shape(wide_c, TILE),
+        (shape(wide_c, TILE), shape(wide_r, TILE)),
         over_row(packed),
         link,
         link_col,
+        owned,
         pick_pair,
         meet,
         first_col,
-        turned,
+        tiles,
         put_col,
     )
     second_col = over_col(second_col)
-    back = call(
-        second_mirror_kernel, shape(n_row, 2 * LANE, TILE), second_col, pick_col, tiles, put_row, first
-    )
-    back = over_row(back)
-    inner = call(
-        inner_kernel,
-        shape(n_row, 8, TILE),
-        meet,
-        energy,
-        v_row,
-        v_col,
-        back,
-        first_col,
-        second_col,
-    )
+    second_row = over_row(
+        call(second_mirror_kernel, shape(wide_r, TILE), second_col, pick_col, tiles, put_row)
+    )
+    products = (first_row, second_row, first_col, second_col)
+    inner = call(inner_kernel, shape(n_row, 8, TILE), meet, energy, v_row, v_col, *products)
     inner = over_row(inner)
-    image, second = [
-        call(functools.partial(spread_kernel, k), shape(pieces, TILE), asked_row, asked_col, back, column)
-        for k, column in enumerate((first_col, second_col))
-    ]
+    image, second = call(
+        spread_kernel, (shape(pieces, TILE), shape(pieces, TILE)), asked_row, asked_col, *products
+    )
     inner = over_col(call(partial_kernel, shape(n_col, TILE), inner))
 
     def finish(*refs):

time: 149 us -> 143 us (0.960)
  blocking collectives: 85 us -> 115 us
  starting transfers between devices: 21.8 us -> 3.83 us
  local copies, waits for them, and re-layouts: 12.2 us -> 4.59 us
  waiting for transfers between devices: 14 us -> 7.45 us
  Pallas kernels: 13.5 us -> 10.7 us
    all_to_all x6 -> x8, blocking collectives: 85 us -> 115 us  [exchange(): got = lax.all_to_all(sent, axis, split_axis=0, concat_axis=0, tiled=True)]
    all_to_all x3 -> x1, starting transfers between devices: 21.8 us -> 3.83 us  [exchange(): got = lax.all_to_all(sent, axis, split_axis=0, concat_axis=0, tiled=True)]
    unnamed x52 -> x10, local copies, waits for them, and re-layouts: 11.4 us -> 3.86 us
    all_to_all x3 -> x1, waiting for transfers between devices: 14 us -> 7.45 us  [exchange(): got = lax.all_to_all(sent, axis, split_axis=0, concat_axis=0, tiled=True)]
    pallas_call x12 -> x10, Pallas kernels: 13.5 us -> 10.7 us  [call(): pl.pallas_call(kernel, out_shape=outs, in_specs=[ins] * len(args), out_sp...]
  transfers between devices with their start and end apart: 3 -> 1, of which waited for: 3 -> 1; matrix products, arithmetic and copies ran while one was open for 0% -> 0% of each run, Pallas kernels for 3% -> 1%
where the time goes in v4:
time: 143 us
  blocking collectives  115 us (80%)
  Pallas kernels  10.7 us (7%)
  waiting for transfers between devices  7.45 us (5%)
  local copies, waits for them, and re-layouts  4.59 us (3%)
  starting transfers between devices  3.83 us (3%)
    all_to_all x8, blocking collectives, exchange(): got = lax.all_to_all(sent, axis, split_axis=0, concat_axis=0, tiled=True)  115 us
    pallas_call x10, Pallas kernels, call(): pl.pallas_call(kernel, out_shape=outs, in_specs=[ins] * len(args), out_sp...  10.7 us
    all_to_all x1, waiting for transfers between devices, exchange(): got = lax.all_to_all(sent, axis, split_axis=0, concat_axis=0, tiled=True)  7.45 us
    unnamed x10, local copies, waits for them, and re-layouts  3.86 us
    all_to_all x1, starting transfers between devices, exchange(): got = lax.all_to_all(sent, axis, split_axis=0, concat_axis=0, tiled=True)  3.83 us
  transfers between devices with their start and end apart: 1, of which 1 were waited for; matrix products, arithmetic and copies ran while one was open for 0% of the time, Pallas kernels for 1%

profile of v4, /device:TPU:1, one launch (start us, length us, event | category | flops | bytes accessed | tf_op | source)
XLA Modules:
  0.0 142.9 jit_solution(9900997948717031381)
XLA Ops:
  1.3 0.7 concatenate.3.slots
  2.0 0.2 shard_map.94
  2.3 17.1 %all_to_all.45 = s32[16,8,128]{2,1,0:T(8,128)S(1)} all-to-all(s32[16,8,128]{2,1,0:T(8,128)S(1)} %bitcast.57), channel_id=1, replica_groups=mesh['row'=16,'col'=32] {'row'}, dimensions={0} | all-to-all | bytes 131072 | tf_op jit(solution)/shard_map/all_to_all | solution.py:310
  19.4 0.0 copy-start.2
  19.4 1.1 copy-done.2
  20.5 0.5 shard_map.95
  21.0 10.4 %all_to_all.46 = f32[16,8,128]{2,1,0:T(8,128)S(1)} all-to-all(f32[16,8,128]{2,1,0:T(8,128)S(1)} %bitcast.52), channel_id=1, replica_groups=mesh['row'=16,'col'=32] {'row'}, dimensions={0} | all-to-all | bytes 131072 | tf_op jit(solution)/shard_map/all_to_all | solution.py:310
  31.4 20.9 %all_to_all.47 = s32[32,8,128]{2,1,0:T(8,128)S(1)} all-to-all(s32[32,8,128]{2,1,0:T(8,128)S(1)} %bitcast.53), channel_id=1, replica_groups=mesh['row'=16,'col'=32] {'col'}, dimensions={0} | all-to-all | bytes 262144 | tf_op jit(solution)/shard_map/all_to_all | solution.py:310
  52.3 0.0 copy-start
  52.4 1.6 %copy-done = bf16[1,1,64,128,128]{4,3,2,1,0:T(8,128)(2,1)S(1)} copy-done((bf16[1,1,64,128,128]{4,3,2,1,0:T(8,128)(2,1)S(1)}, bf16[1,1,64,128,128]{4,3,2,1,0:T(8,128)(2,1)}, u32[]{:S(2)}) %copy-start) | copy-done | bytes 2097176
  53.9 0.0 copy-start.3
  53.9 1.1 copy-done.3
  55.1 0.0 copy-start.1
  55.1 2.2 %shard_map.96 = (f32[256,128]{1,0:T(8,128)S(1)}, f32[256,128]{1,0:T(8,128)S(1)}, bf16[384,384]{1,0:T(8,128)(2,1)S(1)}, bf16[64,1024]{1,0:T(8,128)(2,1)S(1)}, bf1...) custom-call(f32[128,128]{1,0:T(8,128)S(1)} %bitcast.50, bf16[64,128]{1,0:T(8,128)(2,1)S(1)} %get-tuple-element.28.pick, ...), custom_call_target="tpu_custom_call" | custom-call | tf_op jit(solution)/shard_map/pallas_call | solution.py:298
  57.3 13.4 %all_to_all.48 = f32[32,8,128]{2,1,0:T(8,128)S(1)} all-to-all(f32[32,8,128]{2,1,0:T(8,128)S(1)} %bitcast.54), channel_id=1, replica_groups=mesh['row'=16,'col'=32] {'col'}, dimensions={0} | all-to-all | bytes 262144 | tf_op jit(solution)/shard_map/all_to_all | solution.py:310
  70.6 0.0 copy-done.1
  70.6 0.9 shard_map.97
  71.6 18.1 %all_to_all.49.got = bf16[16,80,128]{2,1,0:T(8,128)(2,1)S(1)} all-to-all(bf16[16,80,128]{2,1,0:T(8,128)(2,1)S(1)} %shard_map.97), channel_id=1, replica_groups=mesh['row'=16,'col'=32] {'row'}, dimensions={0} | all-to-all | bytes 655360 | tf_op jit(solution)/shard_map/all_to_all | solution.py:310
  89.6 1.7 %shard_map.98 = (f32[256,128]{1,0:T(8,128)S(1)}, f32[128,128]{1,0:T(8,128)S(1)}) custom-call(bf16[16,80,128]{2,1,0:T(8,128)(2,1)S(1)} %all_to_all.49.got, bf16[64,1024]{1,0:T(8,128)(2,1)S(1)} %get-tuple-element.38.link, bf16[256,1024]{1,0:T(8,128)(2,1)S(1)} %get-tuple-element.39.link_col, bf16[128,1024]{1,0:T(8,128)(2,1)S(1)} %get-tuple-element.40.owned, ...), custom_call_target="tpu_custom_call" | custom-call | tf_op jit(solution)/shard_map/pallas_call | solution.py:298
  91.4 12.8 %all_to_all.50 = f32[32,8,128]{2,1,0:T(8,128)S(1)} all-to-all(f32[32,8,128]{2,1,0:T(8,128)S(1)} %bitcast.55), channel_id=1, replica_groups=mesh['row'=16,'col'=32] {'col'}, dimensions={0} | all-to-all | bytes 262144 | tf_op jit(solution)/shard_map/all_to_all | solution.py:310
  104.2 0.0 copy-start.4
  104.2 0.9 shard_map.99
  105.1 11.8 %all_to_all.51 = f32[16,8,128]{2,1,0:T(8,128)S(1)} all-to-all(f32[16,8,128]{2,1,0:T(8,128)S(1)} %bitcast.51), channel_id=1, replica_groups=mesh['row'=16,'col'=32] {'row'}, dimensions={0} | all-to-all | bytes 131072 | tf_op jit(solution)/shard_map/all_to_all | solution.py:310
  117.0 0.4 shard_map.100
  117.4 10.4 %all_to_all.52.got = f32[16,8,128]{2,1,0:T(8,128)S(1)} all-to-all(f32[16,8,128]{2,1,0:T(8,128)S(1)} %shard_map.100), channel_id=1, replica_groups=mesh['row'=16,'col'=32] {'row'}, dimensions={0} | all-to-all | bytes 131072 | tf_op jit(solution)/shard_map/all_to_all | solution.py:310
  127.8 0.7 shard_map.101
  128.5 3.8 %all-to-all-start.8 = ((f32[32,1,128]{2,1,0:T(1,128)}), f32[32,1,128]{2,1,0:T(1,128)S(1)}, u32[]{:S(2)}, u32[]{:S(2)}) async-start(f32[32,1,128]{2,1,0:T(1,128)} %bitcast.20), calls=%async_computation.8 | async-start | bytes 32768 | tf_op jit(solution)/shard_map/all_to_all | solution.py:310
  132.3 1.1 shard_map.102
  133.4 7.5 %all-to-all-done.8 = f32[32,1,128]{2,1,0:T(1,128)S(1)} async-done(((f32[32,1,128]{2,1,0:T(1,128)}), f32[32,1,128]{2,1,0:T(1,128)S(1)}, u32[]{:S(2)}, u32[]{:S(2)}) %all-to-all-start.8) | async-done | bytes 16416 | tf_op jit(solution)/shard_map/all_to_all | solution.py:310
  140.9 0.0 copy-done.4
  140.9 2.0 %shard_map.103 = (f32[3072,128]{1,0:T(8,128)}, f32[1]{0:T(128)}, f32[3]{0:T(128)}) custom-call(f32[32,128]{1,0:T(8,128)S(1)} %bitcast.56, f32[1536,128]{1,0:T(8,128)S(1)} %bitcast.35, f32[1536,128]{1,0:T(8,128)S(1)} %get-tuple-element.44.refs_2_, f32[1536,128]{1,0:T(8,128)S(1)} %get-tuple-element.45.refs_3_), custom_call_target="tpu_custom_call" | custom-call | tf_op jit(solution)/shard_map/pallas_call | solution.py:298
  (1 shorter events, 0.0 us)
Async XLA Ops:
  19.4 1.1 copy-start.2
  52.3 1.6 %copy-start = (bf16[1,1,64,128,128]{4,3,2,1,0:T(8,128)(2,1)S(1)}, bf16[1,1,64,128,128]{4,3,2,1,0:T(8,128)(2,1)}, u32[]{:S(2)}) copy-start(bf16[1,1,64,128,128]{4,3,2,1,0:T(8,128)(2,1)} %param.8) | copy-start | bytes 6291460
  53.9 1.1 copy-start.3
  55.1 15.6 %copy-start.1 = (bf16[1,1,64,128,128]{4,3,2,1,0:T(8,128)(2,1)S(1)}, bf16[1,1,64,128,128]{4,3,2,1,0:T(8,128)(2,1)}, u32[]{:S(2)}) copy-start(bf16[1,1,64,128,128]{4,3,2,1,0:T(8,128)(2,1)} %param.8) | copy-start | bytes 6291460
  104.2 36.7 %copy-start.4 = (f32[196608]{0:T(1024)S(1)}, f32[196608]{0:T(1024)}, u32[]{:S(2)}) copy-start(f32[196608]{0:T(1024)} %param.7) | copy-start | bytes 2359300
  128.5 12.4 %all-to-all-start.8 = ((f32[32,1,128]{2,1,0:T(1,128)}), f32[32,1,128]{2,1,0:T(1,128)S(1)}, u32[]{:S(2)}, u32[]{:S(2)}) async-start(f32[32,1,128]{2,1,0:T(1,128)} %bitcast.20), calls=%async_computation.8 | async-start | bytes 32768 | tf_op jit(solution)/shard_map/all_to_all | solution.py:310

commit v5 on v4

--- a/solution.py
+++ b/solution.py
@@ -48,40 +48,63 @@
     return (owner * LANE + rank_row).astype(jnp.int32), (column * LANE + rank_column).astype(jnp.int32)
 
 
-def request_kernel(pieces, slots, ask_row, ask_col, pick_row, put_row, pick_col, put_col, pick_pair, mine):
+def request_kernel(pieces, planes, slots, other, ask):
+    n_x, n_z = planes
+    me = slots[5:6, 0:1]
+    x = slots[6:7, 0:1] // n_z
+    count = slots.shape[1]
+    width = ask.shape[0]
+    spot = iota((width, count), 0)
+    col = jnp.zeros((width, 1), F32)
+    row = [[None, None], [None, None]]
+    riders = []
+    for core in range(2):
+        these = jnp.where(me % 2 == core, slots[...], other[...])
+        own_r, blk_r, own_c, blk_c, filled = [these[k : k + 1, :] for k in range(5)]
+        alive = iota((1, count), 1) < filled
+        place = place_of(own_r.astype(F32))[0] + HALF * core
+        value = jnp.where(alive, blk_r + 1, 0).astype(F32)
+        col = col + jnp.sum(jnp.where(spot == place, value, 0.0), axis=1, keepdims=True)
+        place = place_of(own_c.astype(F32))[0]
+        rank, chip = place % LANE, own_c // 2
+        value = jnp.where(alive, blk_c + 1, 0).astype(F32)
+        for side in range(2):
+            there = (spot == (chip * n_x + x) * LANE + rank) & (own_c % 2 == side)
+            row[core][side] = jnp.sum(jnp.where(there, value, 0.0), axis=1, keepdims=True)
+        riders.append((alive, own_c, blk_c, place))
+    lane = iota((width, TILE), 1)
+    down = iota((width, TILE), 0)
+    quarter = lane // 16
+    values = jnp.broadcast_to(row[0][0], (width, TILE))
+    for k in range(1, 4):
+        values = jnp.where(quarter == k, row[k // 2][k % 2], values)
+    values = values.astype(jnp.int32) - 1
+    for core, (alive, own_c, blk_c, place) in enumerate(riders):
+        ident = jnp.where(alive, own_c * pieces + blk_c, -1)
+        for k, rider in ((core, ident), (2 + core, place)):
+            twice = jnp.concatenate([rider, rider], axis=1)
+            values = jnp.where((lane >= count) & (down % LANE == k), twice, values)
+    values = jnp.where(down // LANE % n_x == x, values, -9)
+    ask[...] = jnp.where(me % 2 == 0, jnp.broadcast_to(col, (width, TILE)).astype(jnp.int32) - 1, values)
+
+
+def local_kernel(pieces, slots, vector, tiles, pick_row, put_row, pick_col, put_col, pick_pair, mine, energy):
     own_r, blk_r, own_c, blk_c, filled = [slots[k : k + 1, :] for k in range(5)]
-    count = own_r.shape[1]
-    alive = iota((1, count), 1) < filled
-    for owner, block, ask, pick, put, shift in (
-        (own_c, blk_c, ask_row, pick_row, put_row, 0),
-        (own_r, blk_r, ask_col, pick_col, put_col, HALF),
-    ):
-        width = ask.shape[0]
+    count = slots.shape[1]
+    for owner, pick, put, shift in ((own_c, pick_row, put_row, 0), (own_r, pick_col, put_col, HALF)):
+        width = put.shape[0]
         across, down = place_of(owner.astype(F32))
-        value = jnp.where(alive, block + 1, 0).astype(F32)
-        spot = iota((width, count), 0)
-        there = spot == across
-        back = spot == across + shift
-        wanted = jnp.sum(jnp.where(there | back, value, 0.0), axis=1, keepdims=True) - 1.0
-        ask[...] = jnp.broadcast_to(wanted, (width, TILE)).astype(jnp.int32)
         pick[...] = jnp.where(iota((count, width), 1) == down, 1.0, 0.0).astype(BF16)
-        put[...] = jnp.where(back, 1.0, 0.0).astype(BF16)
-    ident = jnp.where(alive, own_c * pieces + blk_c, -1)
-    width = ask_row.shape[0]
-    lane = iota((width, TILE), 1)
-    number = iota((width, TILE), 0) // LANE
-    spot = place_of(own_c.astype(F32))[0]
-    ids = jnp.concatenate([ident, ident], axis=1)
-    spots = jnp.concatenate([spot, spot], axis=1)
-    ids = jnp.where(iota((width, TILE), 0) % 2 == 0, ids, spots)
-    ask_row[...] = jnp.where(lane >= count, ids, jnp.where(lane == count - 1, number, ask_row[...]))
+        put[...] = jnp.where(iota((width, count), 0) == across + shift, 1.0, 0.0).astype(BF16)
+    ident = jnp.where(iota((1, count), 1) < filled, own_c * pieces + blk_c, -2)
     across = iota((count, count), 0) == iota((count, count), 1)
     down = jnp.sum(jnp.where(across, ident.astype(F32), 0.0), axis=1, keepdims=True).astype(jnp.int32)
-    mine[...] = jnp.broadcast_to(jnp.where(down < 0, -2, down), mine.shape)
+    mine[...] = jnp.broadcast_to(down, mine.shape)
     place = place_of(own_c.astype(F32))[1]
     high = place + place // LANE * LANE
-    lane = iota(pick_pair.shape, 1)
-    pick_pair[...] = jnp.where(lane == high, 1.0, 0.0).astype(BF16)
+    pick_pair[...] = jnp.where(iota(pick_pair.shape, 1) == high, 1.0, 0.0).astype(BF16)
+    v = vector[...] * SCALE
+    energy[...] = jnp.sum((v * v).reshape(-1, 8, TILE), axis=0)
 
 
 def first_lane(asked):
@@ -98,10 +121,30 @@
     return exact_dot(select, vector)
 
 
-def gather_kernel(asked, vector, out, energy):
-    v = vector[...] * SCALE
-    out[...] = gather(first_lane(asked[...]), v)
-    energy[...] = jnp.sum((v * v).reshape(-1, 8, TILE), axis=0)
+def served_kernel(n_x, slots, got, other, vector, asked_row, asked_col, out):
+    me = slots[5:6, 0:1]
+    first = me % 2 == 0
+    width = asked_col.shape[0]
+    col = jnp.where(first, got[...], other[...]).reshape(-1, LANE, TILE)
+    swapped = jnp.concatenate([col[:, HALF:, :], col[:, :HALF, :]], axis=1)
+    lower = iota(col.shape, 1) < HALF
+    keep = lower == first.reshape(1, 1, 1)
+    asked_col[...] = jnp.where(keep, col, swapped).reshape(width, TILE)
+    row = jnp.max(jnp.where(first, other[...], got[...]).reshape(-1, n_x, LANE, TILE), axis=1)
+    slot = iota(row.shape, 1)
+    lane = iota(row.shape, 2)
+    asked, full = [], []
+    for core in range(2):
+        sides = [jnp.broadcast_to(row[:, :, 16 * k : 16 * k + 1], row.shape) for k in (2 * core, 2 * core + 1)]
+        value = jnp.where(first.reshape(1, 1, 1), sides[0], sides[1])
+        riders = jnp.where(slot % 2 == 0, row[:, core : core + 1, :], row[:, 2 + core : 3 + core, :])
+        count = TILE // 2
+        mixed = jnp.where(lane >= count, riders, jnp.where(lane == count - 1, me.reshape(1, 1, 1), value))
+        asked.append(value)
+        full.append(mixed)
+    shape = asked_row.shape
+    asked_row[...] = jnp.stack(full, axis=1).reshape(shape)
+    out[...] = gather(jnp.stack(asked, axis=1).reshape(shape), vector[...] * SCALE)
 
 
 def product_lane(asked_row, asked_col):
@@ -327,28 +370,61 @@
     def over_col(x):
         return exchange(x, "col", n_col)
 
+    n_y = n_row // 2
+    n_x = n_col // n_y
+    n_z = n_col // n_x
+    small = [row_owner, row_block, col_owner, col_block, tile_counts]
+    small += [lax.axis_index("row"), lax.axis_index("col"), jnp.zeros((), jnp.int32)]
     slots = jnp.concatenate(
-        [x.reshape(1, count) for x in (row_owner, row_block, col_owner, col_block)]
-        + [jnp.broadcast_to(tile_counts.reshape(1, 1), (1, count))],
-        axis=0,
-    )
-    ask_row, ask_col, pick_row, put_row, pick_col, put_col, pick_pair, mine = call(
-        functools.partial(request_kernel, pieces),
+        [jnp.broadcast_to(x.reshape(1, -1), (1, count)).astype(jnp.int32) for x in small], axis=0
+    )
+    planes = [[2 * y * n_col + c for c in range(n_col)] for y in range(n_y)]
+    planes += [[(2 * y + 1) * n_col + x * n_z + z for y in range(n_y) for x in range(n_x)] for z in range(n_z)]
+
+    def other_core(x):
+        return lax.ppermute(x, "row", [(r, r ^ 1) for r in range(n_row)])
+
+    ask = call(
+        functools.partial(request_kernel, pieces, (n_x, n_z)),
+        shape(wide_c, TILE, dtype=jnp.int32),
+        slots,
+        other_core(slots),
+    )
+    ask = lax.all_to_all(
+        ask.reshape(n_col, LANE, TILE),
+        ("row", "col"),
+        split_axis=0,
+        concat_axis=0,
+        axis_index_groups=planes,
+        tiled=True,
+    ).reshape(wide_c, TILE)
+    pick_row, put_row, pick_col, put_col, pick_pair, mine, energy = call(
+        functools.partial(local_kernel, pieces),
         (
-            shape(wide_r, TILE, dtype=jnp.int32),
-            shape(wide_c, TILE, dtype=jnp.int32),
             shape(count, wide_r, dtype=BF16),
             shape(wide_r, count, dtype=BF16),
             shape(count, wide_c, dtype=BF16),
             shape(wide_c, count, dtype=BF16),
             shape(count, 2 * wide_r, dtype=BF16),
             shape(count, TILE, dtype=jnp.int32),
+            shape(8, TILE),
         ),
         slots,
-    )
-    asked_row = over_row(ask_row)
-    asked_col = over_col(ask_col)
-    v_row, energy = call(gather_kernel, (shape(wide_r, TILE), shape(8, TILE)), asked_row, vector)
+        vector,
+        tiles,
+    )
+    asked_row, asked_col, v_row = call(
+        functools.partial(served_kernel, n_x),
+        (
+            shape(wide_r, TILE, dtype=jnp.int32),
+            shape(wide_c, TILE, dtype=jnp.int32),
+            shape(wide_r, TILE),
+        ),
+        slots,
+        ask,
+        other_core(ask),
+        vector,
+    )
     x_col = over_row(v_row)
     first_col, v_col, meet, link, link_col, owned = call(
         direct_kernel,

time: 143 us -> 140 us (0.979)
  blocking collectives: 115 us -> 79.2 us
  starting transfers between devices: 3.83 us -> 26.8 us
  waiting for transfers between devices: 7.45 us -> 14 us
  Pallas kernels: 10.7 us -> 12.9 us
    all_to_all x8 -> x5, blocking collectives: 115 us -> 65.8 us  [exchange(): got = lax.all_to_all(sent, axis, split_axis=0, concat_axis=0, tiled=True)]
    ppermute x0 -> x2, starting transfers between devices: none -> 15.5 us  [other_core(): return lax.ppermute(x, 'row', [(r, r ^ 1) for r in range(n_row)])]
    all_to_all x0 -> x1, blocking collectives: none -> 13.4 us  [per_device(): lax.all_to_all(ask.reshape(n_col, LANE, TILE), ('row', 'col'), split_axis...]
    all_to_all x1 -> x2, starting transfers between devices: 3.83 us -> 11.3 us  [exchange(): got = lax.all_to_all(sent, axis, split_axis=0, concat_axis=0, tiled=True)]
    all_to_all x1 -> x2, waiting for transfers between devices: 7.45 us -> 12.2 us  [exchange(): got = lax.all_to_all(sent, axis, split_axis=0, concat_axis=0, tiled=True)]
    pallas_call x10 -> x11, Pallas kernels: 10.7 us -> 12.9 us  [call(): pl.pallas_call(kernel, out_shape=outs, in_specs=[ins] * len(args), out_sp...]
    ppermute x0 -> x2, waiting for transfers between devices: none -> 1.77 us  [other_core(): return lax.ppermute(x, 'row', [(r, r ^ 1) for r in range(n_row)])]
  transfers between devices with their start and end apart: 1 -> 4, of which waited for: 1 -> 4; matrix products, arithmetic and copies ran while one was open for 0% -> 0% of each run, Pallas kernels for 1% -> 1%
where the time goes in v5:
time: 140 us; the launch traced here: 139 us
  blocking collectives  79.2 us (57%)
  starting transfers between devices  26.8 us (19%)
  waiting for transfers between devices  14 us (10%)
  Pallas kernels  12.9 us (9%)
  local copies, waits for them, and re-layouts  4.6 us (3%)
    all_to_all x5, blocking collectives, exchange(): got = lax.all_to_all(sent, axis, split_axis=0, concat_axis=0, tiled=True)  65.8 us
    ppermute x2, starting transfers between devices, other_core(): return lax.ppermute(x, 'row', [(r, r ^ 1) for r in range(n_row)])  15.5 us
    all_to_all x1, blocking collectives, per_device(): lax.all_to_all(ask.reshape(n_col, LANE, TILE), ('row', 'col'), split_axis...  13.4 us
    pallas_call x11, Pallas kernels, call(): pl.pallas_call(kernel, out_shape=outs, in_specs=[ins] * len(args), out_sp...  12.9 us
    all_to_all x2, waiting for transfers between devices, exchange(): got = lax.all_to_all(sent, axis, split_axis=0, concat_axis=0, tiled=True)  12.2 us
    all_to_all x2, starting transfers between devices, exchange(): got = lax.all_to_all(sent, axis, split_axis=0, concat_axis=0, tiled=True)  11.3 us
    unnamed x10, local copies, waits for them, and re-layouts  3.86 us
  transfers between devices with their start and end apart: 4, of which 4 were waited for; matrix products, arithmetic and copies ran while one was open for 0% of the time, Pallas kernels for 1%

profile of v5, /device:TPU:1, one launch (start us, length us, event | category | flops | bytes accessed | tf_op | source)
XLA Modules:
  0.0 138.8 jit_solution(12128079224749388475)
XLA Ops:
  1.3 0.7 concatenate.3.slots
  2.1 8.8 %collective-permute-start = (s32[8,64]{1,0:T(8,128)S(1)}, s32[8,64]{1,0:T(8,128)S(1)}, u32[]{:S(2)}, u32[]{:S(2)}) collective-permute-start(s32[8,64]{1,0:T(8,128)S(1)} %concatenate.3.slots), channel_id=1, source_target_pairs={{0,32},{32,0},{64,96},{96,64},{128,160},{160,128},{192,224},{224,1... | collective-permute-start | bytes 6152 | tf_op jit(solution)/shard_map/ppermute | solution.py:385
  10.8 0.8 collective-permute-done.other
  11.6 0.6 shard_map.94
  12.3 13.4 %all_to_all.40 = s32[32,8,128]{2,1,0:T(8,128)S(1)} all-to-all(s32[32,8,128]{2,1,0:T(8,128)S(1)} %bitcast.45), channel_id=1, replica_groups={{0,1,2,3,4,5,6,7,8,9,10,11,12,13,14,15,16,17,18,19,20,21,22,23,24,25,26..., dimensions={0} | all-to-all | bytes 262144 | tf_op jit(solution)/shard_map/all_to_all | solution.py:393
  25.7 6.7 %collective-permute-start.1 = (s32[256,128]{1,0:T(8,128)S(1)}, s32[256,128]{1,0:T(8,128)S(1)}, u32[]{:S(2)}, u32[]{:S(2)}) collective-permute-start(s32[256,128]{1,0:T(8,128)S(1)} %bitcast.46), channel_id=1, source_target_pairs={{0,32},{32,0},{64,96},{96,64},{128,160},{160,128},{192,224},{224,1... | collective-permute-start | bytes 393224 | tf_op jit(solution)/shard_map/ppermute | solution.py:385
  32.4 1.0 collective-permute-done.1.other
  33.4 0.0 copy-start.2
  33.4 1.1 copy-done.2
  34.5 0.0 copy-start.4
  34.5 1.2 shard_map.95
  35.7 7.5 %all-to-all-start.1 = ((f32[16,8,128]{2,1,0:T(8,128)}), f32[16,8,128]{2,1,0:T(8,128)S(1)}, u32[]{:S(2)}, u32[]{:S(2)}) async-start(f32[16,8,128]{2,1,0:T(8,128)} %bitcast.8), calls=%async_computation.1 | async-start | bytes 131072 | tf_op jit(solution)/shard_map/all_to_all | solution.py:353
  43.1 0.0 copy-start
  43.1 1.6 %copy-done = bf16[1,1,64,128,128]{4,3,2,1,0:T(8,128)(2,1)S(1)} copy-done((bf16[1,1,64,128,128]{4,3,2,1,0:T(8,128)(2,1)S(1)}, bf16[1,1,64,128,128]{4,3,2,1,0:T(8,128)(2,1)}, u32[]{:S(2)}) %copy-start) | copy-done | bytes 2097176
  44.7 0.0 copy-start.3
  44.7 1.1 copy-done.3
  45.9 0.0 copy-start.1
  45.9 0.3 shard_map.96
  46.2 4.7 %all-to-all-done.1 = f32[16,8,128]{2,1,0:T(8,128)S(1)} async-done(((f32[16,8,128]{2,1,0:T(8,128)}), f32[16,8,128]{2,1,0:T(8,128)S(1)}, u32[]{:S(2)}, u32[]{:S(2)}) %all-to-all-start.1) | async-done | bytes 65568 | tf_op jit(solution)/shard_map/all_to_all | solution.py:353
  50.9 0.0 copy-done.4
  51.0 0.0 copy-done.1
  51.0 2.2 %shard_map.97 = (f32[256,128]{1,0:T(8,128)S(1)}, f32[256,128]{1,0:T(8,128)S(1)}, bf16[384,384]{1,0:T(8,128)(2,1)S(1)}, bf16[64,1024]{1,0:T(8,128)(2,1)S(1)}, bf1...) custom-call(f32[128,128]{1,0:T(8,128)S(1)} %bitcast.48, bf16[64,128]{1,0:T(8,128)(2,1)S(1)} %get-tuple-element.27.pick, ...), custom_call_target="tpu_custom_call" | custom-call | tf_op jit(solution)/shard_map/pallas_call | solution.py:341
  53.1 12.4 %all_to_all.41 = f32[32,8,128]{2,1,0:T(8,128)S(1)} all-to-all(f32[32,8,128]{2,1,0:T(8,128)S(1)} %bitcast.50), channel_id=1, replica_groups=mesh['row'=16,'col'=32] {'col'}, dimensions={0} | all-to-all | bytes 262144 | tf_op jit(solution)/shard_map/all_to_all | solution.py:353
  65.6 0.9 shard_map.98
  66.5 18.3 %all_to_all.42.got = bf16[16,80,128]{2,1,0:T(8,128)(2,1)S(1)} all-to-all(bf16[16,80,128]{2,1,0:T(8,128)(2,1)S(1)} %shard_map.98), channel_id=1, replica_groups=mesh['row'=16,'col'=32] {'row'}, dimensions={0} | all-to-all | bytes 655360 | tf_op jit(solution)/shard_map/all_to_all | solution.py:353
  84.8 1.7 %shard_map.99 = (f32[256,128]{1,0:T(8,128)S(1)}, f32[128,128]{1,0:T(8,128)S(1)}) custom-call(bf16[16,80,128]{2,1,0:T(8,128)(2,1)S(1)} %all_to_all.42.got, bf16[64,1024]{1,0:T(8,128)(2,1)S(1)} %get-tuple-element.38.link, bf16[256,1024]{1,0:T(8,128)(2,1)S(1)} %get-tuple-element.39.link_col, bf16[128,1024]{1,0:T(8,128)(2,1)S(1)} %get-tuple-element.40.owned, ...), custom_call_target="tpu_custom_call" | custom-call | tf_op jit(solution)/shard_map/pallas_call | solution.py:341
  86.5 12.9 %all_to_all.43 = f32[32,8,128]{2,1,0:T(8,128)S(1)} all-to-all(f32[32,8,128]{2,1,0:T(8,128)S(1)} %bitcast.51), channel_id=1, replica_groups=mesh['row'=16,'col'=32] {'col'}, dimensions={0} | all-to-all | bytes 262144 | tf_op jit(solution)/shard_map/all_to_all | solution.py:353
  99.4 0.9 shard_map.100
  100.4 11.8 %all_to_all.44 = f32[16,8,128]{2,1,0:T(8,128)S(1)} all-to-all(f32[16,8,128]{2,1,0:T(8,128)S(1)} %bitcast.49), channel_id=1, replica_groups=mesh['row'=16,'col'=32] {'row'}, dimensions={0} | all-to-all | bytes 131072 | tf_op jit(solution)/shard_map/all_to_all | solution.py:353
  112.1 1.2 shard_map.101
  113.4 10.4 %all_to_all.45.got = f32[16,8,128]{2,1,0:T(8,128)S(1)} all-to-all(f32[16,8,128]{2,1,0:T(8,128)S(1)} %shard_map.101), channel_id=1, replica_groups=mesh['row'=16,'col'=32] {'row'}, dimensions={0} | all-to-all | bytes 131072 | tf_op jit(solution)/shard_map/all_to_all | solution.py:353
  123.8 0.7 shard_map.102
  124.5 3.8 %all-to-all-start.7 = ((f32[32,1,128]{2,1,0:T(1,128)}), f32[32,1,128]{2,1,0:T(1,128)S(1)}, u32[]{:S(2)}, u32[]{:S(2)}) async-start(f32[32,1,128]{2,1,0:T(1,128)} %bitcast.18), calls=%async_computation.7 | async-start | bytes 32768 | tf_op jit(solution)/shard_map/all_to_all | solution.py:353
  128.3 1.1 shard_map.103
  129.4 7.5 %all-to-all-done.7 = f32[32,1,128]{2,1,0:T(1,128)S(1)} async-done(((f32[32,1,128]{2,1,0:T(1,128)}), f32[32,1,128]{2,1,0:T(1,128)S(1)}, u32[]{:S(2)}, u32[]{:S(2)}) %all-to-all-start.7) | async-done | bytes 16416 | tf_op jit(solution)/shard_map/all_to_all | solution.py:353
  136.9 2.0 %shard_map.104 = (f32[3072,128]{1,0:T(8,128)}, f32[1]{0:T(128)}, f32[3]{0:T(128)}) custom-call(f32[32,128]{1,0:T(8,128)S(1)} %bitcast.52, f32[1536,128]{1,0:T(8,128)S(1)} %bitcast.35, f32[1536,128]{1,0:T(8,128)S(1)} %get-tuple-element.44.refs_2_, f32[1536,128]{1,0:T(8,128)S(1)} %get-tuple-element.45.refs_3_), custom_call_target="tpu_custom_call" | custom-call | tf_op jit(solution)/shard_map/pallas_call | solution.py:341
  (4 shorter events, 0.0 us)
Async XLA Ops:
  2.1 9.6 %collective-permute-start = (s32[8,64]{1,0:T(8,128)S(1)}, s32[8,64]{1,0:T(8,128)S(1)}, u32[]{:S(2)}, u32[]{:S(2)}) collective-permute-start(s32[8,64]{1,0:T(8,128)S(1)} %concatenate.3.slots), channel_id=1, source_target_pairs={{0,32},{32,0},{64,96},{96,64},{128,160},{160,128},{192,224},{224,1... | collective-permute-start | bytes 6152 | tf_op jit(solution)/shard_map/ppermute | solution.py:385
  25.7 7.7 %collective-permute-start.1 = (s32[256,128]{1,0:T(8,128)S(1)}, s32[256,128]{1,0:T(8,128)S(1)}, u32[]{:S(2)}, u32[]{:S(2)}) collective-permute-start(s32[256,128]{1,0:T(8,128)S(1)} %bitcast.46), channel_id=1, source_target_pairs={{0,32},{32,0},{64,96},{96,64},{128,160},{160,128},{192,224},{224,1... | collective-permute-start | bytes 393224 | tf_op jit(solution)/shard_map/ppermute | solution.py:385
  33.4 1.1 copy-start.2
  34.5 16.4 %copy-start.4 = (f32[196608]{0:T(1024)S(1)}, f32[196608]{0:T(1024)}, u32[]{:S(2)}) copy-start(f32[196608]{0:T(1024)} %param.7) | copy-start | bytes 2359300
  35.7 15.3 %all-to-all-start.1 = ((f32[16,8,128]{2,1,0:T(8,128)}), f32[16,8,128]{2,1,0:T(8,128)S(1)}, u32[]{:S(2)}, u32[]{:S(2)}) async-start(f32[16,8,128]{2,1,0:T(8,128)} %bitcast.8), calls=%async_computation.1 | async-start | bytes 131072 | tf_op jit(solution)/shard_map/all_to_all | solution.py:353
  43.1 1.6 %copy-start = (bf16[1,1,64,128,128]{4,3,2,1,0:T(8,128)(2,1)S(1)}, bf16[1,1,64,128,128]{4,3,2,1,0:T(8,128)(2,1)}, u32[]{:S(2)}) copy-start(bf16[1,1,64,128,128]{4,3,2,1,0:T(8,128)(2,1)} %param.8) | copy-start | bytes 6291460
  44.7 1.1 copy-start.3
  45.9 5.1 %copy-start.1 = (bf16[1,1,64,128,128]{4,3,2,1,0:T(8,128)(2,1)S(1)}, bf16[1,1,64,128,128]{4,3,2,1,0:T(8,128)(2,1)}, u32[]{:S(2)}) copy-start(bf16[1,1,64,128,128]{4,3,2,1,0:T(8,128)(2,1)} %param.8) | copy-start | bytes 6291460
  124.5 12.4 %all-to-all-start.7 = ((f32[32,1,128]{2,1,0:T(1,128)}), f32[32,1,128]{2,1,0:T(1,128)S(1)}, u32[]{:S(2)}, u32[]{:S(2)}) async-start(f32[32,1,128]{2,1,0:T(1,128)} %bitcast.18), calls=%async_computation.7 | async-start | bytes 32768 | tf_op jit(solution)/shard_map/all_to_all | solution.py:353

commit v6 on v5

--- a/solution.py
+++ b/solution.py
@@ -48,7 +48,7 @@
     return (owner * LANE + rank_row).astype(jnp.int32), (column * LANE + rank_column).astype(jnp.int32)
 
 
-def request_kernel(pieces, planes, slots, other, ask):
+def request_kernel(pieces, planes, slots, both, ask):
     n_x, n_z = planes
     me = slots[5:6, 0:1]
     x = slots[6:7, 0:1] // n_z
@@ -59,8 +59,7 @@
     row = [[None, None], [None, None]]
     riders = []
     for core in range(2):
-        these = jnp.where(me % 2 == core, slots[...], other[...])
-        own_r, blk_r, own_c, blk_c, filled = [these[k : k + 1, :] for k in range(5)]
+        own_r, blk_r, own_c, blk_c, filled = [both[8 * core + k : 8 * core + k + 1, :] for k in range(5)]
         alive = iota((1, count), 1) < filled
         place = place_of(own_r.astype(F32))[0] + HALF * core
         value = jnp.where(alive, blk_r + 1, 0).astype(F32)
@@ -121,16 +120,16 @@
     return exact_dot(select, vector)
 
 
-def served_kernel(n_x, slots, got, other, vector, asked_row, asked_col, out):
+def served_kernel(n_x, slots, pair, vector, squares, asked_row, asked_col, out, energy):
     me = slots[5:6, 0:1]
     first = me % 2 == 0
     width = asked_col.shape[0]
-    col = jnp.where(first, got[...], other[...]).reshape(-1, LANE, TILE)
+    col = pair[:width, :].reshape(-1, LANE, TILE)
     swapped = jnp.concatenate([col[:, HALF:, :], col[:, :HALF, :]], axis=1)
     lower = iota(col.shape, 1) < HALF
     keep = lower == first.reshape(1, 1, 1)
     asked_col[...] = jnp.where(keep, col, swapped).reshape(width, TILE)
-    row = jnp.max(jnp.where(first, other[...], got[...]).reshape(-1, n_x, LANE, TILE), axis=1)
+    row = jnp.max(pair[width:, :].reshape(-1, n_x, LANE, TILE), axis=1)
     slot = iota(row.shape, 1)
     lane = iota(row.shape, 2)
     asked, full = [], []
@@ -145,6 +144,7 @@
     shape = asked_row.shape
     asked_row[...] = jnp.stack(full, axis=1).reshape(shape)
     out[...] = gather(jnp.stack(asked, axis=1).reshape(shape), vector[...] * SCALE)
+    energy[...] = jnp.sum(squares[...], axis=0, keepdims=True)
 
 
 def product_lane(asked_row, asked_col):
@@ -259,7 +259,7 @@
         return jnp.sum(a_r * b_r, axis=0, keepdims=True) + jnp.sum(a_c * b_c, axis=0, keepdims=True)
 
     values = [
-        jnp.sum(energy[...], axis=0, keepdims=True),
+        energy[...],
         inner(v_row[...], first_r, v_col[...], first_c),
         inner(image[:width], first_r, image[width:], first_c),
         inner(v_row[...], second_r, v_col[...], second_c),
@@ -381,14 +381,16 @@
     planes = [[2 * y * n_col + c for c in range(n_col)] for y in range(n_y)]
     planes += [[(2 * y + 1) * n_col + x * n_z + z for y in range(n_y) for x in range(n_x)] for z in range(n_z)]
 
-    def other_core(x):
-        return lax.ppermute(x, "row", [(r, r ^ 1) for r in range(n_row)])
+    chips = [[2 * y, 2 * y + 1] for y in range(n_y)]
+
+    def over_chip(x):
+        return lax.all_gather(x, "row", axis_index_groups=chips, tiled=True)
 
     ask = call(
         functools.partial(request_kernel, pieces, (n_x, n_z)),
         shape(wide_c, TILE, dtype=jnp.int32),
         slots,
-        other_core(slots),
+        over_chip(slots),
     )
     ask = lax.all_to_all(
         ask.reshape(n_col, LANE, TILE),
@@ -398,7 +400,7 @@
         axis_index_groups=planes,
         tiled=True,
     ).reshape(wide_c, TILE)
-    pick_row, put_row, pick_col, put_col, pick_pair, mine, energy = call(
+    pick_row, put_row, pick_col, put_col, pick_pair, mine, squares = call(
         functools.partial(local_kernel, pieces),
         (
             shape(count, wide_r, dtype=BF16),
@@ -413,17 +415,18 @@
         vector,
         tiles,
     )
-    asked_row, asked_col, v_row = call(
+    asked_row, asked_col, v_row, energy = call(
         functools.partial(served_kernel, n_x),
         (
             shape(wide_r, TILE, dtype=jnp.int32),
             shape(wide_c, TILE, dtype=jnp.int32),
             shape(wide_r, TILE),
+            shape(1, TILE),
         ),
         slots,
-        ask,
-        other_core(ask),
+        over_chip(ask),
         vector,
+        squares,
     )
     x_col = over_row(v_row)
     first_col, v_col, meet, link, link_col, owned = call(

time: 140 us -> 134 us (0.957)
  starting transfers between devices: 26.8 us -> 8.13 us
  blocking collectives: 79.2 us -> 94.9 us
    ppermute x2 -> x0, starting transfers between devices: 15.5 us -> none  [other_core(): return lax.ppermute(x, 'row', [(r, r ^ 1) for r in range(n_row)])]
    all_gather x0 -> x2, blocking collectives: none -> 14.7 us  [over_chip(): return lax.all_gather(x, 'row', axis_index_groups=chips, tiled=True)]
    all_to_all x5 -> x6, blocking collectives: 65.8 us -> 80.2 us  [exchange(): got = lax.all_to_all(sent, axis, split_axis=0, concat_axis=0, tiled=True)]
    all_to_all x1 -> x0, blocking collectives: 13.4 us -> none  [per_device(): lax.all_to_all(ask.reshape(n_col, LANE, TILE), ('row', 'col'), split_axis...]
    all_to_all x2 -> x1, starting transfers between devices: 11.3 us -> 3.83 us  [exchange(): got = lax.all_to_all(sent, axis, split_axis=0, concat_axis=0, tiled=True)]
    all_to_all x0 -> x1, waiting for transfers between devices: none -> 6.29 us  [per_device(): lax.all_to_all(ask.reshape(n_col, LANE, TILE), ('row', 'col'), split_axis...]
    all_to_all x2 -> x1, waiting for transfers between devices: 12.2 us -> 7.45 us  [exchange(): got = lax.all_to_all(sent, axis, split_axis=0, concat_axis=0, tiled=True)]
    all_to_all x0 -> x1, starting transfers between devices: none -> 4.3 us  [per_device(): lax.all_to_all(ask.reshape(n_col, LANE, TILE), ('row', 'col'), split_axis...]
  transfers between devices with their start and end apart: 4 -> 2, of which waited for: 4 -> 2; matrix products, arithmetic and copies ran while one was open for 0% -> 0% of each run, Pallas kernels for 1% -> 1%
where the time goes in v6:
time: 134 us
  blocking collectives  94.9 us (71%)
  waiting for transfers between devices  13.7 us (10%)
  Pallas kernels  12.1 us (9%)
  starting transfers between devices  8.13 us (6%)
  local copies, waits for them, and re-layouts  3.47 us (3%)
  between operations  1.39 us (1%)
    all_to_all x6, blocking collectives, exchange(): got = lax.all_to_all(sent, axis, split_axis=0, concat_axis=0, tiled=True)  80.2 us
    all_gather x2, blocking collectives, over_chip(): return lax.all_gather(x, 'row', axis_index_groups=chips, tiled=True)  14.7 us
    pallas_call x11, Pallas kernels, call(): pl.pallas_call(kernel, out_shape=outs, in_specs=[ins] * len(args), out_sp...  12.1 us
    all_to_all x1, waiting for transfers between devices, exchange(): got = lax.all_to_all(sent, axis, split_axis=0, concat_axis=0, tiled=True)  7.45 us
    all_to_all x1, waiting for transfers between devices, per_device(): lax.all_to_all(ask.reshape(n_col, LANE, TILE), ('row', 'col'), split_axis...  6.29 us
    all_to_all x1, starting transfers between devices, per_device(): lax.all_to_all(ask.reshape(n_col, LANE, TILE), ('row', 'col'), split_axis...  4.3 us
    all_to_all x1, starting transfers between devices, exchange(): got = lax.all_to_all(sent, axis, split_axis=0, concat_axis=0, tiled=True)  3.83 us
    unnamed x8, local copies, waits for them, and re-layouts  2.73 us
  transfers between devices with their start and end apart: 2, of which 2 were waited for; matrix products, arithmetic and copies ran while one was open for 0% of the time, Pallas kernels for 1%

profile of v6, /device:TPU:1, one launch (start us, length us, event | category | flops | bytes accessed | tf_op | source)
XLA Modules:
  0.0 133.7 jit_solution(15616786640849571768)
XLA Ops:
  1.3 0.7 concatenate.3.slots
  2.1 8.4 %all_gather.6.both = s32[16,64]{1,0:T(8,128)S(1)} all-gather(s32[8,64]{1,0:T(8,128)S(1)} %concatenate.3.slots), channel_id=1, replica_groups={{0,32},{64,96},{128,160},{192,224},{256,288},{320,352},{384,416},{448,4..., dimensions={0}, use_global_device_ids=true | all-gather | bytes 6144 | tf_op jit(solution)/shard_map/all_gather | solution.py:387
  10.4 1.4 %shard_map.94 = s32[256,128]{1,0:T(8,128)} custom-call(s32[8,64]{1,0:T(8,128)S(1)} %concatenate.3.slots, s32[16,64]{1,0:T(8,128)S(1)} %all_gather.6.both), custom_call_target="tpu_custom_call" | custom-call | tf_op jit(solution)/shard_map/pallas_call | solution.py:341
  11.8 4.3 %all-to-all-start = ((s32[32,8,128]{2,1,0:T(8,128)}), s32[32,8,128]{2,1,0:T(8,128)S(1)}, u32[]{:S(2)}, u32[]{:S(2)}) async-start(s32[32,8,128]{2,1,0:T(8,128)} %bitcast.5), calls=%async_computation | async-start | bytes 262144 | tf_op jit(solution)/shard_map/all_to_all | solution.py:395
  16.1 0.0 copy-start
  16.1 1.6 %copy-done = bf16[1,1,64,128,128]{4,3,2,1,0:T(8,128)(2,1)S(1)} copy-done((bf16[1,1,64,128,128]{4,3,2,1,0:T(8,128)(2,1)S(1)}, bf16[1,1,64,128,128]{4,3,2,1,0:T(8,128)(2,1)}, u32[]{:S(2)}) %copy-start) | copy-done | bytes 2097176
  17.7 0.0 copy-start.2
  17.7 1.1 copy-done.2
  18.8 0.0 copy-start.3
  18.8 0.0 copy-start.1
  18.8 0.3 shard_map.95
  19.1 6.3 %all-to-all-done = s32[32,8,128]{2,1,0:T(8,128)S(1)} async-done(((s32[32,8,128]{2,1,0:T(8,128)}), s32[32,8,128]{2,1,0:T(8,128)S(1)}, u32[]{:S(2)}, u32[]{:S(2)}) %all-to-all-start) | async-done | bytes 131104 | tf_op jit(solution)/shard_map/all_to_all | solution.py:395
  25.4 6.4 %all_gather.7.pair = s32[512,128]{1,0:T(8,128)S(1)} all-gather(s32[256,128]{1,0:T(8,128)S(1)} %bitcast.51), channel_id=1, replica_groups={{0,32},{64,96},{128,160},{192,224},{256,288},{320,352},{384,416},{448,4..., dimensions={0}, use_global_device_ids=true | all-gather | bytes 393216 | tf_op jit(solution)/shard_map/all_gather | solution.py:387
  31.8 0.0 copy-done.3
  31.8 0.5 shard_map.96
  32.3 15.1 %all_to_all.40 = f32[16,8,128]{2,1,0:T(8,128)S(1)} all-to-all(f32[16,8,128]{2,1,0:T(8,128)S(1)} %bitcast.45), channel_id=1, replica_groups=mesh['row'=16,'col'=32] {'row'}, dimensions={0} | all-to-all | bytes 131072 | tf_op jit(solution)/shard_map/all_to_all | solution.py:353
  47.4 0.0 copy-done.1
  47.4 2.2 %shard_map.97 = (f32[256,128]{1,0:T(8,128)S(1)}, f32[256,128]{1,0:T(8,128)S(1)}, bf16[384,384]{1,0:T(8,128)(2,1)S(1)}, bf16[64,1024]{1,0:T(8,128)(2,1)S(1)}, bf1...) custom-call(f32[128,128]{1,0:T(8,128)S(1)} %bitcast.46, bf16[64,128]{1,0:T(8,128)(2,1)S(1)} %get-tuple-element.29.pick, ...), custom_call_target="tpu_custom_call" | custom-call | tf_op jit(solution)/shard_map/pallas_call | solution.py:341
  49.5 12.4 %all_to_all.41 = f32[32,8,128]{2,1,0:T(8,128)S(1)} all-to-all(f32[32,8,128]{2,1,0:T(8,128)S(1)} %bitcast.48), channel_id=1, replica_groups=mesh['row'=16,'col'=32] {'col'}, dimensions={0} | all-to-all | bytes 262144 | tf_op jit(solution)/shard_map/all_to_all | solution.py:353
  62.0 0.9 shard_map.98
  62.9 17.6 %all_to_all.42.got = bf16[16,80,128]{2,1,0:T(8,128)(2,1)S(1)} all-to-all(bf16[16,80,128]{2,1,0:T(8,128)(2,1)S(1)} %shard_map.98), channel_id=1, replica_groups=mesh['row'=16,'col'=32] {'row'}, dimensions={0} | all-to-all | bytes 655360 | tf_op jit(solution)/shard_map/all_to_all | solution.py:353
  80.4 1.7 %shard_map.99 = (f32[256,128]{1,0:T(8,128)S(1)}, f32[128,128]{1,0:T(8,128)S(1)}) custom-call(bf16[16,80,128]{2,1,0:T(8,128)(2,1)S(1)} %all_to_all.42.got, bf16[64,1024]{1,0:T(8,128)(2,1)S(1)} %get-tuple-element.40.link, bf16[256,1024]{1,0:T(8,128)(2,1)S(1)} %get-tuple-element.41.link_col, bf16[128,1024]{1,0:T(8,128)(2,1)S(1)} %get-tuple-element.42.owned, ...), custom_call_target="tpu_custom_call" | custom-call | tf_op jit(solution)/shard_map/pallas_call | solution.py:341
  82.2 12.9 %all_to_all.43 = f32[32,8,128]{2,1,0:T(8,128)S(1)} all-to-all(f32[32,8,128]{2,1,0:T(8,128)S(1)} %bitcast.49), channel_id=1, replica_groups=mesh['row'=16,'col'=32] {'col'}, dimensions={0} | all-to-all | bytes 262144 | tf_op jit(solution)/shard_map/all_to_all | solution.py:353
  95.1 0.9 shard_map.100
  96.0 11.8 %all_to_all.44 = f32[16,8,128]{2,1,0:T(8,128)S(1)} all-to-all(f32[16,8,128]{2,1,0:T(8,128)S(1)} %bitcast.47), channel_id=1, replica_groups=mesh['row'=16,'col'=32] {'row'}, dimensions={0} | all-to-all | bytes 131072 | tf_op jit(solution)/shard_map/all_to_all | solution.py:353
  107.8 0.4 shard_map.101
  108.2 10.4 %all_to_all.45.got = f32[16,8,128]{2,1,0:T(8,128)S(1)} all-to-all(f32[16,8,128]{2,1,0:T(8,128)S(1)} %shard_map.101), channel_id=1, replica_groups=mesh['row'=16,'col'=32] {'row'}, dimensions={0} | all-to-all | bytes 131072 | tf_op jit(solution)/shard_map/all_to_all | solution.py:353
  118.7 0.7 shard_map.102
  119.4 3.8 %all-to-all-start.7 = ((f32[32,1,128]{2,1,0:T(1,128)}), f32[32,1,128]{2,1,0:T(1,128)S(1)}, u32[]{:S(2)}, u32[]{:S(2)}) async-start(f32[32,1,128]{2,1,0:T(1,128)} %bitcast.18), calls=%async_computation.7 | async-start | bytes 32768 | tf_op jit(solution)/shard_map/all_to_all | solution.py:353
  123.2 1.1 shard_map.103
  124.3 7.5 %all-to-all-done.7 = f32[32,1,128]{2,1,0:T(1,128)S(1)} async-done(((f32[32,1,128]{2,1,0:T(1,128)}), f32[32,1,128]{2,1,0:T(1,128)S(1)}, u32[]{:S(2)}, u32[]{:S(2)}) %all-to-all-start.7) | async-done | bytes 16416 | tf_op jit(solution)/shard_map/all_to_all | solution.py:353
  131.8 2.0 %shard_map.104 = (f32[3072,128]{1,0:T(8,128)}, f32[1]{0:T(128)}, f32[3]{0:T(128)}) custom-call(f32[32,128]{1,0:T(8,128)S(1)} %bitcast.50, f32[1536,128]{1,0:T(8,128)S(1)} %bitcast.35, f32[1536,128]{1,0:T(8,128)S(1)} %get-tuple-element.46.refs_2_, f32[1536,128]{1,0:T(8,128)S(1)} %get-tuple-element.47.refs_3_), custom_call_target="tpu_custom_call" | custom-call | tf_op jit(solution)/shard_map/pallas_call | solution.py:341
  (4 shorter events, 0.0 us)
Async XLA Ops:
  11.8 13.7 %all-to-all-start = ((s32[32,8,128]{2,1,0:T(8,128)}), s32[32,8,128]{2,1,0:T(8,128)S(1)}, u32[]{:S(2)}, u32[]{:S(2)}) async-start(s32[32,8,128]{2,1,0:T(8,128)} %bitcast.5), calls=%async_computation | async-start | bytes 262144 | tf_op jit(solution)/shard_map/all_to_all | solution.py:395
  16.1 1.6 %copy-start = (bf16[1,1,64,128,128]{4,3,2,1,0:T(8,128)(2,1)S(1)}, bf16[1,1,64,128,128]{4,3,2,1,0:T(8,128)(2,1)}, u32[]{:S(2)}) copy-start(bf16[1,1,64,128,128]{4,3,2,1,0:T(8,128)(2,1)} %param.8) | copy-start | bytes 6291460
  17.7 1.1 copy-start.2
  18.8 13.0 %copy-start.3 = (f32[196608]{0:T(1024)S(1)}, f32[196608]{0:T(1024)}, u32[]{:S(2)}) copy-start(f32[196608]{0:T(1024)} %param.7) | copy-start | bytes 2359300
  18.8 28.6 %copy-start.1 = (bf16[1,1,64,128,128]{4,3,2,1,0:T(8,128)(2,1)S(1)}, bf16[1,1,64,128,128]{4,3,2,1,0:T(8,128)(2,1)}, u32[]{:S(2)}) copy-start(bf16[1,1,64,128,128]{4,3,2,1,0:T(8,128)(2,1)} %param.8) | copy-start | bytes 6291460
  119.4 12.4 %all-to-all-start.7 = ((f32[32,1,128]{2,1,0:T(1,128)}), f32[32,1,128]{2,1,0:T(1,128)S(1)}, u32[]{:S(2)}, u32[]{:S(2)}) async-start(f32[32,1,128]{2,1,0:T(1,128)} %bitcast.18), calls=%async_computation.7 | async-start | bytes 32768 | tf_op jit(solution)/shard_map/all_to_all | solution.py:353

commit v7 on v6

--- a/solution.py
+++ b/solution.py
@@ -9,6 +9,8 @@
 
 TILE = 128
 LANE = 8
+LOW = LANE - 1
+BITS = 3
 HALF = 4
 SCALE = 1024.0
 F32 = jnp.float32
@@ -37,15 +39,19 @@
     return dot(select, high) + dot(select, low)
 
 
-def place_of(owner):
+def place_of(owner, column):
     count = owner.shape[1]
     shape = (count, count)
     down, across = iota(shape, 0), iota(shape, 1)
-    column = jnp.sum(jnp.where(down == across, owner, 0.0), axis=1, keepdims=True)
     same = column == owner
-    rank_row = jnp.sum(jnp.where(same & (down < across), 1.0, 0.0), axis=0, keepdims=True)
-    rank_column = jnp.sum(jnp.where(same & (across < down), 1.0, 0.0), axis=1, keepdims=True)
-    return (owner * LANE + rank_row).astype(jnp.int32), (column * LANE + rank_column).astype(jnp.int32)
+    rank_row = jnp.sum(jnp.where(same & (down < across), 1, 0), axis=0, keepdims=True)
+    rank_column = jnp.sum(jnp.where(same & (across < down), 1, 0), axis=1, keepdims=True)
+    return owner * LANE + rank_row, column * LANE + rank_column
+
+
+def columns_of(slots):
+    twice = jnp.concatenate([slots, slots], axis=1).astype(F32)
+    return twice.T[: slots.shape[1], :].astype(jnp.int32)
 
 
 def request_kernel(pieces, planes, slots, both, ask):
@@ -55,55 +61,64 @@
     count = slots.shape[1]
     width = ask.shape[0]
     spot = iota((width, count), 0)
-    col = jnp.zeros((width, 1), F32)
-    row = [[None, None], [None, None]]
+    quarter = iota((TILE, count), 0) >> 4
+    col = row = jnp.zeros((width, TILE), F32)
     riders = []
+
+    def spread(there, value):
+        there = jnp.where(there, 1.0, 0.0).astype(BF16)
+        rest = value & 15
+        dims = (((1,), (1,)), ((), ()))
+        return sum(
+            lax.dot_general(there, part.astype(F32).astype(BF16), dims, preferred_element_type=F32)
+            for part in (value - rest, rest)
+        )
+
+    columns = columns_of(both[...])
     for core in range(2):
         own_r, blk_r, own_c, blk_c, filled = [both[8 * core + k : 8 * core + k + 1, :] for k in range(5)]
         alive = iota((1, count), 1) < filled
-        place = place_of(own_r.astype(F32))[0] + HALF * core
-        value = jnp.where(alive, blk_r + 1, 0).astype(F32)
-        col = col + jnp.sum(jnp.where(spot == place, value, 0.0), axis=1, keepdims=True)
-        place = place_of(own_c.astype(F32))[0]
-        rank, chip = place % LANE, own_c // 2
-        value = jnp.where(alive, blk_c + 1, 0).astype(F32)
-        for side in range(2):
-            there = (spot == (chip * n_x + x) * LANE + rank) & (own_c % 2 == side)
-            row[core][side] = jnp.sum(jnp.where(there, value, 0.0), axis=1, keepdims=True)
+        place = place_of(own_r, columns[:, 8 * core : 8 * core + 1])[0] + HALF * core
+        value = jnp.broadcast_to(jnp.where(alive, blk_r + 1, 0), (TILE, count))
+        col = col + spread(spot == place, value)
+        place = place_of(own_c, columns[:, 8 * core + 2 : 8 * core + 3])[0]
+        rank, chip = place & LOW, own_c >> 1
+        here = ((quarter >> 1) == core) & ((quarter & 1) == (own_c & 1))
+        value = jnp.where(here, jnp.where(alive, blk_c + 1, 0), 0)
+        row = row + spread(spot == (chip * n_x + x) * LANE + rank, value)
         riders.append((alive, own_c, blk_c, place))
     lane = iota((width, TILE), 1)
     down = iota((width, TILE), 0)
-    quarter = lane // 16
-    values = jnp.broadcast_to(row[0][0], (width, TILE))
-    for k in range(1, 4):
-        values = jnp.where(quarter == k, row[k // 2][k % 2], values)
-    values = values.astype(jnp.int32) - 1
+    values = row.astype(jnp.int32) - 1
     for core, (alive, own_c, blk_c, place) in enumerate(riders):
         ident = jnp.where(alive, own_c * pieces + blk_c, -1)
         for k, rider in ((core, ident), (2 + core, place)):
             twice = jnp.concatenate([rider, rider], axis=1)
-            values = jnp.where((lane >= count) & (down % LANE == k), twice, values)
-    values = jnp.where(down // LANE % n_x == x, values, -9)
-    ask[...] = jnp.where(me % 2 == 0, jnp.broadcast_to(col, (width, TILE)).astype(jnp.int32) - 1, values)
-
-
-def local_kernel(pieces, slots, vector, tiles, pick_row, put_row, pick_col, put_col, pick_pair, mine, energy):
-    own_r, blk_r, own_c, blk_c, filled = [slots[k : k + 1, :] for k in range(5)]
+            values = jnp.where((lane >= count) & ((down & LOW) == k), twice, values)
+    values = jnp.where((down >> BITS) % n_x == x, values, -9)
+    ask[...] = jnp.where((me & 1) == 0, col.astype(jnp.int32) - 1, values)
+
+
+def local_kernel(
+    pieces, slots, vector, tiles, pick_row, put_row, pick_col, put_col, pick_pair, mine, energy, turned
+):
+    own_c = slots[2:3, :]
     count = slots.shape[1]
-    for owner, pick, put, shift in ((own_c, pick_row, put_row, 0), (own_r, pick_col, put_col, HALF)):
+    columns = columns_of(slots[...])
+    for k, pick, put, shift in ((2, pick_row, put_row, 0), (0, pick_col, put_col, HALF)):
         width = put.shape[0]
-        across, down = place_of(owner.astype(F32))
+        across, down = place_of(slots[k : k + 1, :], columns[:, k : k + 1])
         pick[...] = jnp.where(iota((count, width), 1) == down, 1.0, 0.0).astype(BF16)
         put[...] = jnp.where(iota((width, count), 0) == across + shift, 1.0, 0.0).astype(BF16)
-    ident = jnp.where(iota((1, count), 1) < filled, own_c * pieces + blk_c, -2)
-    across = iota((count, count), 0) == iota((count, count), 1)
-    down = jnp.sum(jnp.where(across, ident.astype(F32), 0.0), axis=1, keepdims=True).astype(jnp.int32)
-    mine[...] = jnp.broadcast_to(down, mine.shape)
-    place = place_of(own_c.astype(F32))[1]
-    high = place + place // LANE * LANE
+    ident = jnp.where(iota((count, 1), 0) < columns[:, 4:5], columns[:, 2:3] * pieces + columns[:, 3:4], -2)
+    mine[...] = jnp.broadcast_to(ident, mine.shape)
+    place = place_of(own_c, columns[:, 2:3])[1]
+    high = place + (place & ~LOW)
     pick_pair[...] = jnp.where(iota(pick_pair.shape, 1) == high, 1.0, 0.0).astype(BF16)
     v = vector[...] * SCALE
     energy[...] = jnp.sum((v * v).reshape(-1, 8, TILE), axis=0)
+    for t in range(tiles.shape[0]):
+        turned[t] = tiles[t].T
 
 
 def first_lane(asked):
@@ -122,7 +137,7 @@
 
 def served_kernel(n_x, slots, pair, vector, squares, asked_row, asked_col, out, energy):
     me = slots[5:6, 0:1]
-    first = me % 2 == 0
+    first = (me & 1) == 0
     width = asked_col.shape[0]
     col = pair[:width, :].reshape(-1, LANE, TILE)
     swapped = jnp.concatenate([col[:, HALF:, :], col[:, :HALF, :]], axis=1)
@@ -136,7 +151,7 @@
     for core in range(2):
         sides = [jnp.broadcast_to(row[:, :, 16 * k : 16 * k + 1], row.shape) for k in (2 * core, 2 * core + 1)]
         value = jnp.where(first.reshape(1, 1, 1), sides[0], sides[1])
-        riders = jnp.where(slot % 2 == 0, row[:, core : core + 1, :], row[:, 2 + core : 3 + core, :])
+        riders = jnp.where((slot & 1) == 0, row[:, core : core + 1, :], row[:, 2 + core : 3 + core, :])
         count = TILE // 2
         mixed = jnp.where(lane >= count, riders, jnp.where(lane == count - 1, me.reshape(1, 1, 1), value))
         asked.append(value)
@@ -153,7 +168,7 @@
     for k in range(width // TILE):
         part = asked_col[k * TILE : (k + 1) * TILE, :].astype(F32).T[0:1, :]
         lane = iota((1, TILE), 1)
-        rows.append(jnp.where(lane % LANE >= HALF, part, -2.0))
+        rows.append(jnp.where((lane & LOW) >= HALF, part, -2.0))
     return [row.astype(jnp.int32) for row in rows]
 
 
@@ -171,7 +186,7 @@
     ident = jnp.where(served_col < 0, -3, served_col + index * pieces)
     lane = iota((1, TILE), 1)
     slot = iota(owned.shape[:1] + (TILE,), 0)
-    half = iota(owned.shape[:1] + (TILE,), 1) // count
+    half = jnp.where(iota(owned.shape[:1] + (TILE,), 1) < count, 0, 1)
     for k in range(asked_row.shape[0] // (2 * LANE)):
         start = 2 * k * LANE
         even = [asked_row[start + j : start + j + 1, :] for j in range(2)]
@@ -180,40 +195,37 @@
         cols = slice(k * TILE, (k + 1) * TILE)
         link[:, cols] = jnp.where(mine[...] == ids, 1.0, 0.0).astype(BF16)
         link_col[:, cols] = jnp.where(ident == ids, 1.0, 0.0).astype(BF16)
-        sent = (spots == index * LANE + slot % LANE) & (slot // LANE == 2 * k + half)
+        sent = (spots == index * LANE + (slot & LOW)) & ((slot >> BITS) == 2 * k + half)
         owned[:, cols] = jnp.where(sent, 1.0, 0.0).astype(BF16)
 
 
-def multiply(x, tiles, across):
+def multiply(x, tiles):
     count = x.shape[0]
-    dims = (((1,), (1 if across else 0,)), ((), ()))
-    row = iota((8, TILE), 0)
+    row = iota((16, TILE), 0) & 7
     groups = []
     for g in range(count // 8):
         part = x[g * 8 : (g + 1) * 8, :]
         high = part.astype(BF16).astype(F32)
-        both = jnp.concatenate([high, part - high], axis=0).astype(BF16)
-        total = jnp.zeros((8, TILE), F32)
-        for j in range(8):
-            y = lax.dot_general(both, tiles[g * 8 + j], dims, preferred_element_type=F32)
-            total = jnp.where(row == j, y[0:8] + y[8:16], total)
-        groups.append(total)
+        both = jnp.concatenate([high, part - high], axis=0)
+        apart = jnp.concatenate([jnp.where(row == j, both, 0.0).astype(BF16) for j in range(8)], axis=1)
+        y = dot(apart, tiles[g * 8 : (g + 1) * 8].reshape(8 * TILE, TILE))
+        groups.append(y[0:8] + y[8:16])
     return jnp.concatenate(groups, axis=0)
 
 
 def direct_kernel(
     got, pick, tiles, put, asked_row, asked_col, mine, vector, out, v_col, meet, link, link_col, owned
 ):
-    y = multiply(exact_dot(pick[...], got[...]), tiles, True)
+    y = multiply(exact_dot(pick[...], got[...]), tiles)
     v = gather(asked_col[...], vector[...] * SCALE)
     v_col[...] = v
-    forward = iota(v.shape, 0) % LANE < HALF
+    forward = (iota(v.shape, 0) & LOW) < HALF
     out[...] = exact_dot(put[...], y) + jnp.where(forward, v, 0.0)
     meet_tables(asked_row, asked_col, mine, vector.shape[0], meet, link, link_col, owned)
 
 
 def mirror_kernel(got, pick, tiles, put, meet, out):
-    y = multiply(exact_dot(pick[...], got[...]), tiles, False)
+    y = multiply(exact_dot(pick[...], got[...]), tiles)
     high, low = halves(y)
     width = put.shape[0]
     total = exact_dot(meet[:width, width:], got[...])
@@ -230,18 +242,18 @@
     peers = range(got.shape[0])
     mirrors = jnp.concatenate([got[k, :count, :] for k in peers], axis=0)
     sums = jnp.concatenate([got[k, count:, :] for k in peers], axis=0)
-    y = multiply(dot(link[...], mirrors) + dot(pick[...], sums), tiles, True)
+    y = multiply(dot(link[...], mirrors) + dot(pick[...], sums), tiles)
     width = got.shape[0] * LANE
     image = dot(link_col[...], mirrors) + exact_dot(meet[width:, width:], first_col[...])
-    forward = iota(image.shape, 0) % LANE < HALF
+    forward = (iota(image.shape, 0) & LOW) < HALF
     out[...] = exact_dot(put[...], y) + jnp.where(forward, image, 0.0)
     slot = iota((width, 2 * width), 0)
-    low = iota((width, 2 * width), 1) == slot + slot // LANE * LANE + LANE
+    low = iota((width, 2 * width), 1) == slot + (slot & ~LOW) + LANE
     first_row[...] = dot(owned[...], mirrors) + dot(jnp.where(low, 1.0, 0.0).astype(BF16), sums)
 
 
 def second_mirror_kernel(got, pick, tiles, put, out):
-    out[...] = exact_dot(put[...], multiply(exact_dot(pick[...], got[...]), tiles, False))
+    out[...] = exact_dot(put[...], multiply(exact_dot(pick[...], got[...]), tiles))
 
 
 def inner_kernel(meet, energy, v_row, v_col, first_row, second_row, first_col, second_col, out):
@@ -251,7 +263,7 @@
     both = exact_dot(meet[...], jnp.concatenate([first, second], axis=1))
     image, total = both[:, :TILE], both[:, TILE:]
     width = v_row.shape[0]
-    returned = iota(v_col.shape, 0) % LANE >= HALF
+    returned = (iota(v_col.shape, 0) & LOW) >= HALF
     first_c = jnp.where(returned, first_col[...], 0.0)
     second_c = jnp.where(returned, second_col[...], 0.0)
 
@@ -300,18 +312,23 @@
         return jnp.sum(jnp.where(lane == k, sums, 0.0), axis=1, keepdims=True)
 
     vv, vi, ii, vw, iw, ww = [value(k) for k in range(6)]
-    g = 1.0 / (SCALE * jnp.sqrt(vv / (total * SCALE * SCALE) + 1e-06))
-    c0 = g * (g * vi / total)
-    square = g * (g * (ii - 2.0 * c0 * vi + c0 * c0 * vv) / total)
-    b0 = jnp.sqrt(jnp.maximum(square, 0.0) + 1e-06)
-    h = g / b0
-    c10 = h * (g * (vw - c0 * vi) / total)
-    c11 = h * (h * (iw - c0 * ii - c0 * vw + c0 * c0 * vi) / total)
+    share = 1.0 / total
+    g = lax.rsqrt(vv * (share / (SCALE * SCALE)) + 1e-06) * (1.0 / SCALE)
+    c0 = g * (g * vi * share)
+    square = g * (g * (ii - 2.0 * c0 * vi + c0 * c0 * vv) * share)
+    square = jnp.maximum(square, 0.0) + 1e-06
+    root = lax.rsqrt(square)
+    b0 = square * root
+    h = g * root
+    c10 = h * (g * (vw - c0 * vi) * share)
+    c11 = h * (h * (iw - c0 * ii - c0 * vw + c0 * c0 * vi) * share)
     a = c0 + c11
     b = c11 * c0 - c10 * b0
-    square = h * (h * (ww + a * a * ii + b * b * vv - 2.0 * a * iw + 2.0 * b * vw - 2.0 * a * b * vi) / total)
-    b1 = jnp.sqrt(jnp.maximum(square, 0.0) + 1e-06)
-    f = h / b1
+    square = h * (h * (ww + a * a * ii + b * b * vv - 2.0 * a * iw + 2.0 * b * vw - 2.0 * a * b * vi) * share)
+    square = jnp.maximum(square, 0.0) + 1e-06
+    root = lax.rsqrt(square)
+    b1 = square * root
+    f = h * root
     parts = sems.shape[0]
     step = vector.shape[0] // parts
     copies = []
@@ -400,7 +417,7 @@
         axis_index_groups=planes,
         tiled=True,
     ).reshape(wide_c, TILE)
-    pick_row, put_row, pick_col, put_col, pick_pair, mine, squares = call(
+    pick_row, put_row, pick_col, put_col, pick_pair, mine, squares, turned = call(
         functools.partial(local_kernel, pieces),
         (
             shape(count, wide_r, dtype=BF16),
@@ -410,6 +427,7 @@
             shape(count, 2 * wide_r, dtype=BF16),
             shape(count, TILE, dtype=jnp.int32),
             shape(8, TILE),
+            shape(*tiles.shape, dtype=BF16),
         ),
         slots,
         vector,
@@ -441,7 +459,7 @@
         ),
         x_col,
         pick_row,
-        tiles,
+        turned,
         put_col,
         asked_row,
         asked_col,
@@ -468,7 +486,7 @@
         pick_pair,
         meet,
         first_col,
-        tiles,
+        turned,
         put_col,
     )
     second_col = over_col(second_col)
@@ -494,7 +512,7 @@
         image,
         second,
         out_specs=(HBM, SMEM, SMEM),
-        scratch=[pltpu.VMEM((2 * pieces, TILE), F32), pltpu.SemaphoreType.DMA((4,))],
+        scratch=[pltpu.VMEM((2 * pieces, TILE), F32), pltpu.SemaphoreType.DMA((8,))],
     )
     basis = out.reshape(pieces, 2, TILE).transpose(1, 0, 2).reshape(2, pieces * TILE)
     return (basis, alpha, rest)

time: 134 us -> 132 us (0.985)
  Pallas kernels: 12.1 us -> 10.6 us
    pallas_call x11, Pallas kernels: 12.1 us -> 10.6 us  [call(): pl.pallas_call(kernel, out_shape=outs, in_specs=[ins] * len(args), out_sp...]
  transfers between devices with their start and end apart: 2 -> 2, of which waited for: 2 -> 2; matrix products, arithmetic and copies ran while one was open for 0% -> 0% of each run, Pallas kernels for 1% -> 2%
where the time goes in v7:
time: 132 us
  blocking collectives  95 us (72%)
  waiting for transfers between devices  13 us (10%)
  Pallas kernels  10.6 us (8%)
  starting transfers between devices  8.12 us (6%)
  local copies, waits for them, and re-layouts  3.47 us (3%)
  between operations  1.4 us (1%)
    all_to_all x6, blocking collectives, exchange(): got = lax.all_to_all(sent, axis, split_axis=0, concat_axis=0, tiled=True)  80.3 us
    all_gather x2, blocking collectives, over_chip(): return lax.all_gather(x, 'row', axis_index_groups=chips, tiled=True)  14.7 us
    pallas_call x11, Pallas kernels, call(): pl.pallas_call(kernel, out_shape=outs, in_specs=[ins] * len(args), out_sp...  10.6 us
    all_to_all x1, waiting for transfers between devices, exchange(): got = lax.all_to_all(sent, axis, split_axis=0, concat_axis=0, tiled=True)  7.45 us
    all_to_all x1, waiting for transfers between devices, per_device(): lax.all_to_all(ask.reshape(n_col, LANE, TILE), ('row', 'col'), split_axis...  5.55 us
    all_to_all x1, starting transfers between devices, per_device(): lax.all_to_all(ask.reshape(n_col, LANE, TILE), ('row', 'col'), split_axis...  4.3 us
    all_to_all x1, starting transfers between devices, exchange(): got = lax.all_to_all(sent, axis, split_axis=0, concat_axis=0, tiled=True)  3.83 us
    unnamed x8, local copies, waits for them, and re-layouts  2.73 us
  transfers between devices with their start and end apart: 2, of which 2 were waited for; matrix products, arithmetic and copies ran while one was open for 0% of the time, Pallas kernels for 2%

profile of v7, /device:TPU:1, one launch (start us, length us, event | category | flops | bytes accessed | tf_op | source)
XLA Modules:
  0.0 131.6 jit_solution(6579308226586236024)
XLA Ops:
  1.3 0.7 concatenate.3.slots
  2.1 8.4 %all_gather.6.both = s32[16,64]{1,0:T(8,128)S(1)} all-gather(s32[8,64]{1,0:T(8,128)S(1)} %concatenate.3.slots), channel_id=1, replica_groups={{0,32},{64,96},{128,160},{192,224},{256,288},{320,352},{384,416},{448,4..., dimensions={0}, use_global_device_ids=true | all-gather | bytes 6144 | tf_op jit(solution)/shard_map/all_gather | solution.py:404
  10.4 1.3 shard_map.94
  11.7 4.3 %all-to-all-start = ((s32[32,8,128]{2,1,0:T(8,128)}), s32[32,8,128]{2,1,0:T(8,128)S(1)}, u32[]{:S(2)}, u32[]{:S(2)}) async-start(s32[32,8,128]{2,1,0:T(8,128)} %bitcast.5), calls=%async_computation | async-start | bytes 262144 | tf_op jit(solution)/shard_map/all_to_all | solution.py:412
  16.0 0.0 copy-start
  16.0 1.6 %copy-done = bf16[1,1,64,128,128]{4,3,2,1,0:T(8,128)(2,1)S(1)} copy-done((bf16[1,1,64,128,128]{4,3,2,1,0:T(8,128)(2,1)S(1)}, bf16[1,1,64,128,128]{4,3,2,1,0:T(8,128)(2,1)}, u32[]{:S(2)}) %copy-start) | copy-done | bytes 2097176
  17.6 0.0 copy-start.2
  17.6 1.1 copy-done.2
  18.7 0.0 copy-start.3
  18.7 1.1 shard_map.95
  19.8 5.5 %all-to-all-done = s32[32,8,128]{2,1,0:T(8,128)S(1)} async-done(((s32[32,8,128]{2,1,0:T(8,128)}), s32[32,8,128]{2,1,0:T(8,128)S(1)}, u32[]{:S(2)}, u32[]{:S(2)}) %all-to-all-start) | async-done | bytes 131104 | tf_op jit(solution)/shard_map/all_to_all | solution.py:412
  25.3 6.4 %all_gather.7.pair = s32[512,128]{1,0:T(8,128)S(1)} all-gather(s32[256,128]{1,0:T(8,128)S(1)} %bitcast.49), channel_id=1, replica_groups={{0,32},{64,96},{128,160},{192,224},{256,288},{320,352},{384,416},{448,4..., dimensions={0}, use_global_device_ids=true | all-gather | bytes 393216 | tf_op jit(solution)/shard_map/all_gather | solution.py:404
  31.7 0.0 copy-done.3
  31.7 0.5 shard_map.96
  32.2 0.0 copy-start.1
  32.2 15.2 %all_to_all.40 = f32[16,8,128]{2,1,0:T(8,128)S(1)} all-to-all(f32[16,8,128]{2,1,0:T(8,128)S(1)} %bitcast.43), channel_id=1, replica_groups=mesh['row'=16,'col'=32] {'row'}, dimensions={0} | all-to-all | bytes 131072 | tf_op jit(solution)/shard_map/all_to_all | solution.py:370
  47.4 1.4 %shard_map.97 = (f32[256,128]{1,0:T(8,128)S(1)}, f32[256,128]{1,0:T(8,128)S(1)}, bf16[384,384]{1,0:T(8,128)(2,1)S(1)}, bf16[64,1024]{1,0:T(8,128)(2,1)S(1)}, bf1...) custom-call(f32[128,128]{1,0:T(8,128)S(1)} %bitcast.44, bf16[64,128]{1,0:T(8,128)(2,1)S(1)} %get-tuple-element.30.pick, ...), custom_call_target="tpu_custom_call" | custom-call | tf_op jit(solution)/shard_map/pallas_call | solution.py:358
  48.8 12.4 %all_to_all.41 = f32[32,8,128]{2,1,0:T(8,128)S(1)} all-to-all(f32[32,8,128]{2,1,0:T(8,128)S(1)} %bitcast.46), channel_id=1, replica_groups=mesh['row'=16,'col'=32] {'col'}, dimensions={0} | all-to-all | bytes 262144 | tf_op jit(solution)/shard_map/all_to_all | solution.py:370
  61.2 0.0 copy-done.1
  61.2 0.6 shard_map.98
  61.9 17.6 %all_to_all.42.got = bf16[16,80,128]{2,1,0:T(8,128)(2,1)S(1)} all-to-all(bf16[16,80,128]{2,1,0:T(8,128)(2,1)S(1)} %shard_map.98), channel_id=1, replica_groups=mesh['row'=16,'col'=32] {'row'}, dimensions={0} | all-to-all | bytes 655360 | tf_op jit(solution)/shard_map/all_to_all | solution.py:370
  79.4 0.9 shard_map.99
  80.4 12.9 %all_to_all.43 = f32[32,8,128]{2,1,0:T(8,128)S(1)} all-to-all(f32[32,8,128]{2,1,0:T(8,128)S(1)} %bitcast.47), channel_id=1, replica_groups=mesh['row'=16,'col'=32] {'col'}, dimensions={0} | all-to-all | bytes 262144 | tf_op jit(solution)/shard_map/all_to_all | solution.py:370
  93.3 0.7 shard_map.100
  94.0 11.8 %all_to_all.44 = f32[16,8,128]{2,1,0:T(8,128)S(1)} all-to-all(f32[16,8,128]{2,1,0:T(8,128)S(1)} %bitcast.45), channel_id=1, replica_groups=mesh['row'=16,'col'=32] {'row'}, dimensions={0} | all-to-all | bytes 131072 | tf_op jit(solution)/shard_map/all_to_all | solution.py:370
  105.8 0.4 shard_map.101
  106.2 10.4 %all_to_all.45.got = f32[16,8,128]{2,1,0:T(8,128)S(1)} all-to-all(f32[16,8,128]{2,1,0:T(8,128)S(1)} %shard_map.101), channel_id=1, replica_groups=mesh['row'=16,'col'=32] {'row'}, dimensions={0} | all-to-all | bytes 131072 | tf_op jit(solution)/shard_map/all_to_all | solution.py:370
  116.6 0.7 shard_map.102
  117.3 3.8 %all-to-all-start.7 = ((f32[32,1,128]{2,1,0:T(1,128)}), f32[32,1,128]{2,1,0:T(1,128)S(1)}, u32[]{:S(2)}, u32[]{:S(2)}) async-start(f32[32,1,128]{2,1,0:T(1,128)} %bitcast.18), calls=%async_computation.7 | async-start | bytes 32768 | tf_op jit(solution)/shard_map/all_to_all | solution.py:370
  121.1 1.1 shard_map.103
  122.2 7.5 %all-to-all-done.7 = f32[32,1,128]{2,1,0:T(1,128)S(1)} async-done(((f32[32,1,128]{2,1,0:T(1,128)}), f32[32,1,128]{2,1,0:T(1,128)S(1)}, u32[]{:S(2)}, u32[]{:S(2)}) %all-to-all-start.7) | async-done | bytes 16416 | tf_op jit(solution)/shard_map/all_to_all | solution.py:370
  129.7 1.9 %shard_map.104 = (f32[3072,128]{1,0:T(8,128)}, f32[1]{0:T(128)}, f32[3]{0:T(128)}) custom-call(f32[32,128]{1,0:T(8,128)S(1)} %bitcast.48, f32[1536,128]{1,0:T(8,128)S(1)} %bitcast.33, f32[1536,128]{1,0:T(8,128)S(1)} %get-tuple-element.48.refs_2_, f32[1536,128]{1,0:T(8,128)S(1)} %get-tuple-element.49.refs_3_), custom_call_target="tpu_custom_call" | custom-call | tf_op jit(solution)/shard_map/pallas_call | solution.py:358
  (4 shorter events, 0.0 us)
Async XLA Ops:
  11.7 13.7 %all-to-all-start = ((s32[32,8,128]{2,1,0:T(8,128)}), s32[32,8,128]{2,1,0:T(8,128)S(1)}, u32[]{:S(2)}, u32[]{:S(2)}) async-start(s32[32,8,128]{2,1,0:T(8,128)} %bitcast.5), calls=%async_computation | async-start | bytes 262144 | tf_op jit(solution)/shard_map/all_to_all | solution.py:412
  16.0 1.6 %copy-start = (bf16[1,1,64,128,128]{4,3,2,1,0:T(8,128)(2,1)S(1)}, bf16[1,1,64,128,128]{4,3,2,1,0:T(8,128)(2,1)}, u32[]{:S(2)}) copy-start(bf16[1,1,64,128,128]{4,3,2,1,0:T(8,128)(2,1)} %param.8) | copy-start | bytes 6291460
  17.6 1.1 copy-start.2
  18.7 13.0 %copy-start.3 = (f32[196608]{0:T(1024)S(1)}, f32[196608]{0:T(1024)}, u32[]{:S(2)}) copy-start(f32[196608]{0:T(1024)} %param.7) | copy-start | bytes 2359300
  32.2 29.1 %copy-start.1 = (bf16[1,1,64,128,128]{4,3,2,1,0:T(8,128)(2,1)S(1)}, bf16[1,1,64,128,128]{4,3,2,1,0:T(8,128)(2,1)}, u32[]{:S(2)}) copy-start(bf16[1,1,64,128,128]{4,3,2,1,0:T(8,128)(2,1)} %param.8) | copy-start | bytes 6291460
  117.3 12.4 %all-to-all-start.7 = ((f32[32,1,128]{2,1,0:T(1,128)}), f32[32,1,128]{2,1,0:T(1,128)S(1)}, u32[]{:S(2)}, u32[]{:S(2)}) async-start(f32[32,1,128]{2,1,0:T(1,128)} %bitcast.18), calls=%async_computation.7 | async-start | bytes 32768 | tf_op jit(solution)/shard_map/all_to_all | solution.py:370

commit v8 on v7

--- a/solution.py
+++ b/solution.py
@@ -49,70 +49,74 @@
     return owner * LANE + rank_row, column * LANE + rank_column
 
 
-def columns_of(slots):
-    twice = jnp.concatenate([slots, slots], axis=1).astype(F32)
-    return twice.T[: slots.shape[1], :].astype(jnp.int32)
-
-
-def request_kernel(pieces, planes, slots, both, ask):
+def columns_of(rows):
+    rows = rows + [jnp.zeros_like(rows[0])] * (8 - len(rows))
+    return jnp.concatenate(rows, axis=0).astype(F32).T.astype(jnp.int32)
+
+
+def request_kernel(pieces, planes, both, me, col, ask):
     n_x, n_z = planes
-    me = slots[5:6, 0:1]
-    x = slots[6:7, 0:1] // n_z
-    count = slots.shape[1]
+    first = (jnp.full((1, 1), me[0], jnp.int32) & 1) == 0
+    x = col[0] // n_z
+    count = both.shape[1]
     width = ask.shape[0]
-    spot = iota((width, count), 0)
-    quarter = iota((TILE, count), 0) >> 4
-    col = row = jnp.zeros((width, TILE), F32)
-    riders = []
-
-    def spread(there, value):
-        there = jnp.where(there, 1.0, 0.0).astype(BF16)
-        rest = value & 15
-        dims = (((1,), (1,)), ((), ()))
-        return sum(
-            lax.dot_general(there, part.astype(F32).astype(BF16), dims, preferred_element_type=F32)
-            for part in (value - rest, rest)
-        )
-
-    columns = columns_of(both[...])
-    for core in range(2):
-        own_r, blk_r, own_c, blk_c, filled = [both[8 * core + k : 8 * core + k + 1, :] for k in range(5)]
-        alive = iota((1, count), 1) < filled
-        place = place_of(own_r, columns[:, 8 * core : 8 * core + 1])[0] + HALF * core
-        value = jnp.broadcast_to(jnp.where(alive, blk_r + 1, 0), (TILE, count))
-        col = col + spread(spot == place, value)
-        place = place_of(own_c, columns[:, 8 * core + 2 : 8 * core + 3])[0]
-        rank, chip = place & LOW, own_c >> 1
-        here = ((quarter >> 1) == core) & ((quarter & 1) == (own_c & 1))
-        value = jnp.where(here, jnp.where(alive, blk_c + 1, 0), 0)
-        row = row + spread(spot == (chip * n_x + x) * LANE + rank, value)
-        riders.append((alive, own_c, blk_c, place))
-    lane = iota((width, TILE), 1)
+    lane = iota((1, TILE), 1)
+    core = jnp.where(lane < count, 0, 1)
+
+    owner_r, block_r, owner_c, block_c, filled = [
+        jnp.concatenate([both[k : k + 1, :], both[8 + k : 9 + k, :]], axis=1) for k in range(5)
+    ]
+    alive = lane - core * count < filled
+    tags = [owner_r + core * count, owner_c + core * count]
+    columns = columns_of(tags)
+    earlier = iota((TILE, TILE), 0) < iota((TILE, TILE), 1)
+    rank_r, rank_c = [
+        jnp.sum(jnp.where((columns[:, k : k + 1] == tag) & earlier, 1, 0), axis=0, keepdims=True)
+        for k, tag in enumerate(tags)
+    ]
+    place = owner_c * LANE + rank_c
+    spot = jnp.where(
+        first, owner_r * LANE + rank_r + core * HALF, ((owner_c >> 1) * n_x + x) * LANE + rank_c
+    )
+    quarter = iota((TILE, TILE), 0) >> 4
+    here = ((quarter >> 1) == core) & ((quarter & 1) == (owner_c & 1)) & alive
+    value = jnp.where(first, jnp.where(alive, block_r + 1, 0), jnp.where(here, block_c + 1, 0))
+    there = jnp.where(iota((width, TILE), 0) == spot, 1.0, 0.0).astype(BF16)
+    rest = value & 15
+    dims = (((1,), (1,)), ((), ()))
+    total = sum(
+        lax.dot_general(there, part.astype(F32).astype(BF16), dims, preferred_element_type=F32)
+        for part in (value - rest, rest)
+    )
+    total = total.astype(jnp.int32) - 1
+    ident = jnp.where(alive, owner_c * pieces + block_c, -1)
     down = iota((width, TILE), 0)
-    values = row.astype(jnp.int32) - 1
-    for core, (alive, own_c, blk_c, place) in enumerate(riders):
-        ident = jnp.where(alive, own_c * pieces + blk_c, -1)
-        for k, rider in ((core, ident), (2 + core, place)):
-            twice = jnp.concatenate([rider, rider], axis=1)
-            values = jnp.where((lane >= count) & ((down & LOW) == k), twice, values)
-    values = jnp.where((down >> BITS) % n_x == x, values, -9)
-    ask[...] = jnp.where((me & 1) == 0, col.astype(jnp.int32) - 1, values)
+    slot = down & LOW
+    ids = jnp.where(slot == 0, pltpu.roll(ident, count, 1), ident)
+    places = jnp.where(slot == 2, pltpu.roll(place, count, 1), place)
+    riders = jnp.where(slot < 2, ids, places)
+    full = jnp.where((lane >= count) & (slot < 4), riders, total)
+    full = jnp.where((down >> BITS) % n_x == x, full, -9)
+    ask[...] = jnp.where(first, total, full)
 
 
 def local_kernel(
-    pieces, slots, vector, tiles, pick_row, put_row, pick_col, put_col, pick_pair, mine, energy, turned
+    pieces, both, me, vector, tiles,
+    pick_row, put_row, pick_col, put_col, pick_pair, mine, energy, turned,
 ):
-    own_c = slots[2:3, :]
-    count = slots.shape[1]
-    columns = columns_of(slots[...])
-    for k, pick, put, shift in ((2, pick_row, put_row, 0), (0, pick_col, put_col, HALF)):
+    first = (jnp.full((1, 1), me[0], jnp.int32) & 1) == 0
+    count = both.shape[1]
+    slots = [jnp.where(first, both[k : k + 1, :], both[8 + k : 9 + k, :]) for k in (0, 2, 3)]
+    live = jnp.where(first, both[4:5, 0:1], both[12:13, 0:1])
+    columns = columns_of([jnp.concatenate([row, row], axis=1) for row in slots])[:count, :]
+    for k, pick, put, shift in ((1, pick_row, put_row, 0), (0, pick_col, put_col, HALF)):
         width = put.shape[0]
-        across, down = place_of(slots[k : k + 1, :], columns[:, k : k + 1])
+        across, down = place_of(slots[k], columns[:, k : k + 1])
         pick[...] = jnp.where(iota((count, width), 1) == down, 1.0, 0.0).astype(BF16)
         put[...] = jnp.where(iota((width, count), 0) == across + shift, 1.0, 0.0).astype(BF16)
-    ident = jnp.where(iota((count, 1), 0) < columns[:, 4:5], columns[:, 2:3] * pieces + columns[:, 3:4], -2)
+    ident = jnp.where(iota((count, 1), 0) < live, columns[:, 1:2] * pieces + columns[:, 2:3], -2)
     mine[...] = jnp.broadcast_to(ident, mine.shape)
-    place = place_of(own_c, columns[:, 2:3])[1]
+    place = place_of(slots[1], columns[:, 1:2])[1]
     high = place + (place & ~LOW)
     pick_pair[...] = jnp.where(iota(pick_pair.shape, 1) == high, 1.0, 0.0).astype(BF16)
     v = vector[...] * SCALE
@@ -135,8 +139,8 @@
     return exact_dot(select, vector)
 
 
-def served_kernel(n_x, slots, pair, vector, squares, asked_row, asked_col, out, energy):
-    me = slots[5:6, 0:1]
+def served_kernel(n_x, index, pair, vector, squares, asked_row, asked_col, out, energy):
+    me = jnp.full((1, 1), index[0], jnp.int32)
     first = (me & 1) == 0
     width = asked_col.shape[0]
     col = pair[:width, :].reshape(-1, LANE, TILE)
@@ -290,21 +294,15 @@
     out[...] = jnp.broadcast_to(packed, out.shape)
 
 
-def spread_kernel(asked_row, asked_col, first_row, second_row, first_col, second_col, image, second):
-    lanes = jnp.concatenate(product_lane(asked_row, asked_col), axis=1)
-    rows = jnp.concatenate([first_row[...], second_row[...]], axis=1)
-    columns = jnp.concatenate([first_col[...], second_col[...]], axis=1)
-    high, low = halves(jnp.concatenate([rows, columns], axis=0))
-    step = 256
-    for start in range(0, image.shape[0], step):
-        place = iota((step, lanes.shape[1]), 0) + start
-        select = jnp.where(place == lanes, 1.0, 0.0).astype(BF16)
-        both = dot(select, high) + dot(select, low)
-        image[start : start + step, :] = both[:, :TILE]
-        second[start : start + step, :] = both[:, TILE:]
-
-
-def final_kernel(total, got, vector, image, second, out, alpha, rest, near, sems):
+def returned_rows(x):
+    pairs = x.reshape(-1, 2, LANE, TILE)
+    return jnp.concatenate([pairs[:, 0, HALF:, :], pairs[:, 1, HALF:, :]], axis=1).reshape(-1, TILE)
+
+
+def final_kernel(
+    total, got, vector, asked_row, asked_col, first_row, second_row, first_col, second_col,
+    out, alpha, rest, near, sems,
+):
     sums = jnp.sum(got[...], axis=0, keepdims=True)
     lane = iota((1, TILE), 1)
 
@@ -331,12 +329,20 @@
     f = h * root
     parts = sems.shape[0]
     step = vector.shape[0] // parts
+    asked = [first_lane(asked_row[...]), returned_rows(asked_col[...])]
+    lanes = jnp.concatenate([x.astype(F32).T[0:1, :].astype(jnp.int32) for x in asked], axis=1)
+    image = jnp.concatenate([first_row[...], returned_rows(first_col[...])], axis=0)
+    second = jnp.concatenate([second_row[...], returned_rows(second_col[...])], axis=0)
+    high, low = halves(jnp.concatenate([image, second], axis=1))
     copies = []
     for k in range(parts):
-        rows = pl.ds(k * step, step)
-        v, i = vector[rows, :], image[rows, :]
+        v = vector[pl.ds(k * step, step), :]
+        place = iota((step, lanes.shape[1]), 0) + k * step
+        select = jnp.where(place == lanes, 1.0, 0.0).astype(BF16)
+        both = dot(select, high) + dot(select, low)
+        i, w = both[:, :TILE], both[:, TILE:]
         near[pl.ds(2 * k * step, step, 2), :] = h * i - (h * c0 * SCALE) * v
-        near[pl.ds(2 * k * step + 1, step, 2), :] = f * second[rows, :] - (f * a) * i + (f * b * SCALE) * v
+        near[pl.ds(2 * k * step + 1, step, 2), :] = f * w - (f * a) * i + (f * b * SCALE) * v
         done = pl.ds(2 * k * step, 2 * step)
         copies.append(pltpu.make_async_copy(near.at[done], out.at[done], sems.at[k]))
         copies[-1].start()
@@ -358,7 +364,7 @@
     return pl.pallas_call(
         kernel,
         out_shape=outs,
-        in_specs=[ins] * len(args),
+        in_specs=ins if isinstance(ins, list) else [ins] * len(args),
         out_specs=out_specs,
         scratch_shapes=scratch,
         compiler_params=pltpu.CompilerParams(vmem_limit_bytes=limit * 1024 * 1024),
@@ -390,24 +396,24 @@
     n_y = n_row // 2
     n_x = n_col // n_y
     n_z = n_col // n_x
-    small = [row_owner, row_block, col_owner, col_block, tile_counts]
-    small += [lax.axis_index("row"), lax.axis_index("col"), jnp.zeros((), jnp.int32)]
-    slots = jnp.concatenate(
-        [jnp.broadcast_to(x.reshape(1, -1), (1, count)).astype(jnp.int32) for x in small], axis=0
-    )
     planes = [[2 * y * n_col + c for c in range(n_col)] for y in range(n_y)]
     planes += [[(2 * y + 1) * n_col + x * n_z + z for y in range(n_y) for x in range(n_x)] for z in range(n_z)]
-
     chips = [[2 * y, 2 * y + 1] for y in range(n_y)]
 
     def over_chip(x):
         return lax.all_gather(x, "row", axis_index_groups=chips, tiled=True)
 
+    slots = [row_owner, row_block, col_owner, col_block, tile_counts] + [jnp.zeros((), jnp.int32)] * 3
+    slots = jnp.concatenate([jnp.broadcast_to(x.reshape(1, -1), (1, count)) for x in slots], axis=0)
+    both = over_chip(slots)
+    me, col = lax.axis_index("row").reshape(1), lax.axis_index("col").reshape(1)
     ask = call(
         functools.partial(request_kernel, pieces, (n_x, n_z)),
         shape(wide_c, TILE, dtype=jnp.int32),
-        slots,
-        over_chip(slots),
+        both,
+        me,
+        col,
+        ins=[VMEM] + [SMEM] * 2,
     )
     ask = lax.all_to_all(
         ask.reshape(n_col, LANE, TILE),
@@ -429,9 +435,11 @@
             shape(8, TILE),
             shape(*tiles.shape, dtype=BF16),
         ),
-        slots,
+        both,
+        me,
         vector,
         tiles,
+        ins=[VMEM, SMEM] + [VMEM] * 2,
     )
     asked_row, asked_col, v_row, energy = call(
         functools.partial(served_kernel, n_x),
@@ -441,10 +449,11 @@
             shape(wide_r, TILE),
             shape(1, TILE),
         ),
-        slots,
+        me,
         over_chip(ask),
         vector,
         squares,
+        ins=[SMEM] + [VMEM] * 3,
     )
     x_col = over_row(v_row)
     first_col, v_col, meet, link, link_col, owned = call(
@@ -496,9 +505,6 @@
     products = (first_row, second_row, first_col, second_col)
     inner = call(inner_kernel, shape(n_row, 8, TILE), meet, energy, v_row, v_col, *products)
     inner = over_row(inner)
-    image, second = call(
-        spread_kernel, (shape(pieces, TILE), shape(pieces, TILE)), asked_row, asked_col, *products
-    )
     inner = over_col(call(partial_kernel, shape(n_col, TILE), inner))
 
     def finish(*refs):
@@ -509,8 +515,9 @@
         (shape(2 * pieces, TILE), shape(1), shape(3)),
         inner,
         vector,
-        image,
-        second,
+        asked_row,
+        asked_col,
+        *products,
         out_specs=(HBM, SMEM, SMEM),
         scratch=[pltpu.VMEM((2 * pieces, TILE), F32), pltpu.SemaphoreType.DMA((8,))],
     )

time: 132 us -> 131 us (level)
  blocking collectives: 95 us -> 107 us
  waiting for transfers between devices: 13 us -> 5.62 us
  starting transfers between devices: 8.12 us -> 4.3 us
  Pallas kernels: 10.6 us -> 8.93 us
    all_to_all x6 -> x7, blocking collectives: 80.3 us -> 92.3 us  [exchange(): got = lax.all_to_all(sent, axis, split_axis=0, concat_axis=0, tiled=True)]
    all_to_all x1 -> x0, waiting for transfers between devices: 7.45 us -> none  [exchange(): got = lax.all_to_all(sent, axis, split_axis=0, concat_axis=0, tiled=True)]
    all_to_all x1 -> x0, starting transfers between devices: 3.83 us -> none  [exchange(): got = lax.all_to_all(sent, axis, split_axis=0, concat_axis=0, tiled=True)]
    pallas_call x11 -> x10, Pallas kernels: 10.6 us -> 8.93 us  [call(): pl.pallas_call(kernel, out_shape=outs, in_specs=ins if isinstance(ins, li...]
  transfers between devices with their start and end apart: 2 -> 1, of which waited for: 2 -> 1; matrix products, arithmetic and copies ran while one was open for 0% -> 0% of each run, Pallas kernels for 2% -> 1%
where the time goes in v8:
time: 131 us
  blocking collectives  107 us (82%)
  Pallas kernels  8.93 us (7%)
  waiting for transfers between devices  5.62 us (4%)
  starting transfers between devices  4.3 us (3%)
  local copies, waits for them, and re-layouts  3.46 us (3%)
  between operations  1.38 us (1%)
    all_to_all x7, blocking collectives, exchange(): got = lax.all_to_all(sent, axis, split_axis=0, concat_axis=0, tiled=True)  92.3 us
    all_gather x2, blocking collectives, over_chip(): return lax.all_gather(x, 'row', axis_index_groups=chips, tiled=True)  14.7 us
    pallas_call x10, Pallas kernels, call(): pl.pallas_call(kernel, out_shape=outs, in_specs=ins if isinstance(ins, li...  8.93 us
    all_to_all x1, waiting for transfers between devices, per_device(): lax.all_to_all(ask.reshape(n_col, LANE, TILE), ('row', 'col'), split_axis...  5.62 us
    all_to_all x1, starting transfers between devices, per_device(): lax.all_to_all(ask.reshape(n_col, LANE, TILE), ('row', 'col'), split_axis...  4.3 us
    unnamed x8, local copies, waits for them, and re-layouts  2.73 us
  transfers between devices with their start and end apart: 1, of which 1 were waited for; matrix products, arithmetic and copies ran while one was open for 0% of the time, Pallas kernels for 1%

profile of v8, /device:TPU:1, one launch (start us, length us, event | category | flops | bytes accessed | tf_op | source)
XLA Modules:
  0.0 130.7 jit_solution(13155385435201242411)
XLA Ops:
  1.3 0.7 concatenate.7
  2.0 8.4 %all_gather.6.both = s32[16,64]{1,0:T(8,128)S(1)} all-gather(s32[8,64]{1,0:T(8,128)S(1)} %concatenate.7), channel_id=1, replica_groups={{0,32},{64,96},{128,160},{192,224},{256,288},{320,352},{384,416},{448,4..., dimensions={0}, use_global_device_ids=true | all-gather | bytes 6144 | tf_op jit(solution)/shard_map/all_gather | solution.py:404
  10.4 1.1 shard_map.94
  11.5 4.3 %all-to-all-start = ((s32[32,8,128]{2,1,0:T(8,128)}), s32[32,8,128]{2,1,0:T(8,128)S(1)}, u32[]{:S(2)}, u32[]{:S(2)}) async-start(s32[32,8,128]{2,1,0:T(8,128)} %bitcast.7), calls=%async_computation | async-start | bytes 262144 | tf_op jit(solution)/shard_map/all_to_all | solution.py:418
  15.8 0.0 copy-start
  15.8 1.6 %copy-done = bf16[1,1,64,128,128]{4,3,2,1,0:T(8,128)(2,1)S(1)} copy-done((bf16[1,1,64,128,128]{4,3,2,1,0:T(8,128)(2,1)S(1)}, bf16[1,1,64,128,128]{4,3,2,1,0:T(8,128)(2,1)}, u32[]{:S(2)}) %copy-start) | copy-done | bytes 2097176
  17.4 0.0 copy-start.2
  17.4 1.1 copy-done.2
  18.6 0.0 copy-start.3
  18.6 1.0 shard_map.95
  19.6 5.6 %all-to-all-done = s32[32,8,128]{2,1,0:T(8,128)S(1)} async-done(((s32[32,8,128]{2,1,0:T(8,128)}), s32[32,8,128]{2,1,0:T(8,128)S(1)}, u32[]{:S(2)}, u32[]{:S(2)}) %all-to-all-start) | async-done | bytes 131104 | tf_op jit(solution)/shard_map/all_to_all | solution.py:418
  25.2 6.4 %all_gather.7.pair = s32[512,128]{1,0:T(8,128)S(1)} all-gather(s32[256,128]{1,0:T(8,128)S(1)} %bitcast.52), channel_id=1, replica_groups={{0,32},{64,96},{128,160},{192,224},{256,288},{320,352},{384,416},{448,4..., dimensions={0}, use_global_device_ids=true | all-gather | bytes 393216 | tf_op jit(solution)/shard_map/all_gather | solution.py:404
  31.5 0.0 copy-done.3
  31.5 0.5 shard_map.96
  32.0 0.0 copy-start.1
  32.0 15.2 %all_to_all.40 = f32[16,8,128]{2,1,0:T(8,128)S(1)} all-to-all(f32[16,8,128]{2,1,0:T(8,128)S(1)} %bitcast.45), channel_id=1, replica_groups=mesh['row'=16,'col'=32] {'row'}, dimensions={0} | all-to-all | bytes 131072 | tf_op jit(solution)/shard_map/all_to_all | solution.py:376
  47.3 1.4 %shard_map.97 = (f32[256,128]{1,0:T(8,128)S(1)}, f32[256,128]{1,0:T(8,128)S(1)}, bf16[384,384]{1,0:T(8,128)(2,1)S(1)}, bf16[64,1024]{1,0:T(8,128)(2,1)S(1)}, bf1...) custom-call(f32[128,128]{1,0:T(8,128)S(1)} %bitcast.46, bf16[64,128]{1,0:T(8,128)(2,1)S(1)} %get-tuple-element.28.pick, ...), custom_call_target="tpu_custom_call" | custom-call | tf_op jit(solution)/shard_map/pallas_call | solution.py:364
  48.7 12.4 %all_to_all.41 = f32[32,8,128]{2,1,0:T(8,128)S(1)} all-to-all(f32[32,8,128]{2,1,0:T(8,128)S(1)} %bitcast.48), channel_id=1, replica_groups=mesh['row'=16,'col'=32] {'col'}, dimensions={0} | all-to-all | bytes 262144 | tf_op jit(solution)/shard_map/all_to_all | solution.py:376
  61.1 0.0 copy-done.1
  61.1 0.6 shard_map.98
  61.7 17.6 %all_to_all.42.got = bf16[16,80,128]{2,1,0:T(8,128)(2,1)S(1)} all-to-all(bf16[16,80,128]{2,1,0:T(8,128)(2,1)S(1)} %shard_map.98), channel_id=1, replica_groups=mesh['row'=16,'col'=32] {'row'}, dimensions={0} | all-to-all | bytes 655360 | tf_op jit(solution)/shard_map/all_to_all | solution.py:376
  79.3 0.9 shard_map.99
  80.2 12.9 %all_to_all.43 = f32[32,8,128]{2,1,0:T(8,128)S(1)} all-to-all(f32[32,8,128]{2,1,0:T(8,128)S(1)} %bitcast.49), channel_id=1, replica_groups=mesh['row'=16,'col'=32] {'col'}, dimensions={0} | all-to-all | bytes 262144 | tf_op jit(solution)/shard_map/all_to_all | solution.py:376
  93.1 0.7 shard_map.100
  93.8 11.8 %all_to_all.44 = f32[16,8,128]{2,1,0:T(8,128)S(1)} all-to-all(f32[16,8,128]{2,1,0:T(8,128)S(1)} %bitcast.47), channel_id=1, replica_groups=mesh['row'=16,'col'=32] {'row'}, dimensions={0} | all-to-all | bytes 131072 | tf_op jit(solution)/shard_map/all_to_all | solution.py:376
  105.6 0.4 shard_map.101
  106.0 10.4 %all_to_all.45.got = f32[16,8,128]{2,1,0:T(8,128)S(1)} all-to-all(f32[16,8,128]{2,1,0:T(8,128)S(1)} %shard_map.101), channel_id=1, replica_groups=mesh['row'=16,'col'=32] {'row'}, dimensions={0} | all-to-all | bytes 131072 | tf_op jit(solution)/shard_map/all_to_all | solution.py:376
  116.4 0.1 shard_map.102
  116.5 11.9 %all_to_all.46 = f32[32,1,128]{2,1,0:T(1,128)S(1)} all-to-all(f32[32,1,128]{2,1,0:T(1,128)S(1)} %bitcast.51), channel_id=1, replica_groups=mesh['row'=16,'col'=32] {'col'}, dimensions={0} | all-to-all | bytes 32768 | tf_op jit(solution)/shard_map/all_to_all | solution.py:376
  128.5 2.2 %shard_map.103 = (f32[3072,128]{1,0:T(8,128)}, f32[1]{0:T(128)}, f32[3]{0:T(128)}) custom-call(f32[32,128]{1,0:T(8,128)S(1)} %bitcast.50, f32[1536,128]{1,0:T(8,128)S(1)} %bitcast.35, s32[128,128]{1,0:T(8,128)S(1)} %get-tuple-element.31.asked_row.refs_2_, s32[256,128]{1,0:T(8,128)S(1)} %get-tuple-element.32.asked_col.refs_3_, ...), custom_call_target="tpu_custom_call" | custom-call | tf_op jit(solution)/shard_map/pallas_call | solution.py:364
  (3 shorter events, 0.0 us)
Async XLA Ops:
  11.5 13.7 %all-to-all-start = ((s32[32,8,128]{2,1,0:T(8,128)}), s32[32,8,128]{2,1,0:T(8,128)S(1)}, u32[]{:S(2)}, u32[]{:S(2)}) async-start(s32[32,8,128]{2,1,0:T(8,128)} %bitcast.7), calls=%async_computation | async-start | bytes 262144 | tf_op jit(solution)/shard_map/all_to_all | solution.py:418
  15.8 1.6 %copy-start = (bf16[1,1,64,128,128]{4,3,2,1,0:T(8,128)(2,1)S(1)}, bf16[1,1,64,128,128]{4,3,2,1,0:T(8,128)(2,1)}, u32[]{:S(2)}) copy-start(bf16[1,1,64,128,128]{4,3,2,1,0:T(8,128)(2,1)} %param.8) | copy-start | bytes 6291460
  17.4 1.1 copy-start.2
  18.6 13.0 %copy-start.3 = (f32[196608]{0:T(1024)S(1)}, f32[196608]{0:T(1024)}, u32[]{:S(2)}) copy-start(f32[196608]{0:T(1024)} %param.7) | copy-start | bytes 2359300
  32.0 29.1 %copy-start.1 = (bf16[1,1,64,128,128]{4,3,2,1,0:T(8,128)(2,1)S(1)}, bf16[1,1,64,128,128]{4,3,2,1,0:T(8,128)(2,1)}, u32[]{:S(2)}) copy-start(bf16[1,1,64,128,128]{4,3,2,1,0:T(8,128)(2,1)} %param.8) | copy-start | bytes 6291460

commit v9 on v8

--- a/solution.py
+++ b/solution.py
@@ -54,7 +54,7 @@
     return jnp.concatenate(rows, axis=0).astype(F32).T.astype(jnp.int32)
 
 
-def request_kernel(pieces, planes, both, me, col, ask):
+def request_kernel(bits, planes, both, me, col, ask):
     n_x, n_z = planes
     first = (jnp.full((1, 1), me[0], jnp.int32) & 1) == 0
     x = col[0] // n_z
@@ -74,34 +74,23 @@
         jnp.sum(jnp.where((columns[:, k : k + 1] == tag) & earlier, 1, 0), axis=0, keepdims=True)
         for k, tag in enumerate(tags)
     ]
-    place = owner_c * LANE + rank_c
-    spot = jnp.where(
-        first, owner_r * LANE + rank_r + core * HALF, ((owner_c >> 1) * n_x + x) * LANE + rank_c
-    )
-    quarter = iota((TILE, TILE), 0) >> 4
-    here = ((quarter >> 1) == core) & ((quarter & 1) == (owner_c & 1)) & alive
-    value = jnp.where(first, jnp.where(alive, block_r + 1, 0), jnp.where(here, block_c + 1, 0))
-    there = jnp.where(iota((width, TILE), 0) == spot, 1.0, 0.0).astype(BF16)
+    packed = jnp.where(alive, (((owner_c << bits) + block_c) << BITS) + rank_c, -1)
+    down = iota((width, TILE), 0)
+    packed = jnp.where(down % n_x == x, packed, -9)
+    slot = rank_r + core * HALF
+    value = jnp.where((iota((TILE, TILE), 0) >> 4) == slot, jnp.where(alive, block_r + 1, 0), 0)
+    there = jnp.where(down == owner_r, 1.0, 0.0).astype(BF16)
     rest = value & 15
     dims = (((1,), (1,)), ((), ()))
     total = sum(
         lax.dot_general(there, part.astype(F32).astype(BF16), dims, preferred_element_type=F32)
         for part in (value - rest, rest)
     )
-    total = total.astype(jnp.int32) - 1
-    ident = jnp.where(alive, owner_c * pieces + block_c, -1)
-    down = iota((width, TILE), 0)
-    slot = down & LOW
-    ids = jnp.where(slot == 0, pltpu.roll(ident, count, 1), ident)
-    places = jnp.where(slot == 2, pltpu.roll(place, count, 1), place)
-    riders = jnp.where(slot < 2, ids, places)
-    full = jnp.where((lane >= count) & (slot < 4), riders, total)
-    full = jnp.where((down >> BITS) % n_x == x, full, -9)
-    ask[...] = jnp.where(first, total, full)
+    ask[...] = jnp.where(first, total.astype(jnp.int32) - 1, packed)
 
 
 def local_kernel(
-    pieces, both, me, vector, tiles,
+    bits, both, me, vector, tiles,
     pick_row, put_row, pick_col, put_col, pick_pair, mine, energy, turned,
 ):
     first = (jnp.full((1, 1), me[0], jnp.int32) & 1) == 0
@@ -114,7 +103,7 @@
         across, down = place_of(slots[k], columns[:, k : k + 1])
         pick[...] = jnp.where(iota((count, width), 1) == down, 1.0, 0.0).astype(BF16)
         put[...] = jnp.where(iota((width, count), 0) == across + shift, 1.0, 0.0).astype(BF16)
-    ident = jnp.where(iota((count, 1), 0) < live, columns[:, 1:2] * pieces + columns[:, 2:3], -2)
+    ident = jnp.where(iota((count, 1), 0) < live, (columns[:, 1:2] << bits) + columns[:, 2:3], -2)
     mine[...] = jnp.broadcast_to(ident, mine.shape)
     place = place_of(slots[1], columns[:, 1:2])[1]
     high = place + (place & ~LOW)
@@ -125,10 +114,6 @@
         turned[t] = tiles[t].T
 
 
-def first_lane(asked):
-    return jnp.broadcast_to(asked[:, 0:1], asked.shape)
-
-
 def gather(asked, vector):
     pieces = vector.shape[0]
     rows = asked.shape[0]
@@ -139,35 +124,36 @@
     return exact_dot(select, vector)
 
 
-def served_kernel(n_x, index, pair, vector, squares, asked_row, asked_col, out, energy):
-    me = jnp.full((1, 1), index[0], jnp.int32)
-    first = (me & 1) == 0
-    width = asked_col.shape[0]
-    col = pair[:width, :].reshape(-1, LANE, TILE)
-    swapped = jnp.concatenate([col[:, HALF:, :], col[:, :HALF, :]], axis=1)
-    lower = iota(col.shape, 1) < HALF
-    keep = lower == first.reshape(1, 1, 1)
-    asked_col[...] = jnp.where(keep, col, swapped).reshape(width, TILE)
-    row = jnp.max(pair[width:, :].reshape(-1, n_x, LANE, TILE), axis=1)
-    slot = iota(row.shape, 1)
-    lane = iota(row.shape, 2)
-    asked, full = [], []
-    for core in range(2):
-        sides = [jnp.broadcast_to(row[:, :, 16 * k : 16 * k + 1], row.shape) for k in (2 * core, 2 * core + 1)]
-        value = jnp.where(first.reshape(1, 1, 1), sides[0], sides[1])
-        riders = jnp.where((slot & 1) == 0, row[:, core : core + 1, :], row[:, 2 + core : 3 + core, :])
-        count = TILE // 2
-        mixed = jnp.where(lane >= count, riders, jnp.where(lane == count - 1, me.reshape(1, 1, 1), value))
-        asked.append(value)
-        full.append(mixed)
-    shape = asked_row.shape
-    asked_row[...] = jnp.stack(full, axis=1).reshape(shape)
-    out[...] = gather(jnp.stack(asked, axis=1).reshape(shape), vector[...] * SCALE)
+def served_kernel(n_x, bits, me, pair, vector, squares, asked_row, asked_col, riders, out, energy):
+    first = (jnp.full((1, 1), me[0], jnp.int32) & 1) == 0
+    peers = pair.shape[0] // 2
+    col = pair[:peers, :]
+    for k in range(HALF):
+        sides = [jnp.broadcast_to(col[:, 16 * j : 16 * j + 1], col.shape) for j in (k, k + HALF)]
+        value = jnp.where(first, sides[0], sides[1])
+        asked_col[pl.ds(k, peers, LANE), :] = value
+        asked_col[pl.ds(k + HALF, peers, LANE), :] = value
+    chips = peers // n_x
+    row = pair[pl.ds(peers, chips, n_x), :]
+    for x in range(1, n_x):
+        row = jnp.maximum(row, pair[pl.ds(peers + x, chips, n_x), :])
+    riders[...] = row
+    down = iota((2 * LANE, TILE), 0)
+    side = jnp.where(iota((2 * LANE, TILE), 1) < TILE // 2, 0, 1) == (down >> BITS)
+    parts = []
+    for k in range(chips):
+        rider = row[k : k + 1, :]
+        here = ((rider >> (bits + BITS)) == me[0]) & ((rider & LOW) == (down & LOW)) & side
+        value = jnp.where(here, ((rider >> BITS) & ((1 << bits) - 1)) + 1, 0).astype(F32)
+        parts.append(jnp.sum(value, axis=1, keepdims=True))
+    asked = jnp.broadcast_to(jnp.concatenate(parts, axis=0), asked_row.shape).astype(jnp.int32) - 1
+    asked_row[...] = asked
+    out[...] = gather(asked, vector[...] * SCALE)
     energy[...] = jnp.sum(squares[...], axis=0, keepdims=True)
 
 
 def product_lane(asked_row, asked_col):
-    rows = [first_lane(asked_row[...]).astype(F32).T[0:1, :]]
+    rows = [asked_row[...].astype(F32).T[0:1, :]]
     width = asked_col.shape[0]
     for k in range(width // TILE):
         part = asked_col[k * TILE : (k + 1) * TILE, :].astype(F32).T[0:1, :]
@@ -176,30 +162,26 @@
     return [row.astype(jnp.int32) for row in rows]
 
 
-def meet_tables(asked_row, asked_col, mine, pieces, meet, link, link_col, owned):
+def meet_tables(bits, asked_row, asked_col, mine, riders, me, meet, link, link_col, owned):
     lanes = product_lane(asked_row, asked_col)
     base = 0
-    served_row, served_col = first_lane(asked_row[...]), asked_col[...]
+    served_row, served_col = asked_row[...], asked_col[...]
     for served in (served_row, served_col):
         for k, lane in enumerate(lanes):
             hit = (served == lane) & (served >= 0)
             meet[base : base + served.shape[0], k * TILE : (k + 1) * TILE] = jnp.where(hit, 1.0, 0.0).astype(BF16)
         base += served.shape[0]
-    count = mine.shape[0]
-    index = asked_row[0:1, count - 1 : count]
-    ident = jnp.where(served_col < 0, -3, served_col + index * pieces)
-    lane = iota((1, TILE), 1)
+    ident = jnp.where(served_col < 0, -3, served_col + (me[0] << bits))
     slot = iota(owned.shape[:1] + (TILE,), 0)
-    half = jnp.where(iota(owned.shape[:1] + (TILE,), 1) < count, 0, 1)
-    for k in range(asked_row.shape[0] // (2 * LANE)):
-        start = 2 * k * LANE
-        even = [asked_row[start + j : start + j + 1, :] for j in range(2)]
-        odd = [asked_row[start + LANE + j : start + LANE + j + 1, :] for j in range(2)]
-        ids, spots = [jnp.where(lane < count, pltpu.roll(a, count, 1), b) for a, b in zip(even, odd)]
+    half = jnp.where(iota(owned.shape[:1] + (TILE,), 1) < mine.shape[0], 0, 1)
+    for k in range(riders.shape[0]):
+        rider = riders[k : k + 1, :]
+        ids = rider >> BITS
         cols = slice(k * TILE, (k + 1) * TILE)
         link[:, cols] = jnp.where(mine[...] == ids, 1.0, 0.0).astype(BF16)
         link_col[:, cols] = jnp.where(ident == ids, 1.0, 0.0).astype(BF16)
-        sent = (spots == index * LANE + (slot & LOW)) & ((slot >> BITS) == 2 * k + half)
+        sent = ((rider >> (bits + BITS)) == me[0]) & ((rider & LOW) == (slot & LOW))
+        sent = sent & ((slot >> BITS) == 2 * k + half)
         owned[:, cols] = jnp.where(sent, 1.0, 0.0).astype(BF16)
 
 
@@ -218,14 +200,15 @@
 
 
 def direct_kernel(
-    got, pick, tiles, put, asked_row, asked_col, mine, vector, out, v_col, meet, link, link_col, owned
+    bits, me, got, pick, tiles, put, asked_row, asked_col, mine, riders, vector,
+    out, v_col, meet, link, link_col, owned,
 ):
     y = multiply(exact_dot(pick[...], got[...]), tiles)
     v = gather(asked_col[...], vector[...] * SCALE)
     v_col[...] = v
     forward = (iota(v.shape, 0) & LOW) < HALF
     out[...] = exact_dot(put[...], y) + jnp.where(forward, v, 0.0)
-    meet_tables(asked_row, asked_col, mine, vector.shape[0], meet, link, link_col, owned)
+    meet_tables(bits, asked_row, asked_col, mine, riders, me, meet, link, link_col, owned)
 
 
 def mirror_kernel(got, pick, tiles, put, meet, out):
@@ -329,7 +312,7 @@
     f = h * root
     parts = sems.shape[0]
     step = vector.shape[0] // parts
-    asked = [first_lane(asked_row[...]), returned_rows(asked_col[...])]
+    asked = [asked_row[...], returned_rows(asked_col[...])]
     lanes = jnp.concatenate([x.astype(F32).T[0:1, :].astype(jnp.int32) for x in asked], axis=1)
     image = jnp.concatenate([first_row[...], returned_rows(first_col[...])], axis=0)
     second = jnp.concatenate([second_row[...], returned_rows(second_col[...])], axis=0)
@@ -393,6 +376,7 @@
     def over_col(x):
         return exchange(x, "col", n_col)
 
+    bits = (pieces - 1).bit_length()
     n_y = n_row // 2
     n_x = n_col // n_y
     n_z = n_col // n_x
@@ -408,23 +392,23 @@
     both = over_chip(slots)
     me, col = lax.axis_index("row").reshape(1), lax.axis_index("col").reshape(1)
     ask = call(
-        functools.partial(request_kernel, pieces, (n_x, n_z)),
-        shape(wide_c, TILE, dtype=jnp.int32),
+        functools.partial(request_kernel, bits, (n_x, n_z)),
+        shape(n_col, TILE, dtype=jnp.int32),
         both,
         me,
         col,
         ins=[VMEM] + [SMEM] * 2,
     )
     ask = lax.all_to_all(
-        ask.reshape(n_col, LANE, TILE),
+        ask.reshape(n_col, 1, TILE),
         ("row", "col"),
         split_axis=0,
         concat_axis=0,
         axis_index_groups=planes,
         tiled=True,
-    ).reshape(wide_c, TILE)
+    ).reshape(n_col, TILE)
     pick_row, put_row, pick_col, put_col, pick_pair, mine, squares, turned = call(
-        functools.partial(local_kernel, pieces),
+        functools.partial(local_kernel, bits),
         (
             shape(count, wide_r, dtype=BF16),
             shape(wide_r, count, dtype=BF16),
@@ -441,11 +425,12 @@
         tiles,
         ins=[VMEM, SMEM] + [VMEM] * 2,
     )
-    asked_row, asked_col, v_row, energy = call(
-        functools.partial(served_kernel, n_x),
+    asked_row, asked_col, riders, v_row, energy = call(
+        functools.partial(served_kernel, n_x, bits),
         (
             shape(wide_r, TILE, dtype=jnp.int32),
             shape(wide_c, TILE, dtype=jnp.int32),
+            shape(n_y, TILE, dtype=jnp.int32),
             shape(wide_r, TILE),
             shape(1, TILE),
         ),
@@ -457,7 +442,7 @@
     )
     x_col = over_row(v_row)
     first_col, v_col, meet, link, link_col, owned = call(
-        direct_kernel,
+        functools.partial(direct_kernel, bits),
         (
             shape(wide_c, TILE),
             shape(wide_c, TILE),
@@ -466,6 +451,7 @@
             shape(wide_c, n_row * count, dtype=BF16),
             shape(wide_r, n_row * count, dtype=BF16),
         ),
+        me,
         x_col,
         pick_row,
         turned,
@@ -473,7 +459,9 @@
         asked_row,
         asked_col,
         mine,
+        riders,
         vector,
+        ins=[SMEM] + [VMEM] * 9,
     )
     first_col = over_col(first_col)
     packed = call(

time: 131 us -> 130 us (level)
  no operation moved by 1% of the time
where the time goes in v9:
time: 130 us
  blocking collectives  107 us (82%)
  Pallas kernels  8.92 us (7%)
  waiting for transfers between devices  4.78 us (4%)
  starting transfers between devices  4.3 us (3%)
  local copies, waits for them, and re-layouts  3.46 us (3%)
  between operations  1.37 us (1%)
    all_to_all x7, blocking collectives, exchange(): got = lax.all_to_all(sent, axis, split_axis=0, concat_axis=0, tiled=True)  92.3 us
    all_gather x2, blocking collectives, over_chip(): return lax.all_gather(x, 'row', axis_index_groups=chips, tiled=True)  14.8 us
    pallas_call x10, Pallas kernels, call(): pl.pallas_call(kernel, out_shape=outs, in_specs=ins if isinstance(ins, li...  8.92 us
    all_to_all x1, waiting for transfers between devices, per_device(): lax.all_to_all(ask.reshape(n_col, 1, TILE), ('row', 'col'), split_axis=0,...  4.78 us
    all_to_all x1, starting transfers between devices, per_device(): lax.all_to_all(ask.reshape(n_col, 1, TILE), ('row', 'col'), split_axis=0,...  4.3 us
    unnamed x8, local copies, waits for them, and re-layouts  2.73 us
  transfers between devices with their start and end apart: 1, of which 1 were waited for; matrix products, arithmetic and copies ran while one was open for 0% of the time, Pallas kernels for 1%

profile of v9, /device:TPU:1, one launch (start us, length us, event | category | flops | bytes accessed | tf_op | source)
XLA Modules:
  0.0 130.0 jit_solution(6415359475452211657)
XLA Ops:
  1.3 0.7 concatenate.7
  2.0 8.4 %all_gather.6.both = s32[16,64]{1,0:T(8,128)S(1)} all-gather(s32[8,64]{1,0:T(8,128)S(1)} %concatenate.7), channel_id=1, replica_groups={{0,32},{64,96},{128,160},{192,224},{256,288},{320,352},{384,416},{448,4..., dimensions={0}, use_global_device_ids=true | all-gather | bytes 6144 | tf_op jit(solution)/shard_map/all_gather | solution.py:388
  10.4 1.0 shard_map.94
  11.4 4.3 %all-to-all-start = ((s32[32,1,128]{2,1,0:T(1,128)}), s32[32,1,128]{2,1,0:T(1,128)S(1)}, u32[]{:S(2)}, u32[]{:S(2)}) async-start(s32[32,1,128]{2,1,0:T(1,128)} %bitcast.8), calls=%async_computation | async-start | bytes 32768 | tf_op jit(solution)/shard_map/all_to_all | solution.py:402
  15.7 0.0 copy-start
  15.7 1.6 %copy-done = bf16[1,1,64,128,128]{4,3,2,1,0:T(8,128)(2,1)S(1)} copy-done((bf16[1,1,64,128,128]{4,3,2,1,0:T(8,128)(2,1)S(1)}, bf16[1,1,64,128,128]{4,3,2,1,0:T(8,128)(2,1)}, u32[]{:S(2)}) %copy-start) | copy-done | bytes 2097176
  17.3 0.0 copy-start.2
  17.3 1.1 copy-done.2
  18.5 0.0 copy-start.3
  18.5 1.0 shard_map.95
  19.5 4.8 %all-to-all-done = s32[32,1,128]{2,1,0:T(1,128)S(1)} async-done(((s32[32,1,128]{2,1,0:T(1,128)}), s32[32,1,128]{2,1,0:T(1,128)S(1)}, u32[]{:S(2)}, u32[]{:S(2)}) %all-to-all-start) | async-done | bytes 16416 | tf_op jit(solution)/shard_map/all_to_all | solution.py:402
  24.2 6.5 %all-gather = s32[64,1,128]{2,0,1:T(8,128)S(1)} all-gather(s32[32,1,128]{2,0,1:T(8,128)S(1)} %bitcast.56), channel_id=2, replica_groups={{0,32},{64,96},{128,160},{192,224},{256,288},{320,352},{384,416},{448,4..., dimensions={0}, use_global_device_ids=true | all-gather | bytes 49152 | tf_op jit(solution)/shard_map/all_gather | solution.py:388
  30.7 0.0 copy-done.3
  30.7 0.0 copy-start.1
  30.7 0.6 shard_map.96
  31.3 15.2 %all_to_all.40 = f32[16,8,128]{2,1,0:T(8,128)S(1)} all-to-all(f32[16,8,128]{2,1,0:T(8,128)S(1)} %bitcast.48), channel_id=1, replica_groups=mesh['row'=16,'col'=32] {'row'}, dimensions={0} | all-to-all | bytes 131072 | tf_op jit(solution)/shard_map/all_to_all | solution.py:359
  46.5 1.4 %shard_map.97 = (f32[256,128]{1,0:T(8,128)S(1)}, f32[256,128]{1,0:T(8,128)S(1)}, bf16[384,384]{1,0:T(8,128)(2,1)S(1)}, bf16[64,1024]{1,0:T(8,128)(2,1)S(1)}, bf1...) custom-call(s32[1]{0:T(128)} %bitcast.me, f32[128,128]{1,0:T(8,128)S(1)} %bitcast.49, ...), custom_call_target="tpu_custom_call" | custom-call | tf_op jit(solution)/shard_map/pallas_call | solution.py:347
  47.9 12.5 %all_to_all.41 = f32[32,8,128]{2,1,0:T(8,128)S(1)} all-to-all(f32[32,8,128]{2,1,0:T(8,128)S(1)} %bitcast.52), channel_id=1, replica_groups=mesh['row'=16,'col'=32] {'col'}, dimensions={0} | all-to-all | bytes 262144 | tf_op jit(solution)/shard_map/all_to_all | solution.py:359
  60.4 0.0 copy-done.1
  60.5 0.6 shard_map.98
  61.1 17.6 %all_to_all.42.got = bf16[16,80,128]{2,1,0:T(8,128)(2,1)S(1)} all-to-all(bf16[16,80,128]{2,1,0:T(8,128)(2,1)S(1)} %shard_map.98), channel_id=1, replica_groups=mesh['row'=16,'col'=32] {'row'}, dimensions={0} | all-to-all | bytes 655360 | tf_op jit(solution)/shard_map/all_to_all | solution.py:359
  78.6 0.9 shard_map.99
  79.6 12.9 %all_to_all.43 = f32[32,8,128]{2,1,0:T(8,128)S(1)} all-to-all(f32[32,8,128]{2,1,0:T(8,128)S(1)} %bitcast.53), channel_id=1, replica_groups=mesh['row'=16,'col'=32] {'col'}, dimensions={0} | all-to-all | bytes 262144 | tf_op jit(solution)/shard_map/all_to_all | solution.py:359
  92.5 0.7 shard_map.100
  93.2 11.8 %all_to_all.44 = f32[16,8,128]{2,1,0:T(8,128)S(1)} all-to-all(f32[16,8,128]{2,1,0:T(8,128)S(1)} %bitcast.50), channel_id=1, replica_groups=mesh['row'=16,'col'=32] {'row'}, dimensions={0} | all-to-all | bytes 131072 | tf_op jit(solution)/shard_map/all_to_all | solution.py:359
  105.0 0.4 shard_map.101
  105.4 10.4 %all_to_all.45.got = f32[16,8,128]{2,1,0:T(8,128)S(1)} all-to-all(f32[16,8,128]{2,1,0:T(8,128)S(1)} %shard_map.101), channel_id=1, replica_groups=mesh['row'=16,'col'=32] {'row'}, dimensions={0} | all-to-all | bytes 131072 | tf_op jit(solution)/shard_map/all_to_all | solution.py:359
  115.8 0.1 shard_map.102
  115.9 11.9 %all_to_all.46 = f32[32,1,128]{2,1,0:T(1,128)S(1)} all-to-all(f32[32,1,128]{2,1,0:T(1,128)S(1)} %bitcast.55), channel_id=1, replica_groups=mesh['row'=16,'col'=32] {'col'}, dimensions={0} | all-to-all | bytes 32768 | tf_op jit(solution)/shard_map/all_to_all | solution.py:359
  127.9 2.1 %shard_map.103 = (f32[3072,128]{1,0:T(8,128)}, f32[1]{0:T(128)}, f32[3]{0:T(128)}) custom-call(f32[32,128]{1,0:T(8,128)S(1)} %bitcast.54, f32[1536,128]{1,0:T(8,128)S(1)} %bitcast.38, s32[128,128]{1,0:T(8,128)S(1)} %get-tuple-element.32.asked_row.refs_2_, s32[256,128]{1,0:T(8,128)S(1)} %get-tuple-element.33.asked_col.refs_3_, ...), custom_call_target="tpu_custom_call" | custom-call | tf_op jit(solution)/shard_map/pallas_call | solution.py:347
  (3 shorter events, 0.0 us)
Async XLA Ops:
  11.4 12.8 %all-to-all-start = ((s32[32,1,128]{2,1,0:T(1,128)}), s32[32,1,128]{2,1,0:T(1,128)S(1)}, u32[]{:S(2)}, u32[]{:S(2)}) async-start(s32[32,1,128]{2,1,0:T(1,128)} %bitcast.8), calls=%async_computation | async-start | bytes 32768 | tf_op jit(solution)/shard_map/all_to_all | solution.py:402
  15.7 1.6 %copy-start = (bf16[1,1,64,128,128]{4,3,2,1,0:T(8,128)(2,1)S(1)}, bf16[1,1,64,128,128]{4,3,2,1,0:T(8,128)(2,1)}, u32[]{:S(2)}) copy-start(bf16[1,1,64,128,128]{4,3,2,1,0:T(8,128)(2,1)} %param.8) | copy-start | bytes 6291460
  17.3 1.1 copy-start.2
  18.5 12.3 %copy-start.3 = (f32[196608]{0:T(1024)S(1)}, f32[196608]{0:T(1024)}, u32[]{:S(2)}) copy-start(f32[196608]{0:T(1024)} %param.7) | copy-start | bytes 2359300
  30.7 29.7 %copy-start.1 = (bf16[1,1,64,128,128]{4,3,2,1,0:T(8,128)(2,1)S(1)}, bf16[1,1,64,128,128]{4,3,2,1,0:T(8,128)(2,1)}, u32[]{:S(2)}) copy-start(bf16[1,1,64,128,128]{4,3,2,1,0:T(8,128)(2,1)} %param.8) | copy-start | bytes 6291460

commit v10 on v9

--- a/solution.py
+++ b/solution.py
@@ -106,7 +106,7 @@
     ident = jnp.where(iota((count, 1), 0) < live, (columns[:, 1:2] << bits) + columns[:, 2:3], -2)
     mine[...] = jnp.broadcast_to(ident, mine.shape)
     place = place_of(slots[1], columns[:, 1:2])[1]
-    high = place + (place & ~LOW)
+    high = place + (place & ~LOW) + (me[0] & 1) * LANE
     pick_pair[...] = jnp.where(iota(pick_pair.shape, 1) == high, 1.0, 0.0).astype(BF16)
     v = vector[...] * SCALE
     energy[...] = jnp.sum((v * v).reshape(-1, 8, TILE), axis=0)
@@ -216,27 +216,31 @@
     high, low = halves(y)
     width = put.shape[0]
     total = exact_dot(meet[:width, width:], got[...])
-    low = dot(put[...], low)
+    total, low = total.astype(BF16), dot(put[...], low).astype(BF16)
     count = y.shape[0]
     for k in range(out.shape[0]):
-        rows = slice(k * LANE, (k + 1) * LANE)
+        rows = slice(2 * k * LANE, 2 * (k + 1) * LANE)
         out[k, :count, :] = high
-        out[k, count:, :] = jnp.concatenate([total[rows], low[rows]], axis=0).astype(BF16)
-
-
-def second_direct_kernel(got, link, link_col, owned, pick, meet, first_col, tiles, put, out, first_row):
+        out[k, count : count + 2 * LANE, :] = total[rows]
+        out[k, count + 2 * LANE :, :] = low[rows]
+
+
+def second_direct_kernel(me, got, link, link_col, owned, pick, meet, first_col, tiles, put, out, first_row):
     count = link.shape[0]
-    peers = range(got.shape[0])
+    chips = got.shape[0] // 2
+    peers = [core * chips + chip for chip in range(chips) for core in range(2)]
+    middle = count + 2 * LANE
     mirrors = jnp.concatenate([got[k, :count, :] for k in peers], axis=0)
-    sums = jnp.concatenate([got[k, count:, :] for k in peers], axis=0)
+    sums = jnp.concatenate([got[k, count:middle, :] for k in peers], axis=0)
+    lows = jnp.concatenate([got[k, middle:, :] for k in peers], axis=0)
     y = multiply(dot(link[...], mirrors) + dot(pick[...], sums), tiles)
     width = got.shape[0] * LANE
     image = dot(link_col[...], mirrors) + exact_dot(meet[width:, width:], first_col[...])
     forward = (iota(image.shape, 0) & LOW) < HALF
     out[...] = exact_dot(put[...], y) + jnp.where(forward, image, 0.0)
     slot = iota((width, 2 * width), 0)
-    low = iota((width, 2 * width), 1) == slot + (slot & ~LOW) + LANE
-    first_row[...] = dot(owned[...], mirrors) + dot(jnp.where(low, 1.0, 0.0).astype(BF16), sums)
+    low = iota((width, 2 * width), 1) == slot + (slot & ~LOW) + (me[0] & 1) * LANE
+    first_row[...] = dot(owned[...], mirrors) + dot(jnp.where(low, 1.0, 0.0).astype(BF16), lows)
 
 
 def second_mirror_kernel(got, pick, tiles, put, out):
@@ -466,17 +470,20 @@
     first_col = over_col(first_col)
     packed = call(
         mirror_kernel,
-        shape(n_row, count + 2 * LANE, TILE, dtype=BF16),
+        shape(n_y, count + 4 * LANE, TILE, dtype=BF16),
         first_col,
         pick_col,
         tiles,
         put_row,
         meet,
     )
+    cores = [[2 * y + core for y in range(n_y)] for core in range(2)]
+    packed = lax.all_to_all(packed, "row", split_axis=0, concat_axis=0, axis_index_groups=cores, tiled=True)
     second_col, first_row = call(
         second_direct_kernel,
         (shape(wide_c, TILE), shape(wide_r, TILE)),
-        over_row(packed),
+        me,
+        over_chip(packed),
         link,
         link_col,
         owned,
@@ -485,6 +492,7 @@
         first_col,
         turned,
         put_col,
+        ins=[SMEM] + [VMEM] * 9,
     )
     second_col = over_col(second_col)
     second_row = over_row(

time: 130 us -> 129 us (level)
    all_to_all x7 -> x6, blocking collectives: 92.3 us -> 75.2 us  [exchange(): got = lax.all_to_all(sent, axis, split_axis=0, concat_axis=0, tiled=True)]
    all_to_all x0 -> x1, blocking collectives: none -> 11.1 us  [per_device(): lax.all_to_all(packed, 'row', split_axis=0, concat_axis=0, axis_index_gro...]
    all_gather x2 -> x3, blocking collectives: 14.8 us -> 19.8 us  [over_chip(): return lax.all_gather(x, 'row', axis_index_groups=chips, tiled=True)]
where the time goes in v10:
time: 129 us
  blocking collectives  106 us (82%)
  Pallas kernels  8.92 us (7%)
  waiting for transfers between devices  4.78 us (4%)
  starting transfers between devices  4.3 us (3%)
  local copies, waits for them, and re-layouts  3.46 us (3%)
  between operations  1.37 us (1%)
    all_to_all x6, blocking collectives, exchange(): got = lax.all_to_all(sent, axis, split_axis=0, concat_axis=0, tiled=True)  75.2 us
    all_gather x3, blocking collectives, over_chip(): return lax.all_gather(x, 'row', axis_index_groups=chips, tiled=True)  19.8 us
    all_to_all x1, blocking collectives, per_device(): lax.all_to_all(packed, 'row', split_axis=0, concat_axis=0, axis_index_gro...  11.1 us
    pallas_call x10, Pallas kernels, call(): pl.pallas_call(kernel, out_shape=outs, in_specs=ins if isinstance(ins, li...  8.92 us
    all_to_all x1, waiting for transfers between devices, per_device(): lax.all_to_all(ask.reshape(n_col, 1, TILE), ('row', 'col'), split_axis=0,...  4.78 us
    all_to_all x1, starting transfers between devices, per_device(): lax.all_to_all(ask.reshape(n_col, 1, TILE), ('row', 'col'), split_axis=0,...  4.3 us
    unnamed x8, local copies, waits for them, and re-layouts  2.73 us
  transfers between devices with their start and end apart: 1, of which 1 were waited for; matrix products, arithmetic and copies ran while one was open for 0% of the time, Pallas kernels for 1%

profile of v10, /device:TPU:1, one launch (start us, length us, event | category | flops | bytes accessed | tf_op | source)
XLA Modules:
  0.0 128.9 jit_solution(10958796721039621736)
XLA Ops:
  1.3 0.7 concatenate.7
  2.0 8.4 %all_gather.9.both = s32[16,64]{1,0:T(8,128)S(1)} all-gather(s32[8,64]{1,0:T(8,128)S(1)} %concatenate.7), channel_id=1, replica_groups={{0,32},{64,96},{128,160},{192,224},{256,288},{320,352},{384,416},{448,4..., dimensions={0}, use_global_device_ids=true | all-gather | bytes 6144 | tf_op jit(solution)/shard_map/all_gather | solution.py:392
  10.4 1.0 shard_map.94
  11.4 4.3 %all-to-all-start = ((s32[32,1,128]{2,1,0:T(1,128)}), s32[32,1,128]{2,1,0:T(1,128)S(1)}, u32[]{:S(2)}, u32[]{:S(2)}) async-start(s32[32,1,128]{2,1,0:T(1,128)} %bitcast.8), calls=%async_computation | async-start | bytes 32768 | tf_op jit(solution)/shard_map/all_to_all | solution.py:406
  15.7 0.0 copy-start
  15.7 1.6 %copy-done = bf16[1,1,64,128,128]{4,3,2,1,0:T(8,128)(2,1)S(1)} copy-done((bf16[1,1,64,128,128]{4,3,2,1,0:T(8,128)(2,1)S(1)}, bf16[1,1,64,128,128]{4,3,2,1,0:T(8,128)(2,1)}, u32[]{:S(2)}) %copy-start) | copy-done | bytes 2097176
  17.3 0.0 copy-start.2
  17.3 1.1 copy-done.2
  18.5 0.0 copy-start.3
  18.5 1.0 shard_map.95
  19.5 4.8 %all-to-all-done = s32[32,1,128]{2,1,0:T(1,128)S(1)} async-done(((s32[32,1,128]{2,1,0:T(1,128)}), s32[32,1,128]{2,1,0:T(1,128)S(1)}, u32[]{:S(2)}, u32[]{:S(2)}) %all-to-all-start) | async-done | bytes 16416 | tf_op jit(solution)/shard_map/all_to_all | solution.py:406
  24.2 6.5 %all-gather = s32[64,1,128]{2,0,1:T(8,128)S(1)} all-gather(s32[32,1,128]{2,0,1:T(8,128)S(1)} %bitcast.56), channel_id=2, replica_groups={{0,32},{64,96},{128,160},{192,224},{256,288},{320,352},{384,416},{448,4..., dimensions={0}, use_global_device_ids=true | all-gather | bytes 49152 | tf_op jit(solution)/shard_map/all_gather | solution.py:392
  30.7 0.0 copy-done.3
  30.7 0.0 copy-start.1
  30.7 0.6 shard_map.96
  31.3 15.2 %all_to_all.40 = f32[16,8,128]{2,1,0:T(8,128)S(1)} all-to-all(f32[16,8,128]{2,1,0:T(8,128)S(1)} %bitcast.48), channel_id=1, replica_groups=mesh['row'=16,'col'=32] {'row'}, dimensions={0} | all-to-all | bytes 131072 | tf_op jit(solution)/shard_map/all_to_all | solution.py:363
  46.5 1.4 %shard_map.97 = (f32[256,128]{1,0:T(8,128)S(1)}, f32[256,128]{1,0:T(8,128)S(1)}, bf16[384,384]{1,0:T(8,128)(2,1)S(1)}, bf16[64,1024]{1,0:T(8,128)(2,1)S(1)}, bf1...) custom-call(s32[1]{0:T(128)} %bitcast.me, f32[128,128]{1,0:T(8,128)S(1)} %bitcast.49, ...), custom_call_target="tpu_custom_call" | custom-call | tf_op jit(solution)/shard_map/pallas_call | solution.py:351
  47.9 12.5 %all_to_all.41 = f32[32,8,128]{2,1,0:T(8,128)S(1)} all-to-all(f32[32,8,128]{2,1,0:T(8,128)S(1)} %bitcast.52), channel_id=1, replica_groups=mesh['row'=16,'col'=32] {'col'}, dimensions={0} | all-to-all | bytes 262144 | tf_op jit(solution)/shard_map/all_to_all | solution.py:363
  60.4 0.0 copy-done.1
  60.5 0.6 shard_map.98
  61.1 11.1 %all_to_all.42 = bf16[8,96,128]{2,1,0:T(8,128)(2,1)S(1)} all-to-all(bf16[8,96,128]{2,1,0:T(8,128)(2,1)S(1)} %shard_map.98), channel_id=1, replica_groups={{0,64,128,192,256,320,384,448},{32,96,160,224,288,352,416,480},{1,65,12..., dimensions={0} | all-to-all | bytes 393216 | tf_op jit(solution)/shard_map/all_to_all | solution.py:481
  72.2 4.9 %all_gather.11.got = bf16[16,96,128]{2,1,0:T(8,128)(2,1)S(1)} all-gather(bf16[8,96,128]{2,1,0:T(8,128)(2,1)S(1)} %all_to_all.42), channel_id=1, replica_groups={{0,32},{64,96},{128,160},{192,224},{256,288},{320,352},{384,416},{448,4..., dimensions={0}, use_global_device_ids=true | all-gather | bytes 589824 | tf_op jit(solution)/shard_map/all_gather | solution.py:392
  77.1 0.9 shard_map.99
  78.0 12.9 %all_to_all.43 = f32[32,8,128]{2,1,0:T(8,128)S(1)} all-to-all(f32[32,8,128]{2,1,0:T(8,128)S(1)} %bitcast.53), channel_id=1, replica_groups=mesh['row'=16,'col'=32] {'col'}, dimensions={0} | all-to-all | bytes 262144 | tf_op jit(solution)/shard_map/all_to_all | solution.py:363
  90.9 0.7 shard_map.100
  91.6 12.3 %all_to_all.44 = f32[16,8,128]{2,1,0:T(8,128)S(1)} all-to-all(f32[16,8,128]{2,1,0:T(8,128)S(1)} %bitcast.50), channel_id=1, replica_groups=mesh['row'=16,'col'=32] {'row'}, dimensions={0} | all-to-all | bytes 131072 | tf_op jit(solution)/shard_map/all_to_all | solution.py:363
  104.0 0.4 shard_map.101
  104.4 10.4 %all_to_all.45.got = f32[16,8,128]{2,1,0:T(8,128)S(1)} all-to-all(f32[16,8,128]{2,1,0:T(8,128)S(1)} %shard_map.101), channel_id=1, replica_groups=mesh['row'=16,'col'=32] {'row'}, dimensions={0} | all-to-all | bytes 131072 | tf_op jit(solution)/shard_map/all_to_all | solution.py:363
  114.8 0.1 shard_map.102
  114.9 11.9 %all_to_all.46 = f32[32,1,128]{2,1,0:T(1,128)S(1)} all-to-all(f32[32,1,128]{2,1,0:T(1,128)S(1)} %bitcast.55), channel_id=1, replica_groups=mesh['row'=16,'col'=32] {'col'}, dimensions={0} | all-to-all | bytes 32768 | tf_op jit(solution)/shard_map/all_to_all | solution.py:363
  126.8 2.1 %shard_map.103 = (f32[3072,128]{1,0:T(8,128)}, f32[1]{0:T(128)}, f32[3]{0:T(128)}) custom-call(f32[32,128]{1,0:T(8,128)S(1)} %bitcast.54, f32[1536,128]{1,0:T(8,128)S(1)} %bitcast.38, s32[128,128]{1,0:T(8,128)S(1)} %get-tuple-element.32.asked_row.refs_2_, s32[256,128]{1,0:T(8,128)S(1)} %get-tuple-element.33.asked_col.refs_3_, ...), custom_call_target="tpu_custom_call" | custom-call | tf_op jit(solution)/shard_map/pallas_call | solution.py:351
  (3 shorter events, 0.0 us)
Async XLA Ops:
  11.4 12.8 %all-to-all-start = ((s32[32,1,128]{2,1,0:T(1,128)}), s32[32,1,128]{2,1,0:T(1,128)S(1)}, u32[]{:S(2)}, u32[]{:S(2)}) async-start(s32[32,1,128]{2,1,0:T(1,128)} %bitcast.8), calls=%async_computation | async-start | bytes 32768 | tf_op jit(solution)/shard_map/all_to_all | solution.py:406
  15.7 1.6 %copy-start = (bf16[1,1,64,128,128]{4,3,2,1,0:T(8,128)(2,1)S(1)}, bf16[1,1,64,128,128]{4,3,2,1,0:T(8,128)(2,1)}, u32[]{:S(2)}) copy-start(bf16[1,1,64,128,128]{4,3,2,1,0:T(8,128)(2,1)} %param.8) | copy-start | bytes 6291460
  17.3 1.1 copy-start.2
  18.5 12.3 %copy-start.3 = (f32[196608]{0:T(1024)S(1)}, f32[196608]{0:T(1024)}, u32[]{:S(2)}) copy-start(f32[196608]{0:T(1024)} %param.7) | copy-start | bytes 2359300
  30.7 29.7 %copy-start.1 = (bf16[1,1,64,128,128]{4,3,2,1,0:T(8,128)(2,1)S(1)}, bf16[1,1,64,128,128]{4,3,2,1,0:T(8,128)(2,1)}, u32[]{:S(2)}) copy-start(bf16[1,1,64,128,128]{4,3,2,1,0:T(8,128)(2,1)} %param.8) | copy-start | bytes 6291460

commit v11 on v10

--- a/solution.py
+++ b/solution.py
@@ -152,6 +152,17 @@
     energy[...] = jnp.sum(squares[...], axis=0, keepdims=True)
 
 
+def returned_rows(x):
+    pairs = x.reshape(-1, 2, LANE, TILE)
+    return jnp.concatenate([pairs[:, 0, HALF:, :], pairs[:, 1, HALF:, :]], axis=1).reshape(-1, TILE)
+
+
+def laid_twice(x):
+    halves_of = [x.reshape(-1, LANE, TILE)[:, k : k + HALF, :] for k in (0, HALF)]
+    pairs = [jnp.concatenate([half, half], axis=1) for half in halves_of]
+    return jnp.stack(pairs, axis=1).reshape(-1, TILE)
+
+
 def product_lane(asked_row, asked_col):
     rows = [asked_row[...].astype(F32).T[0:1, :]]
     width = asked_col.shape[0]
@@ -171,7 +182,8 @@
             hit = (served == lane) & (served >= 0)
             meet[base : base + served.shape[0], k * TILE : (k + 1) * TILE] = jnp.where(hit, 1.0, 0.0).astype(BF16)
         base += served.shape[0]
-    ident = jnp.where(served_col < 0, -3, served_col + (me[0] << bits))
+    ident = returned_rows(served_col)
+    ident = jnp.where(ident < 0, -3, ident + (me[0] << bits))
     slot = iota(owned.shape[:1] + (TILE,), 0)
     half = jnp.where(iota(owned.shape[:1] + (TILE,), 1) < mine.shape[0], 0, 1)
     for k in range(riders.shape[0]):
@@ -204,7 +216,7 @@
     out, v_col, meet, link, link_col, owned,
 ):
     y = multiply(exact_dot(pick[...], got[...]), tiles)
-    v = gather(asked_col[...], vector[...] * SCALE)
+    v = laid_twice(gather(returned_rows(asked_col[...]), vector[...] * SCALE))
     v_col[...] = v
     forward = (iota(v.shape, 0) & LOW) < HALF
     out[...] = exact_dot(put[...], y) + jnp.where(forward, v, 0.0)
@@ -235,7 +247,7 @@
     lows = jnp.concatenate([got[k, middle:, :] for k in peers], axis=0)
     y = multiply(dot(link[...], mirrors) + dot(pick[...], sums), tiles)
     width = got.shape[0] * LANE
-    image = dot(link_col[...], mirrors) + exact_dot(meet[width:, width:], first_col[...])
+    image = laid_twice(dot(link_col[...], mirrors)) + exact_dot(meet[width:, width:], first_col[...])
     forward = (iota(image.shape, 0) & LOW) < HALF
     out[...] = exact_dot(put[...], y) + jnp.where(forward, image, 0.0)
     slot = iota((width, 2 * width), 0)
@@ -279,11 +291,6 @@
     sums = jnp.sum(total, axis=1, keepdims=True)
     packed = jnp.sum(jnp.where(iota(total.shape, 0) == iota(total.shape, 1), sums, 0.0), axis=0, keepdims=True)
     out[...] = jnp.broadcast_to(packed, out.shape)
-
-
-def returned_rows(x):
-    pairs = x.reshape(-1, 2, LANE, TILE)
-    return jnp.concatenate([pairs[:, 0, HALF:, :], pairs[:, 1, HALF:, :]], axis=1).reshape(-1, TILE)
 
 
 def final_kernel(
@@ -452,7 +459,7 @@
             shape(wide_c, TILE),
             shape(every, every, dtype=BF16),
             shape(count, n_row * count, dtype=BF16),
-            shape(wide_c, n_row * count, dtype=BF16),
+            shape(wide_c // 2, n_row * count, dtype=BF16),
             shape(wide_r, n_row * count, dtype=BF16),
         ),
         me,

time: 129 us -> 129 us (level)
  no operation moved by 1% of the time
where the time goes in v11:
time: 129 us
  blocking collectives  106 us (82%)
  Pallas kernels  8.54 us (7%)
  waiting for transfers between devices  4.78 us (4%)
  starting transfers between devices  4.3 us (3%)
  local copies, waits for them, and re-layouts  3.46 us (3%)
  between operations  1.37 us (1%)
    all_to_all x6, blocking collectives, exchange(): got = lax.all_to_all(sent, axis, split_axis=0, concat_axis=0, tiled=True)  75.2 us
    all_gather x3, blocking collectives, over_chip(): return lax.all_gather(x, 'row', axis_index_groups=chips, tiled=True)  19.8 us
    all_to_all x1, blocking collectives, per_device(): lax.all_to_all(packed, 'row', split_axis=0, concat_axis=0, axis_index_gro...  11.1 us
    pallas_call x10, Pallas kernels, call(): pl.pallas_call(kernel, out_shape=outs, in_specs=ins if isinstance(ins, li...  8.54 us
    all_to_all x1, waiting for transfers between devices, per_device(): lax.all_to_all(ask.reshape(n_col, 1, TILE), ('row', 'col'), split_axis=0,...  4.78 us
    all_to_all x1, starting transfers between devices, per_device(): lax.all_to_all(ask.reshape(n_col, 1, TILE), ('row', 'col'), split_axis=0,...  4.3 us
    unnamed x8, local copies, waits for them, and re-layouts  2.73 us
  transfers between devices with their start and end apart: 1, of which 1 were waited for; matrix products, arithmetic and copies ran while one was open for 0% of the time, Pallas kernels for 1%

profile of v11, /device:TPU:1, one launch (start us, length us, event | category | flops | bytes accessed | tf_op | source)
XLA Modules:
  0.0 128.5 jit_solution(16282115183109536780)
XLA Ops:
  1.3 0.7 concatenate.7
  2.0 8.4 %all_gather.9.both = s32[16,64]{1,0:T(8,128)S(1)} all-gather(s32[8,64]{1,0:T(8,128)S(1)} %concatenate.7), channel_id=1, replica_groups={{0,32},{64,96},{128,160},{192,224},{256,288},{320,352},{384,416},{448,4..., dimensions={0}, use_global_device_ids=true | all-gather | bytes 6144 | tf_op jit(solution)/shard_map/all_gather | solution.py:399
  10.4 1.0 shard_map.94
  11.4 4.3 %all-to-all-start = ((s32[32,1,128]{2,1,0:T(1,128)}), s32[32,1,128]{2,1,0:T(1,128)S(1)}, u32[]{:S(2)}, u32[]{:S(2)}) async-start(s32[32,1,128]{2,1,0:T(1,128)} %bitcast.8), calls=%async_computation | async-start | bytes 32768 | tf_op jit(solution)/shard_map/all_to_all | solution.py:413
  15.7 0.0 copy-start
  15.7 1.6 %copy-done = bf16[1,1,64,128,128]{4,3,2,1,0:T(8,128)(2,1)S(1)} copy-done((bf16[1,1,64,128,128]{4,3,2,1,0:T(8,128)(2,1)S(1)}, bf16[1,1,64,128,128]{4,3,2,1,0:T(8,128)(2,1)}, u32[]{:S(2)}) %copy-start) | copy-done | bytes 2097176
  17.3 0.0 copy-start.2
  17.3 1.1 copy-done.2
  18.5 0.0 copy-start.3
  18.5 1.0 shard_map.95
  19.5 4.8 %all-to-all-done = s32[32,1,128]{2,1,0:T(1,128)S(1)} async-done(((s32[32,1,128]{2,1,0:T(1,128)}), s32[32,1,128]{2,1,0:T(1,128)S(1)}, u32[]{:S(2)}, u32[]{:S(2)}) %all-to-all-start) | async-done | bytes 16416 | tf_op jit(solution)/shard_map/all_to_all | solution.py:413
  24.2 6.5 %all-gather = s32[64,1,128]{2,0,1:T(8,128)S(1)} all-gather(s32[32,1,128]{2,0,1:T(8,128)S(1)} %bitcast.56), channel_id=2, replica_groups={{0,32},{64,96},{128,160},{192,224},{256,288},{320,352},{384,416},{448,4..., dimensions={0}, use_global_device_ids=true | all-gather | bytes 49152 | tf_op jit(solution)/shard_map/all_gather | solution.py:399
  30.7 0.0 copy-done.3
  30.7 0.0 copy-start.1
  30.7 0.6 shard_map.96
  31.3 15.2 %all_to_all.40 = f32[16,8,128]{2,1,0:T(8,128)S(1)} all-to-all(f32[16,8,128]{2,1,0:T(8,128)S(1)} %bitcast.48), channel_id=1, replica_groups=mesh['row'=16,'col'=32] {'row'}, dimensions={0} | all-to-all | bytes 131072 | tf_op jit(solution)/shard_map/all_to_all | solution.py:370
  46.5 1.1 shard_map.97
  47.6 12.5 %all_to_all.41 = f32[32,8,128]{2,1,0:T(8,128)S(1)} all-to-all(f32[32,8,128]{2,1,0:T(8,128)S(1)} %bitcast.52), channel_id=1, replica_groups=mesh['row'=16,'col'=32] {'col'}, dimensions={0} | all-to-all | bytes 262144 | tf_op jit(solution)/shard_map/all_to_all | solution.py:370
  60.1 0.0 copy-done.1
  60.1 0.6 shard_map.98
  60.8 11.1 %all_to_all.42 = bf16[8,96,128]{2,1,0:T(8,128)(2,1)S(1)} all-to-all(bf16[8,96,128]{2,1,0:T(8,128)(2,1)S(1)} %shard_map.98), channel_id=1, replica_groups={{0,64,128,192,256,320,384,448},{32,96,160,224,288,352,416,480},{1,65,12..., dimensions={0} | all-to-all | bytes 393216 | tf_op jit(solution)/shard_map/all_to_all | solution.py:488
  71.8 4.9 %all_gather.11.got = bf16[16,96,128]{2,1,0:T(8,128)(2,1)S(1)} all-gather(bf16[8,96,128]{2,1,0:T(8,128)(2,1)S(1)} %all_to_all.42), channel_id=1, replica_groups={{0,32},{64,96},{128,160},{192,224},{256,288},{320,352},{384,416},{448,4..., dimensions={0}, use_global_device_ids=true | all-gather | bytes 589824 | tf_op jit(solution)/shard_map/all_gather | solution.py:399
  76.8 0.9 shard_map.99
  77.6 12.9 %all_to_all.43 = f32[32,8,128]{2,1,0:T(8,128)S(1)} all-to-all(f32[32,8,128]{2,1,0:T(8,128)S(1)} %bitcast.53), channel_id=1, replica_groups=mesh['row'=16,'col'=32] {'col'}, dimensions={0} | all-to-all | bytes 262144 | tf_op jit(solution)/shard_map/all_to_all | solution.py:370
  90.6 0.7 shard_map.100
  91.2 12.3 %all_to_all.44 = f32[16,8,128]{2,1,0:T(8,128)S(1)} all-to-all(f32[16,8,128]{2,1,0:T(8,128)S(1)} %bitcast.50), channel_id=1, replica_groups=mesh['row'=16,'col'=32] {'row'}, dimensions={0} | all-to-all | bytes 131072 | tf_op jit(solution)/shard_map/all_to_all | solution.py:370
  103.6 0.4 shard_map.101
  104.0 10.4 %all_to_all.45.got = f32[16,8,128]{2,1,0:T(8,128)S(1)} all-to-all(f32[16,8,128]{2,1,0:T(8,128)S(1)} %shard_map.101), channel_id=1, replica_groups=mesh['row'=16,'col'=32] {'row'}, dimensions={0} | all-to-all | bytes 131072 | tf_op jit(solution)/shard_map/all_to_all | solution.py:370
  114.4 0.1 shard_map.102
  114.5 11.9 %all_to_all.46 = f32[32,1,128]{2,1,0:T(1,128)S(1)} all-to-all(f32[32,1,128]{2,1,0:T(1,128)S(1)} %bitcast.55), channel_id=1, replica_groups=mesh['row'=16,'col'=32] {'col'}, dimensions={0} | all-to-all | bytes 32768 | tf_op jit(solution)/shard_map/all_to_all | solution.py:370
  126.4 2.1 %shard_map.103 = (f32[3072,128]{1,0:T(8,128)}, f32[1]{0:T(128)}, f32[3]{0:T(128)}) custom-call(f32[32,128]{1,0:T(8,128)S(1)} %bitcast.54, f32[1536,128]{1,0:T(8,128)S(1)} %bitcast.38, s32[128,128]{1,0:T(8,128)S(1)} %get-tuple-element.32.asked_row.refs_2_, s32[256,128]{1,0:T(8,128)S(1)} %get-tuple-element.33.asked_col.refs_3_, ...), custom_call_target="tpu_custom_call" | custom-call | tf_op jit(solution)/shard_map/pallas_call | solution.py:358
  (3 shorter events, 0.0 us)
Async XLA Ops:
  11.4 12.8 %all-to-all-start = ((s32[32,1,128]{2,1,0:T(1,128)}), s32[32,1,128]{2,1,0:T(1,128)S(1)}, u32[]{:S(2)}, u32[]{:S(2)}) async-start(s32[32,1,128]{2,1,0:T(1,128)} %bitcast.8), calls=%async_computation | async-start | bytes 32768 | tf_op jit(solution)/shard_map/all_to_all | solution.py:413
  15.7 1.6 %copy-start = (bf16[1,1,64,128,128]{4,3,2,1,0:T(8,128)(2,1)S(1)}, bf16[1,1,64,128,128]{4,3,2,1,0:T(8,128)(2,1)}, u32[]{:S(2)}) copy-start(bf16[1,1,64,128,128]{4,3,2,1,0:T(8,128)(2,1)} %param.8) | copy-start | bytes 6291460
  17.3 1.1 copy-start.2
  18.5 12.3 %copy-start.3 = (f32[196608]{0:T(1024)S(1)}, f32[196608]{0:T(1024)}, u32[]{:S(2)}) copy-start(f32[196608]{0:T(1024)} %param.7) | copy-start | bytes 2359300
  30.7 29.4 %copy-start.1 = (bf16[1,1,64,128,128]{4,3,2,1,0:T(8,128)(2,1)S(1)}, bf16[1,1,64,128,128]{4,3,2,1,0:T(8,128)(2,1)}, u32[]{:S(2)}) copy-start(bf16[1,1,64,128,128]{4,3,2,1,0:T(8,128)(2,1)} %param.8) | copy-start | bytes 6291460

commit v12 on v11

--- a/solution.py
+++ b/solution.py
@@ -56,7 +56,7 @@
 
 def request_kernel(bits, planes, both, me, col, ask):
     n_x, n_z = planes
-    first = (jnp.full((1, 1), me[0], jnp.int32) & 1) == 0
+    first = (jnp.full((1, 1), me[0], jnp.int32) & 1) == 1
     x = col[0] // n_z
     count = both.shape[1]
     width = ask.shape[0]
@@ -127,16 +127,16 @@
 def served_kernel(n_x, bits, me, pair, vector, squares, asked_row, asked_col, riders, out, energy):
     first = (jnp.full((1, 1), me[0], jnp.int32) & 1) == 0
     peers = pair.shape[0] // 2
-    col = pair[:peers, :]
+    col = pair[peers:, :]
     for k in range(HALF):
         sides = [jnp.broadcast_to(col[:, 16 * j : 16 * j + 1], col.shape) for j in (k, k + HALF)]
         value = jnp.where(first, sides[0], sides[1])
         asked_col[pl.ds(k, peers, LANE), :] = value
         asked_col[pl.ds(k + HALF, peers, LANE), :] = value
     chips = peers // n_x
-    row = pair[pl.ds(peers, chips, n_x), :]
+    row = pair[pl.ds(0, chips, n_x), :]
     for x in range(1, n_x):
-        row = jnp.maximum(row, pair[pl.ds(peers + x, chips, n_x), :])
+        row = jnp.maximum(row, pair[pl.ds(x, chips, n_x), :])
     riders[...] = row
     down = iota((2 * LANE, TILE), 0)
     side = jnp.where(iota((2 * LANE, TILE), 1) < TILE // 2, 0, 1) == (down >> BITS)
@@ -391,8 +391,8 @@
     n_y = n_row // 2
     n_x = n_col // n_y
     n_z = n_col // n_x
-    planes = [[2 * y * n_col + c for c in range(n_col)] for y in range(n_y)]
-    planes += [[(2 * y + 1) * n_col + x * n_z + z for y in range(n_y) for x in range(n_x)] for z in range(n_z)]
+    planes = [[(2 * y + 1) * n_col + c for c in range(n_col)] for y in range(n_y)]
+    planes += [[2 * y * n_col + x * n_z + z for y in range(n_y) for x in range(n_x)] for z in range(n_z)]
     chips = [[2 * y, 2 * y + 1] for y in range(n_y)]
 
     def over_chip(x):

time: 129 us -> 129 us (level)
  starting transfers between devices: 4.3 us -> 7.51 us
  blocking collectives: 106 us -> 103 us
    all_gather x3, blocking collectives: 19.8 us -> 15.1 us  [over_chip(): return lax.all_gather(x, 'row', axis_index_groups=chips, tiled=True)]
    all_to_all x1, starting transfers between devices: 4.3 us -> 7.51 us  [per_device(): lax.all_to_all(ask.reshape(n_col, 1, TILE), ('row', 'col'), split_axis=0,...]
    all_to_all x6, blocking collectives: 75.2 us -> 76.6 us  [exchange(): got = lax.all_to_all(sent, axis, split_axis=0, concat_axis=0, tiled=True)]
where the time goes in v12:
time: 129 us
  blocking collectives  103 us (80%)
  Pallas kernels  8.54 us (7%)
  starting transfers between devices  7.51 us (6%)
  waiting for transfers between devices  4.83 us (4%)
  local copies, waits for them, and re-layouts  3.46 us (3%)
  between operations  1.37 us (1%)
    all_to_all x6, blocking collectives, exchange(): got = lax.all_to_all(sent, axis, split_axis=0, concat_axis=0, tiled=True)  76.6 us
    all_gather x3, blocking collectives, over_chip(): return lax.all_gather(x, 'row', axis_index_groups=chips, tiled=True)  15.1 us
    all_to_all x1, blocking collectives, per_device(): lax.all_to_all(packed, 'row', split_axis=0, concat_axis=0, axis_index_gro...  11.1 us
    pallas_call x10, Pallas kernels, call(): pl.pallas_call(kernel, out_shape=outs, in_specs=ins if isinstance(ins, li...  8.54 us
    all_to_all x1, starting transfers between devices, per_device(): lax.all_to_all(ask.reshape(n_col, 1, TILE), ('row', 'col'), split_axis=0,...  7.51 us
    all_to_all x1, waiting for transfers between devices, per_device(): lax.all_to_all(ask.reshape(n_col, 1, TILE), ('row', 'col'), split_axis=0,...  4.83 us
    unnamed x8, local copies, waits for them, and re-layouts  2.73 us
  transfers between devices with their start and end apart: 1, of which 1 were waited for; matrix products, arithmetic and copies ran while one was open for 0% of the time, Pallas kernels for 1%

profile of v12, /device:TPU:1, one launch (start us, length us, event | category | flops | bytes accessed | tf_op | source)
XLA Modules:
  0.0 128.5 jit_solution(1678507165797703823)
XLA Ops:
  1.3 0.7 concatenate.7
  2.0 8.4 %all_gather.9.both = s32[16,64]{1,0:T(8,128)S(1)} all-gather(s32[8,64]{1,0:T(8,128)S(1)} %concatenate.7), channel_id=1, replica_groups={{0,32},{64,96},{128,160},{192,224},{256,288},{320,352},{384,416},{448,4..., dimensions={0}, use_global_device_ids=true | all-gather | bytes 6144 | tf_op jit(solution)/shard_map/all_gather | solution.py:399
  10.4 1.0 shard_map.94
  11.4 7.5 %all-to-all-start = ((s32[32,1,128]{2,1,0:T(1,128)}), s32[32,1,128]{2,1,0:T(1,128)S(1)}, u32[]{:S(2)}, u32[]{:S(2)}) async-start(s32[32,1,128]{2,1,0:T(1,128)} %bitcast.8), calls=%async_computation | async-start | bytes 32768 | tf_op jit(solution)/shard_map/all_to_all | solution.py:413
  18.9 0.0 copy-start
  19.0 1.6 %copy-done = bf16[1,1,64,128,128]{4,3,2,1,0:T(8,128)(2,1)S(1)} copy-done((bf16[1,1,64,128,128]{4,3,2,1,0:T(8,128)(2,1)S(1)}, bf16[1,1,64,128,128]{4,3,2,1,0:T(8,128)(2,1)}, u32[]{:S(2)}) %copy-start) | copy-done | bytes 2097176
  20.5 0.0 copy-start.2
  20.5 1.1 copy-done.2
  21.7 0.0 copy-start.3
  21.7 1.0 shard_map.95
  22.7 4.8 %all-to-all-done = s32[32,1,128]{2,1,0:T(1,128)S(1)} async-done(((s32[32,1,128]{2,1,0:T(1,128)}), s32[32,1,128]{2,1,0:T(1,128)S(1)}, u32[]{:S(2)}, u32[]{:S(2)}) %all-to-all-start) | async-done | bytes 16416 | tf_op jit(solution)/shard_map/all_to_all | solution.py:413
  27.5 1.8 %all-gather = s32[64,1,128]{2,0,1:T(8,128)S(1)} all-gather(s32[32,1,128]{2,0,1:T(8,128)S(1)} %bitcast.56), channel_id=2, replica_groups={{0,32},{64,96},{128,160},{192,224},{256,288},{320,352},{384,416},{448,4..., dimensions={0}, use_global_device_ids=true | all-gather | bytes 49152 | tf_op jit(solution)/shard_map/all_gather | solution.py:399
  29.3 0.0 copy-done.3
  29.3 0.0 copy-start.1
  29.3 0.6 shard_map.96
  29.9 15.0 %all_to_all.40 = f32[16,8,128]{2,1,0:T(8,128)S(1)} all-to-all(f32[16,8,128]{2,1,0:T(8,128)S(1)} %bitcast.48), channel_id=1, replica_groups=mesh['row'=16,'col'=32] {'row'}, dimensions={0} | all-to-all | bytes 131072 | tf_op jit(solution)/shard_map/all_to_all | solution.py:370
  45.0 1.1 shard_map.97
  46.1 14.0 %all_to_all.41 = f32[32,8,128]{2,1,0:T(8,128)S(1)} all-to-all(f32[32,8,128]{2,1,0:T(8,128)S(1)} %bitcast.52), channel_id=1, replica_groups=mesh['row'=16,'col'=32] {'col'}, dimensions={0} | all-to-all | bytes 262144 | tf_op jit(solution)/shard_map/all_to_all | solution.py:370
  60.1 0.0 copy-done.1
  60.1 0.6 shard_map.98
  60.8 11.1 %all_to_all.42 = bf16[8,96,128]{2,1,0:T(8,128)(2,1)S(1)} all-to-all(bf16[8,96,128]{2,1,0:T(8,128)(2,1)S(1)} %shard_map.98), channel_id=1, replica_groups={{0,64,128,192,256,320,384,448},{32,96,160,224,288,352,416,480},{1,65,12..., dimensions={0} | all-to-all | bytes 393216 | tf_op jit(solution)/shard_map/all_to_all | solution.py:488
  71.8 4.9 %all_gather.11.got = bf16[16,96,128]{2,1,0:T(8,128)(2,1)S(1)} all-gather(bf16[8,96,128]{2,1,0:T(8,128)(2,1)S(1)} %all_to_all.42), channel_id=1, replica_groups={{0,32},{64,96},{128,160},{192,224},{256,288},{320,352},{384,416},{448,4..., dimensions={0}, use_global_device_ids=true | all-gather | bytes 589824 | tf_op jit(solution)/shard_map/all_gather | solution.py:399
  76.7 0.9 shard_map.99
  77.6 12.9 %all_to_all.43 = f32[32,8,128]{2,1,0:T(8,128)S(1)} all-to-all(f32[32,8,128]{2,1,0:T(8,128)S(1)} %bitcast.53), channel_id=1, replica_groups=mesh['row'=16,'col'=32] {'col'}, dimensions={0} | all-to-all | bytes 262144 | tf_op jit(solution)/shard_map/all_to_all | solution.py:370
  90.5 0.7 shard_map.100
  91.2 12.3 %all_to_all.44 = f32[16,8,128]{2,1,0:T(8,128)S(1)} all-to-all(f32[16,8,128]{2,1,0:T(8,128)S(1)} %bitcast.50), channel_id=1, replica_groups=mesh['row'=16,'col'=32] {'row'}, dimensions={0} | all-to-all | bytes 131072 | tf_op jit(solution)/shard_map/all_to_all | solution.py:370
  103.6 0.4 shard_map.101
  104.0 10.4 %all_to_all.45.got = f32[16,8,128]{2,1,0:T(8,128)S(1)} all-to-all(f32[16,8,128]{2,1,0:T(8,128)S(1)} %shard_map.101), channel_id=1, replica_groups=mesh['row'=16,'col'=32] {'row'}, dimensions={0} | all-to-all | bytes 131072 | tf_op jit(solution)/shard_map/all_to_all | solution.py:370
  114.4 0.1 shard_map.102
  114.5 11.9 %all_to_all.46 = f32[32,1,128]{2,1,0:T(1,128)S(1)} all-to-all(f32[32,1,128]{2,1,0:T(1,128)S(1)} %bitcast.55), channel_id=1, replica_groups=mesh['row'=16,'col'=32] {'col'}, dimensions={0} | all-to-all | bytes 32768 | tf_op jit(solution)/shard_map/all_to_all | solution.py:370
  126.4 2.1 %shard_map.103 = (f32[3072,128]{1,0:T(8,128)}, f32[1]{0:T(128)}, f32[3]{0:T(128)}) custom-call(f32[32,128]{1,0:T(8,128)S(1)} %bitcast.54, f32[1536,128]{1,0:T(8,128)S(1)} %bitcast.38, s32[128,128]{1,0:T(8,128)S(1)} %get-tuple-element.32.asked_row.refs_2_, s32[256,128]{1,0:T(8,128)S(1)} %get-tuple-element.33.asked_col.refs_3_, ...), custom_call_target="tpu_custom_call" | custom-call | tf_op jit(solution)/shard_map/pallas_call | solution.py:358
  (3 shorter events, 0.0 us)
Async XLA Ops:
  11.4 16.1 %all-to-all-start = ((s32[32,1,128]{2,1,0:T(1,128)}), s32[32,1,128]{2,1,0:T(1,128)S(1)}, u32[]{:S(2)}, u32[]{:S(2)}) async-start(s32[32,1,128]{2,1,0:T(1,128)} %bitcast.8), calls=%async_computation | async-start | bytes 32768 | tf_op jit(solution)/shard_map/all_to_all | solution.py:413
  18.9 1.6 %copy-start = (bf16[1,1,64,128,128]{4,3,2,1,0:T(8,128)(2,1)S(1)}, bf16[1,1,64,128,128]{4,3,2,1,0:T(8,128)(2,1)}, u32[]{:S(2)}) copy-start(bf16[1,1,64,128,128]{4,3,2,1,0:T(8,128)(2,1)} %param.8) | copy-start | bytes 6291460
  20.5 1.1 copy-start.2
  21.7 7.7 %copy-start.3 = (f32[196608]{0:T(1024)S(1)}, f32[196608]{0:T(1024)}, u32[]{:S(2)}) copy-start(f32[196608]{0:T(1024)} %param.7) | copy-start | bytes 2359300
  29.3 30.8 %copy-start.1 = (bf16[1,1,64,128,128]{4,3,2,1,0:T(8,128)(2,1)S(1)}, bf16[1,1,64,128,128]{4,3,2,1,0:T(8,128)(2,1)}, u32[]{:S(2)}) copy-start(bf16[1,1,64,128,128]{4,3,2,1,0:T(8,128)(2,1)} %param.8) | copy-start | bytes 6291460
